TPU v7x, 32 devices: a whole 2x2x4 slice. The times are simulated.
32 devices in a mesh: grp: 2 (over x), chol: 16 (over z, y, core).
Axes of the slice: x: 2, y: 2, z: 4, core: 2. Of those that a mesh axis runs over, the one named last changes fastest.
Arguments:
- walkers: bfloat16 [1024, 64, 256], P(('grp', 'chol')), parts along dimension 0, may hold values from -6 to 6
- fields: bfloat16 [1024, 1024], P(('grp', 'chol')), parts along dimension 0, may hold values from -6 to 6
- chol_vectors: bfloat16 [1024, 256, 256], P(None, 'chol'), may hold values from -0.375 to 0.375
- rotated: bfloat16 [1024, 64, 256], P(None, 'chol'), may hold values from -0.046875 to 0.046875
- send_walker: int32 [32, 16, 2], P(('grp', 'chol')), parts along dimension 0, may hold values from -1 to 31, as said below
- slot_row: int32 [1024], P(('grp', 'chol')), parts along dimension 0, may hold values from 0 to 31, as said below
Outputs:
- new_walkers: bfloat16 [1024, 64, 256], P(('grp', 'chol')), parts along dimension 0
- force_bias: float32 [1024, 1024], P(('grp', 'chol')), parts along dimension 0
There are 2 independent parts, one for each index of `grp`. A program takes and returns all parts, laid end to end along the dimension named above; an argument that names none is the same for every part. Nothing has to cross between parts.
Inputs may be any that keep to these rules, and one draw needn't show every extreme that they name: `send_walker`: entry [s, d, c] is the index, among the 32 walkers of block s, of the walker that block s sends as its c-th one to block d, or -1 where it sends none; indices of one [s, d] row come first, -1 after. Some pair of blocks uses all 2 entries. `slot_row`: for every slot of block d, s * 2 + c names a valid entry [s, d, c] of send_walker, and every valid entry is named by exactly one slot of block d.
All inputs are finite; a program needn't handle non-finite values.
Results may differ from a plain program's by a relative error of at most 0.0075.
Values may be sent and summed in bfloat16 or wider, within the bound.
No kernel may reach another device: no remote copies, remote signals or barrier semaphores. Data moves between devices by JAX's collectives and lax.ppermute only.
A program may use at most 64 MiB of HBM per device.

v0:
```python
import math

import jax
import jax.numpy as jnp
from jax import lax
from jax.sharding import PartitionSpec as P

field_scale = 1.5


def branch_walkers(walkers, send_walker, slot_row):
    slots, electrons, orbitals = walkers.shape
    flat_walkers = walkers.reshape(slots, electrons * orbitals)
    send_list = send_walker.reshape(-1)
    choose_send = (send_list[:, None] == jnp.arange(slots, dtype=jnp.int32)[None, :]).astype(
        jnp.bfloat16
    )
    outgoing = jnp.dot(choose_send, flat_walkers, preferred_element_type=jnp.float32).astype(
        jnp.bfloat16
    )
    incoming = lax.all_to_all(outgoing, "chol", split_axis=0, concat_axis=0, tiled=True)
    choose_recv = (
        slot_row[:, None] == jnp.arange(incoming.shape[0], dtype=jnp.int32)[None, :]
    ).astype(jnp.bfloat16)
    branched = jnp.dot(choose_recv, incoming, preferred_element_type=jnp.float32).astype(
        jnp.bfloat16
    )
    return branched.reshape(slots, electrons, orbitals)


def build_operators(fields, chol_vectors):
    nchol, row_local, orbitals = chol_vectors.shape
    chol_flat = chol_vectors.reshape(nchol, row_local * orbitals)
    scale = field_scale / math.sqrt(nchol)

    def operator_rows(field_rows, first_row):
        return (jnp.dot(field_rows, chol_flat, preferred_element_type=jnp.float32) * scale).astype(
            jnp.bfloat16
        )

    all_rows = operator_rows(lax.all_gather(fields, "chol", axis=0, tiled=True), jnp.int32(0))
    return all_rows.reshape(all_rows.shape[0], row_local, orbitals)


def shards(walkers, fields, chol_vectors, rotated, send_walker, slot_row):
    slots, electrons, orbitals = walkers.shape
    branched = branch_walkers(walkers, send_walker, slot_row)
    operator_rows = build_operators(fields, chol_vectors)
    operator = lax.all_to_all(operator_rows, "chol", split_axis=0, concat_axis=1, tiled=True)
    total = branched.astype(jnp.float32)
    term = branched
    for degree in range(1, 6):
        product = jnp.einsum("waj,wij->wai", term, operator, preferred_element_type=jnp.float32)
        term = (product / degree).astype(jnp.bfloat16)
        total = total + term.astype(jnp.float32)
    new_walkers = total.astype(jnp.bfloat16)
    nchol, elec_local, _ = rotated.shape
    electron_rows = lax.all_to_all(new_walkers, "chol", split_axis=1, concat_axis=0, tiled=True)
    electron_flat = electron_rows.reshape(electron_rows.shape[0], elec_local * orbitals)
    rot_flat = rotated.reshape(nchol, elec_local * orbitals)
    force_bias = lax.psum_scatter(
        lax.dot_general(
            electron_flat, rot_flat, (((1,), (1,)), ((), ())), preferred_element_type=jnp.float32
        ),
        "chol",
        scatter_dimension=0,
        tiled=True,
    )
    return (new_walkers, force_bias)


def solution(mesh):
    in_specs = (
        P(("grp", "chol"), None, None),
        P(("grp", "chol"), None),
        P(None, "chol", None),
        P(None, "chol", None),
        P(("grp", "chol"), None, None),
        P(("grp", "chol")),
    )
    out_specs = (P(("grp", "chol"), None, None), P(("grp", "chol"), None))
    return jax.shard_map(shards, mesh=mesh, in_specs=in_specs, out_specs=out_specs, check_vma=False)
```

profile of v0, /device:TPU:0, one launch (start us, length us, event | category | flops | bytes accessed | tf_op | source)
XLA Modules:
  0.0 282.4 jit_solution(2436412152007579640)
XLA Ops:
  7.2 0.0 copy-start.1
  7.2 0.0 all-gather.2.cloned.1.call-start
  7.2 0.7 all-gather.2.cloned.1.call-update
  7.9 1.8 copy.17
  9.7 0.0 copy-done.1
  9.7 0.1 copy.13
  9.8 0.1 eq.31
  9.9 0.5 convolution_convert_fusion.1
  10.4 1.5 all_to_all.32
  11.9 7.4 %all-to-all-start = ((bf16[16,2,16384]{2,1,0:T(2,128)(2,1)}), bf16[16,2,16384]{2,1,0:T(2,128)(2,1)S(1)}, u32[]{:S(2)}, u32[]{:S(2)}) async-start(bf16[16,2,16384]{2,1,0:T(2,128)(2,1)} %all_to_all.32), calls=%async_computation | async-start | bytes 2097152 | tf_op jit(solution)/shard_map/all_to_all | solution.py:21
  19.3 12.3 %copy.19 = bf16[128,8,16,256]{3,1,2,0:T(8,128)(2,1)} copy(bf16[128,8,16,256]{3,2,1,0:T(8,128)(2,1)} %bitcast.43) | data formatting | bytes 16777216
  31.6 28.8 %all-gather.2.cloned.1.call-done = bf16[512,1024]{1,0:T(8,128)(2,1)} async-done(((bf16[32,1024]{1,0:T(8,128)(2,1)}), bf16[512,1024]{1,0:T(8,128)(2,1)}) %all-gather.2.cloned.1.call-update) | async-done | bytes 1048592 | tf_op jit(solution)/shard_map/all_gather | solution.py:41
  60.4 8.2 %multiply_convert_fusion = bf16[512,4096]{1,0:T(8,128)(2,1)S(1)} fusion(bf16[512,1024]{1,0:T(8,128)(2,1)} %all-gather.2.cloned.1.call-done, bf16[1024,4096]{1,0:T(8,128)(2,1)} %bitcast.44), kind=kOutput, calls=%fused_computation.2 | convolution fusion | flops 4299161600 | bytes 13631488 | tf_op jit(solution)/shard_map/dot_general | solution.py:37
  68.6 3.4 %copy.20 = bf16[64,8,16,256]{3,2,1,0:T(8,128)(2,1)} copy(bf16[64,8,16,256]{3,1,2,0:T(8,128)(2,1)S(1)} %bitcast.47) | data formatting | bytes 8388608
  72.0 0.0 all-to-all-done
  72.0 4.7 %all-to-all-start.1 = ((bf16[512,16,256]{2,1,0:T(8,128)(2,1)}), bf16[512,16,256]{2,1,0:T(8,128)(2,1)}, u32[]{:S(2)}, u32[]{:S(2)}) async-start(bf16[512,16,256]{2,1,0:T(8,128)(2,1)} %bitcast.40), calls=%async_computation.1 | async-start | bytes 8388608 | tf_op jit(solution)/shard_map/all_to_all | solution.py:49
  76.8 0.0 copy-start.2
  76.8 0.4 all_to_all.34
  77.2 0.2 copy-done.2
  77.4 0.5 convolution_convert_fusion
  77.9 0.2 copy.18
  78.1 76.0 %all-to-all-done.1 = bf16[512,16,256]{2,1,0:T(8,128)(2,1)} async-done(((bf16[512,16,256]{2,1,0:T(8,128)(2,1)}), bf16[512,16,256]{2,1,0:T(8,128)(2,1)}, u32[]{:S(2)}, u32[]{:S(2)}) %all-to-all-start.1) | async-done | bytes 4194336 | tf_op jit(solution)/shard_map/all_to_all | solution.py:49
  154.2 2.7 copy.14
  156.9 1.4 convolution_convert_fusion.2
  158.3 1.4 multiply_convert_fusion.4
  159.7 1.4 multiply_convert_fusion.3
  161.1 1.4 multiply_convert_fusion.2
  162.5 1.4 add_convert_fusion
  163.9 0.0 copy-start
  163.9 1.6 copy.15
  165.4 0.0 copy-done
  165.4 19.6 %all-to-all-start.2 = ((bf16[32,64,256]{2,0,1:T(8,128)(2,1)}), bf16[32,64,256]{2,0,1:T(8,128)(2,1)S(1)}, u32[]{:S(2)}, u32[]{:S(2)}) async-start(bf16[32,64,256]{2,0,1:T(8,128)(2,1)} %copy.15), calls=%async_computation.2 | async-start | bytes 2097152 | tf_op jit(solution)/shard_map/all_to_all | solution.py:58
  185.0 0.0 reduce-scatter.2.cloned.1.call-start
  185.1 2.1 copy.22
  187.2 20.8 %all-to-all-done.2 = bf16[32,64,256]{2,0,1:T(8,128)(2,1)S(1)} async-done(((bf16[32,64,256]{2,0,1:T(8,128)(2,1)}), bf16[32,64,256]{2,0,1:T(8,128)(2,1)S(1)}, u32[]{:S(2)}, u32[]{:S(2)}) %all-to-all-start.2) | async-done | bytes 1048608 | tf_op jit(solution)/shard_map/all_to_all | solution.py:58
  208.0 0.9 copy.16
  208.9 0.2 copy.21
  209.1 2.6 fusion.2
  211.7 0.0 reduce-scatter.2.cloned.1.call-update
  211.8 63.8 %reduce-scatter.2.cloned.1.call-done = f32[32,1024]{1,0:T(8,128)} async-done(((f32[512,1024]{1,0:T(8,128)}), f32[32,1024]{1,0:T(8,128)}) %reduce-scatter.2.cloned.1.call-update) | async-done | bytes 131088 | tf_op jit(solution)/shard_map/reduce_scatter | solution.py:61
Async XLA Ops:
  7.2 2.6 copy-start.1
  7.2 53.2 %all-gather.2.cloned.1.call-start = ((), (), s32[]{:S(2)}) async-start(), calls=%async_computation.4 | async-start | bytes 1114112 | tf_op jit(solution)/shard_map/all_gather | solution.py:41
  11.9 60.1 %all-to-all-start = ((bf16[16,2,16384]{2,1,0:T(2,128)(2,1)}), bf16[16,2,16384]{2,1,0:T(2,128)(2,1)S(1)}, u32[]{:S(2)}, u32[]{:S(2)}) async-start(bf16[16,2,16384]{2,1,0:T(2,128)(2,1)} %all_to_all.32), calls=%async_computation | async-start | bytes 2097152 | tf_op jit(solution)/shard_map/all_to_all | solution.py:21
  72.0 82.2 %all-to-all-start.1 = ((bf16[512,16,256]{2,1,0:T(8,128)(2,1)}), bf16[512,16,256]{2,1,0:T(8,128)(2,1)}, u32[]{:S(2)}, u32[]{:S(2)}) async-start(bf16[512,16,256]{2,1,0:T(8,128)(2,1)} %bitcast.40), calls=%async_computation.1 | async-start | bytes 8388608 | tf_op jit(solution)/shard_map/all_to_all | solution.py:49
  76.8 0.7 copy-start.2
  163.9 1.6 copy-start
  165.4 42.6 %all-to-all-start.2 = ((bf16[32,64,256]{2,0,1:T(8,128)(2,1)}), bf16[32,64,256]{2,0,1:T(8,128)(2,1)S(1)}, u32[]{:S(2)}, u32[]{:S(2)}) async-start(bf16[32,64,256]{2,0,1:T(8,128)(2,1)} %copy.15), calls=%async_computation.2 | async-start | bytes 2097152 | tf_op jit(solution)/shard_map/all_to_all | solution.py:58
  185.0 90.6 %reduce-scatter.2.cloned.1.call-start = ((), (), s32[]{:S(2)}) async-start(), calls=%async_computation.5 | async-start | bytes 2228224 | tf_op jit(solution)/shard_map/reduce_scatter | solution.py:61
Sparse Core Ops, SparseCore 0:
  10.2 50.1 all-gather.1
  211.9 63.6 reduce-scatter.1
where the time goes:
time: 283 us; the launch traced here: 282 us
  waiting for transfers between devices  190 us (67%)
  starting transfers between devices  31.8 us (11%)
  local copies, waits for them, and re-layouts  27.5 us (10%)
  matrix products  18.7 us (7%)
  between operations  14.2 us (5%)
    all_to_all x1, waiting for transfers between devices, shards(): lax.all_to_all(operator_rows, 'chol', split_axis=0, concat_axis=1, tiled=...  76 us
    reduce_scatter x1, waiting for transfers between devices, shards(): lax.psum_scatter(lax.dot_general(electron_flat, rot_flat, (((1,), (1,)),...  63.8 us
    all_gather x1, waiting for transfers between devices, build_operators(): lax.all_gather(fields, 'chol', axis=0, tiled=True)  28.8 us
    all_to_all x1, waiting for transfers between devices, shards(): lax.all_to_all(new_walkers, 'chol', split_axis=1, concat_axis=0, tiled=True)  20.8 us
    unnamed x13, local copies, waits for them, and re-layouts  20.3 us
    all_to_all x1, starting transfers between devices, shards(): lax.all_to_all(new_walkers, 'chol', split_axis=1, concat_axis=0, tiled=True)  19.6 us
    dot_general x1, matrix products, operator_rows(): jnp.dot(field_rows, chol_flat, preferred_element_type=jnp.float32) * scale  8.22 us
    all_to_all x1, starting transfers between devices, branch_walkers(): lax.all_to_all(outgoing, 'chol', split_axis=0, concat_axis=0, tiled=True)  7.4 us
  transfers between devices with their start and end apart: 5, of which 4 were waited for; matrix products, arithmetic and copies ran while one was open for 10% of the time, Pallas kernels for 0%

commit v1 on v0

--- a/solution.py
+++ b/solution.py
@@ -1,11 +1,17 @@
+import functools
 import math
 
 import jax
 import jax.numpy as jnp
+import numpy as np
 from jax import lax
+from jax.experimental import pallas as pl
+from jax.experimental.pallas import tpu as pltpu
 from jax.sharding import PartitionSpec as P
 
 field_scale = 1.5
+degrees = 5
+inner = 4
 
 
 def branch_walkers(walkers, send_walker, slot_row):
@@ -32,24 +38,21 @@
     nchol, row_local, orbitals = chol_vectors.shape
     chol_flat = chol_vectors.reshape(nchol, row_local * orbitals)
     scale = field_scale / math.sqrt(nchol)
-
-    def operator_rows(field_rows, first_row):
-        return (jnp.dot(field_rows, chol_flat, preferred_element_type=jnp.float32) * scale).astype(
-            jnp.bfloat16
-        )
-
-    all_rows = operator_rows(lax.all_gather(fields, "chol", axis=0, tiled=True), jnp.int32(0))
+    all_fields = lax.all_gather(fields, "chol", axis=0, tiled=True)
+    all_rows = (jnp.dot(all_fields, chol_flat, preferred_element_type=jnp.float32) * scale).astype(
+        jnp.bfloat16
+    )
     return all_rows.reshape(all_rows.shape[0], row_local, orbitals)
 
 
-def shards(walkers, fields, chol_vectors, rotated, send_walker, slot_row):
+def plain_shards(walkers, fields, chol_vectors, rotated, send_walker, slot_row):
     slots, electrons, orbitals = walkers.shape
     branched = branch_walkers(walkers, send_walker, slot_row)
     operator_rows = build_operators(fields, chol_vectors)
     operator = lax.all_to_all(operator_rows, "chol", split_axis=0, concat_axis=1, tiled=True)
     total = branched.astype(jnp.float32)
     term = branched
-    for degree in range(1, 6):
+    for degree in range(1, degrees + 1):
         product = jnp.einsum("waj,wij->wai", term, operator, preferred_element_type=jnp.float32)
         term = (product / degree).astype(jnp.bfloat16)
         total = total + term.astype(jnp.float32)
@@ -69,6 +72,120 @@
     return (new_walkers, force_bias)
 
 
+def propagate_kernel(pieces, planes, rows, elec, place_ref, phi_ref, *refs):
+    piece_refs = refs[:pieces]
+    new_ref = refs[pieces]
+    part_refs = refs[pieces + 1 : pieces + 1 + planes]
+    op_ref, done_ref = refs[pieces + 1 + planes :]
+    block = phi_ref.shape[0]
+    for r in range(pieces):
+        at = pl.multiple_of(place_ref[r] * rows, rows)
+        op_ref[:, pl.ds(at, rows), :] = piece_refs[r][...]
+    terms = [phi_ref[w] for w in range(block)]
+    totals = [t.astype(jnp.float32) for t in terms]
+    for degree in range(1, degrees + 1):
+        for w in range(block):
+            product = lax.dot_general(
+                terms[w], op_ref[w], (((1,), (1,)), ((), ())), preferred_element_type=jnp.float32
+            )
+            terms[w] = (product * np.float32(1.0 / degree)).astype(jnp.bfloat16)
+            totals[w] = totals[w] + terms[w].astype(jnp.float32)
+    for w in range(block):
+        out = totals[w].astype(jnp.bfloat16)
+        new_ref[w] = out
+        done_ref[w] = out
+    for k in range(planes):
+        at = pl.multiple_of(place_ref[pieces + k] * elec, elec)
+        part_refs[k][...] = done_ref[:, pl.ds(at, elec), :]
+
+
+def propagate(phi, pieces, place, planes):
+    slots, electrons, orbitals = phi.shape
+    rows = pieces[0].shape[1]
+    elec = electrons // planes
+    block = 4 if slots % 4 == 0 else 1
+    spec = lambda height: pl.BlockSpec((block, height, orbitals), lambda i: (i, 0, 0))
+    shape = lambda height: jax.ShapeDtypeStruct((slots, height, orbitals), jnp.bfloat16)
+    outs = pl.pallas_call(
+        functools.partial(propagate_kernel, len(pieces), planes, rows, elec),
+        grid=(slots // block,),
+        in_specs=[pl.BlockSpec(memory_space=pltpu.SMEM), spec(electrons)]
+        + [spec(rows)] * len(pieces),
+        out_specs=[spec(electrons)] + [spec(elec)] * planes,
+        out_shape=[shape(electrons)] + [shape(elec)] * planes,
+        scratch_shapes=[
+            pltpu.VMEM((block, orbitals, orbitals), jnp.bfloat16),
+            pltpu.VMEM((block, electrons, orbitals), jnp.bfloat16),
+        ],
+        compiler_params=pltpu.CompilerParams(vmem_limit_bytes=24 * 2**20),
+        cost_estimate=pl.CostEstimate(
+            flops=2 * degrees * slots * electrons * orbitals * orbitals,
+            bytes_accessed=2 * slots * orbitals * (orbitals + 3 * electrons),
+            transcendentals=0,
+        ),
+    )(place, phi, *pieces)
+    return outs[0], outs[1:]
+
+
+def plane_shards(chunks, walkers, fields, chol_vectors, rotated, send_walker, slot_row):
+    slots, electrons, orbitals = walkers.shape
+    nchol, rows, _ = chol_vectors.shape
+    elec_local = rotated.shape[1]
+    devices = orbitals // rows
+    planes = devices // inner
+    me = lax.axis_index("chol")
+    plane, spot = me // inner, me % inner
+    scale = field_scale / math.sqrt(nchol)
+
+    def move(x, k, m):
+        route = [
+            (p * inner + q, (p + k) % planes * inner + (q ^ m))
+            for p in range(planes)
+            for q in range(inner)
+        ]
+        return lax.ppermute(x, "chol", route)
+
+    column = jnp.stack([fields] + [move(fields, planes - k, 0) for k in range(1, planes)])
+    everyone = jnp.stack([column] + [move(column, 0, m) for m in range(1, inner)])
+
+    branched = branch_walkers(walkers, send_walker, slot_row)
+
+    rot_mine = jnp.transpose(rotated, (1, 0, 2))
+    groups = [[p * inner + q for q in range(inner)] for p in range(planes)]
+    rot_plane = lax.all_gather(
+        rot_mine, "chol", axis=0, tiled=True, axis_index_groups=groups
+    )
+
+    sources = [
+        ((plane - k) % planes) * inner + (spot ^ m) for m in range(inner) for k in range(planes)
+    ]
+    place = jnp.stack(sources + [(plane + k) % planes for k in range(planes)]).astype(jnp.int32)
+
+    per = slots // chunks
+    news, biases = [], []
+    for c in range(chunks):
+        part = everyone[:, :, c * per : (c + 1) * per, :]
+        made = (
+            jnp.einsum("mkpg,gij->mkpij", part, chol_vectors, preferred_element_type=jnp.float32)
+            * scale
+        ).astype(jnp.bfloat16)
+        pieces = [
+            made[m, k] if m == 0 and k == 0 else move(made[m, k], k, m)
+            for m in range(inner)
+            for k in range(planes)
+        ]
+        new, parts = propagate(branched[c * per : (c + 1) * per], pieces, place, planes)
+        news.append(new)
+        held = jnp.stack([parts[0]] + [move(parts[k], k, 0) for k in range(1, planes)])
+        sums = jnp.einsum("kpej,egj->kpg", held, rot_plane, preferred_element_type=jnp.float32)
+        bias = sums[0]
+        for k in range(1, planes):
+            back = move(sums[k].astype(jnp.bfloat16), planes - k, 0)
+            bias = bias + back.astype(jnp.float32)
+        biases.append(bias)
+    return (jnp.concatenate(news), jnp.concatenate(biases))
+
+
 def solution(mesh):
     in_specs = (
         P(("grp", "chol"), None, None),
@@ -79,4 +196,15 @@
         P(("grp", "chol")),
     )
     out_specs = (P(("grp", "chol"), None, None), P(("grp", "chol"), None))
+    devices = mesh.shape["chol"]
+
+    def shards(walkers, fields, chol_vectors, rotated, send_walker, slot_row):
+        rows = chol_vectors.shape[1]
+        plane_elec = walkers.shape[1] * inner // devices
+        if devices % inner == 0 and rows % 16 == 0 and plane_elec % 16 == 0:
+            body = functools.partial(plane_shards, 2 if walkers.shape[0] % 32 == 0 else 1)
+        else:
+            body = plain_shards
+        return body(walkers, fields, chol_vectors, rotated, send_walker, slot_row)
+
     return jax.shard_map(shards, mesh=mesh, in_specs=in_specs, out_specs=out_specs, check_vma=False)

time: 283 us -> 213 us (0.75)
  waiting for transfers between devices: 190 us -> 47.9 us
  starting transfers between devices: 31.8 us -> 103 us
  local copies, waits for them, and re-layouts: 27.5 us -> 9.61 us
  Pallas kernels: 0 us -> 9.1 us
  other arithmetic: 0 us -> 6.7 us
    ppermute x0 -> x48, starting transfers between devices: none -> 97.2 us  [move(): return lax.ppermute(x, 'chol', route)]
    all_to_all x2 -> x0, waiting for transfers between devices: 96.8 us -> none  [the longest x1 76 us: shards(): lax.all_to_all(operator_rows, 'chol', split_axis=0, concat_axis=1, tiled=...]
    reduce_scatter x1 -> x0, waiting for transfers between devices: 63.8 us -> none  [shards(): lax.psum_scatter(lax.dot_general(electron_flat, rot_flat, (((1,), (1,)),...]
    ppermute x0 -> x48, waiting for transfers between devices: none -> 47.8 us  [move(): return lax.ppermute(x, 'chol', route)]
    all_gather x1, waiting for transfers between devices: 28.8 us -> 0.02 us  [plane_shards(): lax.all_gather(rot_mine, 'chol', axis=0, tiled=True, axis_index_groups=gr...]
    all_to_all x2 -> x0, starting transfers between devices: 24.3 us -> none  [the longest x1 19.6 us: shards(): lax.all_to_all(new_walkers, 'chol', split_axis=1, concat_axis=0, tiled=True)]
    unnamed x13 -> x25, local copies, waits for them, and re-layouts: 20.3 us -> 4.18 us
    pallas_call x0 -> x2, Pallas kernels: none -> 9.1 us  [propagate(): pl.pallas_call(functools.partial(propagate_kernel, len(pieces), planes, r...]
  transfers between devices with their start and end apart: 5 -> 50, of which waited for: 4 -> 11; matrix products, arithmetic and copies ran while one was open for 10% -> 11% of each run, Pallas kernels for 0% -> 4%
where the time goes in v1:
time: 213 us; the launch traced here: 210 us
  starting transfers between devices  103 us (48%)
  waiting for transfers between devices  47.9 us (22%)
  matrix products  19.6 us (9%)
  between operations  14.4 us (7%)
  local copies, waits for them, and re-layouts  9.61 us (5%)
  Pallas kernels  9.1 us (4%)
  other arithmetic  6.7 us (3%)
    ppermute x48, starting transfers between devices, move(): return lax.ppermute(x, 'chol', route)  97.2 us
    ppermute x48, waiting for transfers between devices, move(): return lax.ppermute(x, 'chol', route)  47.8 us
    dot_general x2, matrix products, plane_shards(): jnp.einsum('mkpg,gij->mkpij', part, chol_vectors, preferred_element_type=...  9.9 us
    pallas_call x2, Pallas kernels, propagate(): pl.pallas_call(functools.partial(propagate_kernel, len(pieces), planes, r...  9.1 us
    dot_general x2, matrix products, plane_shards(): jnp.einsum('kpej,egj->kpg', held, rot_plane, preferred_element_type=jnp.f...  8.78 us
    all_to_all x1, starting transfers between devices, branch_walkers(): lax.all_to_all(outgoing, 'chol', split_axis=0, concat_axis=0, tiled=True)  5.42 us
    convert_element_type x2, other arithmetic, plane_shards(): made = (jnp.einsum('mkpg,gij->mkpij', part, chol_vectors, preferred_eleme...  4.63 us
  transfers between devices with their start and end apart: 50, of which 11 were waited for; matrix products, arithmetic and copies ran while one was open for 11% of the time, Pallas kernels for 4%

profile of v1, /device:TPU:0, one launch (start us, length us, event | category | flops | bytes accessed | tf_op | source)
XLA Modules:
  0.0 210.0 jit_solution(2244686165440552010)
XLA Ops:
  7.2 3.2 %copy.64 = bf16[1024,4,256]{2,0,1:T(8,128)(2,1)} copy(bf16[1024,4,256]{2,1,0:T(4,128)(2,1)} %param.9) | data formatting | bytes 4194304 | tf_op args[3]
  10.5 3.1 %collective-permute-start.2 = (bf16[32,1024]{1,0:T(8,128)(2,1)S(1)}, bf16[32,1024]{1,0:T(8,128)(2,1)S(1)}, u32[]{:S(2)}, u32[]{:S(2)}) collective-permute-start(bf16[32,1024]{1,0:T(8,128)(2,1)S(1)} %copy-done.5), channel_id=1, source_target_pairs={{0,4},{1,5},{2,6},{3,7},{4,8},{5,9},{6,10},{7,11},{8,12},{9,13},{1... | collective-permute-start | bytes 196616 | tf_op jit(solution)/shard_map/ppermute | solution.py:146
  13.6 2.6 %collective-permute-start.1 = (bf16[32,1024]{1,0:T(8,128)(2,1)S(1)}, bf16[32,1024]{1,0:T(8,128)(2,1)S(1)}, u32[]{:S(2)}, u32[]{:S(2)}) collective-permute-start(bf16[32,1024]{1,0:T(8,128)(2,1)S(1)} %copy-done.5), channel_id=1, source_target_pairs={{0,8},{1,9},{2,10},{3,11},{4,12},{5,13},{6,14},{7,15},{8,0},{9,1},... | collective-permute-start | bytes 196616 | tf_op jit(solution)/shard_map/ppermute | solution.py:146
  16.2 1.3 collective-permute-start
  17.5 0.6 copy.42
  18.3 2.3 %collective-permute-done.1 = bf16[32,1024]{1,0:T(8,128)(2,1)S(1)} collective-permute-done((bf16[32,1024]{1,0:T(8,128)(2,1)S(1)}, bf16[32,1024]{1,0:T(8,128)(2,1)S(1)}, u32[]{:S(2)}, u32[]{:S(2)}) %collective-permute-start.1) | collective-permute-done | bytes 65568 | tf_op jit(solution)/shard_map/ppermute | solution.py:146
  21.0 1.6 collective-permute-start.4
  22.9 0.5 convolution_convert_fusion.1
  23.4 1.5 all_to_all.8
  24.9 5.4 %all-to-all-start = ((bf16[16,2,16384]{2,1,0:T(2,128)(2,1)}), bf16[16,2,16384]{2,1,0:T(2,128)(2,1)}, u32[]{:S(2)}, u32[]{:S(2)}) async-start(bf16[16,2,16384]{2,1,0:T(2,128)(2,1)} %all_to_all.8), calls=%async_computation | async-start | bytes 2097152 | tf_op jit(solution)/shard_map/all_to_all | solution.py:27
  30.3 3.8 %collective-permute-done.5 = bf16[4,32,1024]{2,1,0:T(8,128)(2,1)S(1)} collective-permute-done((bf16[4,32,1024]{2,1,0:T(8,128)(2,1)S(1)}, bf16[4,32,1024]{2,1,0:T(8,128)(2,1)S(1)}, u32[]{:S(2)}, u32[]{:S(2)}) %collective-permute-start.5) | collective-permute-done | bytes 262176 | tf_op jit(solution)/shard_map/ppermute | solution.py:146
  34.1 20.2 %collective-permute-done.4 = bf16[4,32,1024]{2,1,0:T(8,128)(2,1)S(1)} collective-permute-done((bf16[4,32,1024]{2,1,0:T(8,128)(2,1)S(1)}, bf16[4,32,1024]{2,1,0:T(8,128)(2,1)S(1)}, u32[]{:S(2)}, u32[]{:S(2)}) %collective-permute-start.4) | collective-permute-done | bytes 262176 | tf_op jit(solution)/shard_map/ppermute | solution.py:146
  54.4 6.7 %fusion.4 = f32[4,4,16,16,256]{4,2,3,1,0:T(8,128)S(1)} fusion(bf16[1024,16,256,1,1]{2,1,0,4,3:T(8,128)(2,1)} %bitcast.193, bf16[4,4,32,1024]{3,2,1,0:T(8,128)(2,1)S(1)} %pad_maximum_fusion), kind=kOutput, calls=%fused_computation.6 | convolution fusion | flops 2147483648 | bytes 13107200 | tf_op jit(solution)/shard_map/mkpg,gij->mkpij/dot_general | solution.py:169
  61.1 2.3 %fusion.8 = bf16[4,4,16,16,256]{4,3,2,1,0:T(8,128)(2,1)S(1)} fusion(f32[4,4,16,16,256]{4,2,3,1,0:T(8,128)S(1)} %fusion.4), kind=kLoop, calls=%fused_computation.11 | loop fusion | flops 2097152 | bytes 6291456 | tf_op jit(solution)/shard_map/convert_element_type | solution.py:171
  63.4 0.9 slice_bitcast_fusion.4
  64.6 3.2 %fusion.6 = f32[4,4,16,16,256]{4,2,3,1,0:T(8,128)S(1)} fusion(bf16[1024,16,256,1,1]{2,1,0,4,3:T(8,128)(2,1)S(1)} %bitcast.196, bf16[4,4,32,1024]{3,2,1,0:T(8,128)(2,1)S(1)} %pad_maximum_fusion), kind=kOutput, calls=%fused_computation.8 | convolution fusion | flops 2147483648 | bytes 13107200 | tf_op jit(solution)/shard_map/mkpg,gij->mkpij/dot_general | solution.py:169
  67.8 2.9 %collective-permute-start.22 = (bf16[16,16,256]{2,1,0:T(8,128)(2,1)S(1)}, bf16[16,16,256]{2,1,0:T(8,128)(2,1)S(1)}, u32[]{:S(2)}, u32[]{:S(2)}) collective-permute-start(bf16[16,16,256]{2,1,0:T(8,128)(2,1)S(1)} %get-tuple-element.51), channel_id=1, source_target_pairs={{0,8},{1,9},{2,10},{3,11},{4,12},{5,13},{6,14},{7,15},{8,0},{9,1},... | collective-permute-start | bytes 393224 | tf_op jit(solution)/shard_map/ppermute | solution.py:146
  70.7 0.8 collective-permute-start.23
  71.5 1.3 collective-permute-start.25
  72.8 0.8 collective-permute-start.26
  73.6 2.3 %fusion.9 = bf16[4,4,16,16,256]{4,3,2,1,0:T(8,128)(2,1)S(1)} fusion(f32[4,4,16,16,256]{4,2,3,1,0:T(8,128)S(1)} %fusion.6), kind=kLoop, calls=%fused_computation.13 | loop fusion | flops 2097152 | bytes 6291456 | tf_op jit(solution)/shard_map/convert_element_type | solution.py:171
  75.9 2.0 collective-permute-done.22.refs_2_
  78.0 4.9 %collective-permute-start.27 = (bf16[16,16,256]{2,1,0:T(8,128)(2,1)S(1)}, bf16[16,16,256]{2,1,0:T(8,128)(2,1)S(1)}, u32[]{:S(2)}, u32[]{:S(2)}) collective-permute-start(bf16[16,16,256]{2,1,0:T(8,128)(2,1)S(1)} %get-tuple-element.46), channel_id=1, source_target_pairs={{0,13},{1,12},{2,15},{3,14},{4,1},{5,0},{6,3},{7,2},{8,5},{9,4},{1... | collective-permute-start | bytes 393224 | tf_op jit(solution)/shard_map/ppermute | solution.py:146
  82.9 0.4 collective-permute-start.28
  83.3 4.7 %collective-permute-start.29 = (bf16[16,16,256]{2,1,0:T(8,128)(2,1)S(1)}, bf16[16,16,256]{2,1,0:T(8,128)(2,1)S(1)}, u32[]{:S(2)}, u32[]{:S(2)}) collective-permute-start(bf16[16,16,256]{2,1,0:T(8,128)(2,1)S(1)} %get-tuple-element.44), channel_id=1, source_target_pairs={{0,6},{1,7},{2,4},{3,5},{4,10},{5,11},{6,8},{7,9},{8,14},{9,15},{1... | collective-permute-start | bytes 393224 | tf_op jit(solution)/shard_map/ppermute | solution.py:146
  88.0 2.7 %collective-permute-start.30 = (bf16[16,16,256]{2,1,0:T(8,128)(2,1)S(1)}, bf16[16,16,256]{2,1,0:T(8,128)(2,1)S(1)}, u32[]{:S(2)}, u32[]{:S(2)}) collective-permute-start(bf16[16,16,256]{2,1,0:T(8,128)(2,1)S(1)} %get-tuple-element.43), channel_id=1, source_target_pairs={{0,10},{1,11},{2,8},{3,9},{4,14},{5,15},{6,12},{7,13},{8,2},{9,3},... | collective-permute-start | bytes 393224 | tf_op jit(solution)/shard_map/ppermute | solution.py:146
  90.6 2.5 %collective-permute-start.31 = (bf16[16,16,256]{2,1,0:T(8,128)(2,1)S(1)}, bf16[16,16,256]{2,1,0:T(8,128)(2,1)S(1)}, u32[]{:S(2)}, u32[]{:S(2)}) collective-permute-start(bf16[16,16,256]{2,1,0:T(8,128)(2,1)S(1)} %get-tuple-element.42), channel_id=1, source_target_pairs={{0,14},{1,15},{2,12},{3,13},{4,2},{5,3},{6,0},{7,1},{8,6},{9,7},{1... | collective-permute-start | bytes 393224 | tf_op jit(solution)/shard_map/ppermute | solution.py:146
  93.1 1.3 slice_bitcast_fusion.20
  94.4 2.7 %collective-permute-start.32 = (bf16[16,16,256]{2,1,0:T(8,128)(2,1)}, bf16[16,16,256]{2,1,0:T(8,128)(2,1)S(1)}, u32[]{:S(2)}, u32[]{:S(2)}) collective-permute-start(bf16[16,16,256]{2,1,0:T(8,128)(2,1)} %get-tuple-element.41), channel_id=1, source_target_pairs={{0,3},{1,2},{2,1},{3,0},{4,7},{5,6},{6,5},{7,4},{8,11},{9,10},{10,... | collective-permute-start | bytes 393224 | tf_op jit(solution)/shard_map/ppermute | solution.py:146
  97.1 2.9 %collective-permute-start.33 = (bf16[16,16,256]{2,1,0:T(8,128)(2,1)}, bf16[16,16,256]{2,1,0:T(8,128)(2,1)S(1)}, u32[]{:S(2)}, u32[]{:S(2)}) collective-permute-start(bf16[16,16,256]{2,1,0:T(8,128)(2,1)} %get-tuple-element.40), channel_id=1, source_target_pairs={{0,7},{1,6},{2,5},{3,4},{4,11},{5,10},{6,9},{7,8},{8,15},{9,14},{1... | collective-permute-start | bytes 393224 | tf_op jit(solution)/shard_map/ppermute | solution.py:146
  100.0 1.8 collective-permute-start.34
  101.8 3.8 %collective-permute-start.35 = (bf16[16,16,256]{2,1,0:T(8,128)(2,1)}, bf16[16,16,256]{2,1,0:T(8,128)(2,1)S(1)}, u32[]{:S(2)}, u32[]{:S(2)}) collective-permute-start(bf16[16,16,256]{2,1,0:T(8,128)(2,1)} %get-tuple-element.38), channel_id=1, source_target_pairs={{0,15},{1,14},{2,13},{3,12},{4,3},{5,2},{6,1},{7,0},{8,7},{9,6},{1... | collective-permute-start | bytes 393224 | tf_op jit(solution)/shard_map/ppermute | solution.py:146
  105.8 1.5 all_to_all.10
  107.3 5.0 %collective-permute-done.32.refs_12_ = bf16[16,16,256]{2,1,0:T(8,128)(2,1)S(1)} collective-permute-done((bf16[16,16,256]{2,1,0:T(8,128)(2,1)}, bf16[16,16,256]{2,1,0:T(8,128)(2,1)S(1)}, u32[]{:S(2)}, u32[]{:S(2)}) %collective-permute-start.32) | collective-permute-done | bytes 131104 | tf_op jit(solution)/shard_map/ppermute | solution.py:146
  112.4 4.0 %collective-permute-start.8 = (bf16[16,16,256]{2,1,0:T(8,128)(2,1)}, bf16[16,16,256]{2,1,0:T(8,128)(2,1)S(1)}, u32[]{:S(2)}, u32[]{:S(2)}) collective-permute-start(bf16[16,16,256]{2,1,0:T(8,128)(2,1)} %get-tuple-element.34), channel_id=1, source_target_pairs={{0,12},{1,13},{2,14},{3,15},{4,0},{5,1},{6,2},{7,3},{8,4},{9,5},{1... | collective-permute-start | bytes 393224 | tf_op jit(solution)/shard_map/ppermute | solution.py:146
  116.4 6.0 %collective-permute-start.10 = (bf16[16,16,256]{2,1,0:T(8,128)(2,1)}, bf16[16,16,256]{2,1,0:T(8,128)(2,1)S(1)}, u32[]{:S(2)}, u32[]{:S(2)}) collective-permute-start(bf16[16,16,256]{2,1,0:T(8,128)(2,1)} %get-tuple-element.32), channel_id=1, source_target_pairs={{0,5},{1,4},{2,7},{3,6},{4,9},{5,8},{6,11},{7,10},{8,13},{9,12},{1... | collective-permute-start | bytes 393224 | tf_op jit(solution)/shard_map/ppermute | solution.py:146
  122.5 3.3 %collective-permute-start.11 = (bf16[16,16,256]{2,1,0:T(8,128)(2,1)}, bf16[16,16,256]{2,1,0:T(8,128)(2,1)S(1)}, u32[]{:S(2)}, u32[]{:S(2)}) collective-permute-start(bf16[16,16,256]{2,1,0:T(8,128)(2,1)} %get-tuple-element.31), channel_id=1, source_target_pairs={{0,9},{1,8},{2,11},{3,10},{4,13},{5,12},{6,15},{7,14},{8,1},{9,0},... | collective-permute-start | bytes 393224 | tf_op jit(solution)/shard_map/ppermute | solution.py:146
  125.8 0.5 convolution_convert_fusion
  126.3 3.3 %collective-permute-start.12 = (bf16[16,16,256]{2,1,0:T(8,128)(2,1)}, bf16[16,16,256]{2,1,0:T(8,128)(2,1)S(1)}, u32[]{:S(2)}, u32[]{:S(2)}) collective-permute-start(bf16[16,16,256]{2,1,0:T(8,128)(2,1)} %get-tuple-element.30), channel_id=1, source_target_pairs={{0,13},{1,12},{2,15},{3,14},{4,1},{5,0},{6,3},{7,2},{8,5},{9,4},{1... | collective-permute-start | bytes 393224 | tf_op jit(solution)/shard_map/ppermute | solution.py:146
  129.6 1.9 collective-permute-start.13
  131.5 3.9 %collective-permute-start.14 = (bf16[16,16,256]{2,1,0:T(8,128)(2,1)}, bf16[16,16,256]{2,1,0:T(8,128)(2,1)S(1)}, u32[]{:S(2)}, u32[]{:S(2)}) collective-permute-start(bf16[16,16,256]{2,1,0:T(8,128)(2,1)} %get-tuple-element.28), channel_id=1, source_target_pairs={{0,6},{1,7},{2,4},{3,5},{4,10},{5,11},{6,8},{7,9},{8,14},{9,15},{1... | collective-permute-start | bytes 393224 | tf_op jit(solution)/shard_map/ppermute | solution.py:146
  135.4 0.4 collective-permute-start.15
  135.8 2.5 %collective-permute-start.16 = (bf16[16,16,256]{2,1,0:T(8,128)(2,1)}, bf16[16,16,256]{2,1,0:T(8,128)(2,1)S(1)}, u32[]{:S(2)}, u32[]{:S(2)}) collective-permute-start(bf16[16,16,256]{2,1,0:T(8,128)(2,1)} %get-tuple-element.26), channel_id=1, source_target_pairs={{0,14},{1,15},{2,12},{3,13},{4,2},{5,3},{6,0},{7,1},{8,6},{9,7},{1... | collective-permute-start | bytes 393224 | tf_op jit(solution)/shard_map/ppermute | solution.py:146
  138.4 0.8 collective-permute-start.17
  139.2 4.8 %collective-permute-start.18 = (bf16[16,16,256]{2,1,0:T(8,128)(2,1)S(1)}, bf16[16,16,256]{2,1,0:T(8,128)(2,1)S(1)}, u32[]{:S(2)}, u32[]{:S(2)}) collective-permute-start(bf16[16,16,256]{2,1,0:T(8,128)(2,1)S(1)} %copy-done.3), channel_id=1, source_target_pairs={{0,7},{1,6},{2,5},{3,4},{4,11},{5,10},{6,9},{7,8},{8,15},{9,14},{1... | collective-permute-start | bytes 393224 | tf_op jit(solution)/shard_map/ppermute | solution.py:146
  144.0 4.4 %collective-permute-start.19 = (bf16[16,16,256]{2,1,0:T(8,128)(2,1)S(1)}, bf16[16,16,256]{2,1,0:T(8,128)(2,1)S(1)}, u32[]{:S(2)}, u32[]{:S(2)}) collective-permute-start(bf16[16,16,256]{2,1,0:T(8,128)(2,1)S(1)} %copy-done.2), channel_id=1, source_target_pairs={{0,11},{1,10},{2,9},{3,8},{4,15},{5,14},{6,13},{7,12},{8,3},{9,2},... | collective-permute-start | bytes 393224 | tf_op jit(solution)/shard_map/ppermute | solution.py:146
  148.5 3.8 %collective-permute-start.20 = (bf16[16,16,256]{2,1,0:T(8,128)(2,1)S(1)}, bf16[16,16,256]{2,1,0:T(8,128)(2,1)S(1)}, u32[]{:S(2)}, u32[]{:S(2)}) collective-permute-start(bf16[16,16,256]{2,1,0:T(8,128)(2,1)S(1)} %get-tuple-element.22), channel_id=1, source_target_pairs={{0,15},{1,14},{2,13},{3,12},{4,3},{5,2},{6,1},{7,0},{8,7},{9,6},{1... | collective-permute-start | bytes 393224 | tf_op jit(solution)/shard_map/ppermute | solution.py:146
  152.3 4.6 %shard_map.78 = (bf16[16,64,256]{2,1,0:T(8,128)(2,1)S(1)}, bf16[16,16,256]{2,1,0:T(8,128)(2,1)S(1)}, bf16[16,16,256]{2,1,0:T(8,128)(2,1)S(1)}, bf16[16,16,256]{2,1,0:T(8,128)(2,1)S(1)}, bf16[16,16,256]{2,1,0:T(8,128)(2,1)S(1)}) custom-call(s32[20]{0:T(128)S(1)} %stack.143.place_ref, bf16[16,64,256]{2,1,0:T(8,128)(2,1)S(1)} %bitcast.172, ...), custom_call_target="tpu_custom_call" | custom-call | flops 671088640 | bytes 3670016 | tf_op jit(solution)/shard_map/pallas_call | solution.py:109
  156.9 2.6 %collective-permute-start.44 = (bf16[16,16,256]{2,1,0:T(8,128)(2,1)S(1)}, bf16[16,16,256]{2,1,0:T(8,128)(2,1)S(1)}, u32[]{:S(2)}, u32[]{:S(2)}) collective-permute-start(bf16[16,16,256]{2,1,0:T(8,128)(2,1)S(1)} %get-tuple-element.21), channel_id=1, source_target_pairs={{0,12},{1,13},{2,14},{3,15},{4,0},{5,1},{6,2},{7,3},{8,4},{9,5},{1... | collective-permute-start | bytes 393224 | tf_op jit(solution)/shard_map/ppermute | solution.py:146
  160.3 4.5 %shard_map.77 = (bf16[16,64,256]{2,1,0:T(8,128)(2,1)S(1)}, bf16[16,16,256]{2,1,0:T(8,128)(2,1)S(1)}, bf16[16,16,256]{2,1,0:T(8,128)(2,1)S(1)}, bf16[16,16,256]{2,1,0:T(8,128)(2,1)S(1)}, bf16[16,16,256]{2,1,0:T(8,128)(2,1)S(1)}) custom-call(s32[20]{0:T(128)S(1)} %stack.143.place_ref, bf16[16,64,256]{2,1,0:T(8,128)(2,1)S(1)} %bitcast.171, ...), custom_call_target="tpu_custom_call" | custom-call | flops 671088640 | bytes 3670016 | tf_op jit(solution)/shard_map/pallas_call | solution.py:109
  164.8 3.6 %collective-permute-start.38 = (bf16[16,16,256]{2,1,0:T(8,128)(2,1)S(1)}, bf16[16,16,256]{2,1,0:T(8,128)(2,1)S(1)}, u32[]{:S(2)}, u32[]{:S(2)}) collective-permute-start(bf16[16,16,256]{2,1,0:T(8,128)(2,1)S(1)} %get-tuple-element.17), channel_id=1, source_target_pairs={{0,12},{1,13},{2,14},{3,15},{4,0},{5,1},{6,2},{7,3},{8,4},{9,5},{1... | collective-permute-start | bytes 393224 | tf_op jit(solution)/shard_map/ppermute | solution.py:146
  168.4 0.8 collective-permute-start.37
  169.3 1.1 pad_maximum_fusion.1
  170.4 1.3 collective-permute-done.43
  171.8 2.0 collective-permute-done.38
  173.8 9.0 %collective-permute-done.37 = bf16[16,16,256]{2,1,0:T(8,128)(2,1)S(1)} collective-permute-done((bf16[16,16,256]{2,1,0:T(8,128)(2,1)S(1)}, bf16[16,16,256]{2,1,0:T(8,128)(2,1)S(1)}, u32[]{:S(2)}, u32[]{:S(2)}) %collective-permute-start.37) | collective-permute-done | bytes 131104 | tf_op jit(solution)/shard_map/ppermute | solution.py:146
  182.9 6.2 %fusion.28 = (bf16[4,16,1024]{2,1,0:T(8,128)(2,1)S(1)}, f32[4,16,1024]{2,1,0:T(8,128)S(1)}) fusion(bf16[16,1024,256]{2,1,0:T(8,128)(2,1)} %all-gather.2.cloned.1.call-done, bf16[4,16,16,256]{3,2,1,0:T(8,128)(2,1)S(1)} %pad_maximum_fusion.3), kind=kOutput, calls=%fused_computation.79 | convolution fusion | flops 536936448 | bytes 9306112 | tf_op jit(solution)/shard_map/kpej,egj->kpg/dot_general | solution.py:180
  189.2 1.3 collective-permute-start.46
  190.5 2.8 %collective-permute-start.45 = (bf16[16,1024]{1,0:T(8,128)(2,1)S(1)}, bf16[16,1024]{1,0:T(8,128)(2,1)S(1)}, u32[]{:S(2)}, u32[]{:S(2)}) collective-permute-start(bf16[16,1024]{1,0:T(8,128)(2,1)S(1)} %get-tuple-element.61), channel_id=1, source_target_pairs={{0,12},{1,13},{2,14},{3,15},{4,0},{5,1},{6,2},{7,3},{8,4},{9,5},{1... | collective-permute-start | bytes 98312 | tf_op jit(solution)/shard_map/ppermute | solution.py:146
  193.3 2.6 %fusion.29 = (bf16[4,16,1024]{2,1,0:T(8,128)(2,1)S(1)}, f32[4,16,1024]{2,1,0:T(8,128)S(1)}) fusion(bf16[16,1024,256]{2,1,0:T(8,128)(2,1)S(1)} %copy-done, bf16[4,16,16,256]{3,2,1,0:T(8,128)(2,1)S(1)} %pad_maximum_fusion.2), kind=kOutput, calls=%fused_computation.80 | convolution fusion | flops 536936448 | bytes 9306112 | tf_op jit(solution)/shard_map/kpej,egj->kpg/dot_general | solution.py:180
  196.3 1.5 collective-permute-start.40
  197.8 2.8 %collective-permute-start.39 = (bf16[16,1024]{1,0:T(8,128)(2,1)S(1)}, bf16[16,1024]{1,0:T(8,128)(2,1)S(1)}, u32[]{:S(2)}, u32[]{:S(2)}) collective-permute-start(bf16[16,1024]{1,0:T(8,128)(2,1)S(1)} %get-tuple-element.58), channel_id=1, source_target_pairs={{0,12},{1,13},{2,14},{3,15},{4,0},{5,1},{6,2},{7,3},{8,4},{9,5},{1... | collective-permute-start | bytes 98312 | tf_op jit(solution)/shard_map/ppermute | solution.py:146
  200.7 1.4 collective-permute-done.41
  202.5 0.7 pad_maximum_fusion.5
  (90 shorter events, 3.4 us)
Async XLA Ops:
  7.2 3.3 %copy-start.5 = (bf16[32,1024]{1,0:T(8,128)(2,1)S(1)}, bf16[32,1024]{1,0:T(8,128)(2,1)}, u32[]{:S(2)}) copy-start(bf16[32,1024]{1,0:T(8,128)(2,1)} %param.7) | copy-start | bytes 196612
  7.2 10.4 %copy-start.1 = (bf16[32,64,256]{2,1,0:T(8,128)(2,1)S(1)}, bf16[32,64,256]{2,1,0:T(8,128)(2,1)}, u32[]{:S(2)}) copy-start(bf16[32,64,256]{2,1,0:T(8,128)(2,1)} %param.6) | copy-start | bytes 3145732
  7.2 10.9 %copy-start.6 = (s32[1,16,2]{1,2,0:T(2,128)S(1)}, s32[1,16,2]{1,2,0:T(2,128)}, u32[]{:S(2)}) copy-start(s32[1,16,2]{1,2,0:T(2,128)} %param.10) | copy-start | bytes 388
  7.2 175.7 %all-gather.2.cloned.1.call-start = ((), (), s32[]{:S(2)}) async-start(), calls=%async_computation.1 | async-start | bytes 10485760 | tf_op jit(solution)/shard_map/all_gather | solution.py:155
  10.5 7.8 %collective-permute-start.2 = (bf16[32,1024]{1,0:T(8,128)(2,1)S(1)}, bf16[32,1024]{1,0:T(8,128)(2,1)S(1)}, u32[]{:S(2)}, u32[]{:S(2)}) collective-permute-start(bf16[32,1024]{1,0:T(8,128)(2,1)S(1)} %copy-done.5), channel_id=1, source_target_pairs={{0,4},{1,5},{2,6},{3,7},{4,8},{5,9},{6,10},{7,11},{8,12},{9,13},{1... | collective-permute-start | bytes 196616 | tf_op jit(solution)/shard_map/ppermute | solution.py:146
  13.6 7.1 %collective-permute-start.1 = (bf16[32,1024]{1,0:T(8,128)(2,1)S(1)}, bf16[32,1024]{1,0:T(8,128)(2,1)S(1)}, u32[]{:S(2)}, u32[]{:S(2)}) collective-permute-start(bf16[32,1024]{1,0:T(8,128)(2,1)S(1)} %copy-done.5), channel_id=1, source_target_pairs={{0,8},{1,9},{2,10},{3,11},{4,12},{5,13},{6,14},{7,15},{8,0},{9,1},... | collective-permute-start | bytes 196616 | tf_op jit(solution)/shard_map/ppermute | solution.py:146
  16.2 4.7 %collective-permute-start = (bf16[32,1024]{1,0:T(8,128)(2,1)S(1)}, bf16[32,1024]{1,0:T(8,128)(2,1)S(1)}, u32[]{:S(2)}, u32[]{:S(2)}) collective-permute-start(bf16[32,1024]{1,0:T(8,128)(2,1)S(1)} %copy-done.5), channel_id=1, source_target_pairs={{0,12},{1,13},{2,14},{3,15},{4,0},{5,1},{6,2},{7,3},{8,4},{9,5},{1... | collective-permute-start | bytes 196616 | tf_op jit(solution)/shard_map/ppermute | solution.py:146
  21.0 13.1 %collective-permute-start.5 = (bf16[4,32,1024]{2,1,0:T(8,128)(2,1)S(1)}, bf16[4,32,1024]{2,1,0:T(8,128)(2,1)S(1)}, u32[]{:S(2)}, u32[]{:S(2)}) collective-permute-start(bf16[4,32,1024]{2,1,0:T(8,128)(2,1)S(1)} %get-tuple-element.57), channel_id=1, source_target_pairs={{0,3},{1,2},{2,1},{3,0},{4,7},{5,6},{6,5},{7,4},{8,11},{9,10},{10,... | collective-permute-start | bytes 786440 | tf_op jit(solution)/shard_map/ppermute | solution.py:146
  21.0 33.2 %collective-permute-start.4 = (bf16[4,32,1024]{2,1,0:T(8,128)(2,1)S(1)}, bf16[4,32,1024]{2,1,0:T(8,128)(2,1)S(1)}, u32[]{:S(2)}, u32[]{:S(2)}) collective-permute-start(bf16[4,32,1024]{2,1,0:T(8,128)(2,1)S(1)} %get-tuple-element.57), channel_id=1, source_target_pairs={{0,2},{1,3},{2,0},{3,1},{4,6},{5,7},{6,4},{7,5},{8,10},{9,11},{10,... | collective-permute-start | bytes 786440 | tf_op jit(solution)/shard_map/ppermute | solution.py:146
  22.7 31.6 %collective-permute-start.3 = (bf16[4,32,1024]{2,1,0:T(8,128)(2,1)S(1)}, bf16[4,32,1024]{2,1,0:T(8,128)(2,1)S(1)}, u32[]{:S(2)}, u32[]{:S(2)}) collective-permute-start(bf16[4,32,1024]{2,1,0:T(8,128)(2,1)S(1)} %get-tuple-element.57), channel_id=1, source_target_pairs={{0,1},{1,0},{2,3},{3,2},{4,5},{5,4},{6,7},{7,6},{8,9},{9,8},{10,11... | collective-permute-start | bytes 786440 | tf_op jit(solution)/shard_map/ppermute | solution.py:146
  24.9 81.0 %all-to-all-start = ((bf16[16,2,16384]{2,1,0:T(2,128)(2,1)}), bf16[16,2,16384]{2,1,0:T(2,128)(2,1)}, u32[]{:S(2)}, u32[]{:S(2)}) async-start(bf16[16,2,16384]{2,1,0:T(2,128)(2,1)} %all_to_all.8), calls=%async_computation | async-start | bytes 2097152 | tf_op jit(solution)/shard_map/all_to_all | solution.py:27
  54.2 10.4 %slice-start = ((s8[8388608]{0:T(1024)(128)(4,1)}), s8[4194304]{0:T(1024)(128)(4,1)S(1)}, s32[]{:S(2)}) async-start(s8[8388608]{0:T(1024)(128)(4,1)} %bitcast.194), calls=%async_computation.2 | async-start | bytes 8388608
  54.4 10.2 %slice-start.1 = ((s8[8388608]{0:T(1024)(128)(4,1)}), s8[4194304]{0:T(1024)(128)(4,1)S(1)}, s32[]{:S(2)}) async-start(s8[8388608]{0:T(1024)(128)(4,1)} %bitcast.194), calls=%async_computation.3 | async-start | bytes 8388608
  64.4 8.5 %collective-permute-start.21 = (bf16[16,16,256]{2,1,0:T(8,128)(2,1)S(1)}, bf16[16,16,256]{2,1,0:T(8,128)(2,1)S(1)}, u32[]{:S(2)}, u32[]{:S(2)}) collective-permute-start(bf16[16,16,256]{2,1,0:T(8,128)(2,1)S(1)} %get-tuple-element.52), channel_id=1, source_target_pairs={{0,4},{1,5},{2,6},{3,7},{4,8},{5,9},{6,10},{7,11},{8,12},{9,13},{1... | collective-permute-start | bytes 393224 | tf_op jit(solution)/shard_map/ppermute | solution.py:146
  67.8 10.1 %collective-permute-start.22 = (bf16[16,16,256]{2,1,0:T(8,128)(2,1)S(1)}, bf16[16,16,256]{2,1,0:T(8,128)(2,1)S(1)}, u32[]{:S(2)}, u32[]{:S(2)}) collective-permute-start(bf16[16,16,256]{2,1,0:T(8,128)(2,1)S(1)} %get-tuple-element.51), channel_id=1, source_target_pairs={{0,8},{1,9},{2,10},{3,11},{4,12},{5,13},{6,14},{7,15},{8,0},{9,1},... | collective-permute-start | bytes 393224 | tf_op jit(solution)/shard_map/ppermute | solution.py:146
  70.7 12.2 %collective-permute-start.23 = (bf16[16,16,256]{2,1,0:T(8,128)(2,1)S(1)}, bf16[16,16,256]{2,1,0:T(8,128)(2,1)S(1)}, u32[]{:S(2)}, u32[]{:S(2)}) collective-permute-start(bf16[16,16,256]{2,1,0:T(8,128)(2,1)S(1)} %get-tuple-element.50), channel_id=1, source_target_pairs={{0,12},{1,13},{2,14},{3,15},{4,0},{5,1},{6,2},{7,3},{8,4},{9,5},{1... | collective-permute-start | bytes 393224 | tf_op jit(solution)/shard_map/ppermute | solution.py:146
  71.5 11.8 %collective-permute-start.24 = (bf16[16,16,256]{2,1,0:T(8,128)(2,1)S(1)}, bf16[16,16,256]{2,1,0:T(8,128)(2,1)S(1)}, u32[]{:S(2)}, u32[]{:S(2)}) collective-permute-start(bf16[16,16,256]{2,1,0:T(8,128)(2,1)S(1)} %get-tuple-element.49), channel_id=1, source_target_pairs={{0,1},{1,0},{2,3},{3,2},{4,5},{5,4},{6,7},{7,6},{8,9},{9,8},{10,11... | collective-permute-start | bytes 393224 | tf_op jit(solution)/shard_map/ppermute | solution.py:146
  71.5 16.4 %collective-permute-start.25 = (bf16[16,16,256]{2,1,0:T(8,128)(2,1)S(1)}, bf16[16,16,256]{2,1,0:T(8,128)(2,1)S(1)}, u32[]{:S(2)}, u32[]{:S(2)}) collective-permute-start(bf16[16,16,256]{2,1,0:T(8,128)(2,1)S(1)} %get-tuple-element.48), channel_id=1, source_target_pairs={{0,5},{1,4},{2,7},{3,6},{4,9},{5,8},{6,11},{7,10},{8,13},{9,12},{1... | collective-permute-start | bytes 393224 | tf_op jit(solution)/shard_map/ppermute | solution.py:146
  72.8 17.8 %collective-permute-start.26 = (bf16[16,16,256]{2,1,0:T(8,128)(2,1)S(1)}, bf16[16,16,256]{2,1,0:T(8,128)(2,1)S(1)}, u32[]{:S(2)}, u32[]{:S(2)}) collective-permute-start(bf16[16,16,256]{2,1,0:T(8,128)(2,1)S(1)} %get-tuple-element.47), channel_id=1, source_target_pairs={{0,9},{1,8},{2,11},{3,10},{4,13},{5,12},{6,15},{7,14},{8,1},{9,0},... | collective-permute-start | bytes 393224 | tf_op jit(solution)/shard_map/ppermute | solution.py:146
  75.9 49.8 %copy-start.7 = (s32[32]{0:T(128)S(1)}, s32[32]{0:T(128)}, u32[]{:S(2)}) copy-start(s32[32]{0:T(128)} %param.11) | copy-start | bytes 388
  78.0 16.4 %collective-permute-start.27 = (bf16[16,16,256]{2,1,0:T(8,128)(2,1)S(1)}, bf16[16,16,256]{2,1,0:T(8,128)(2,1)S(1)}, u32[]{:S(2)}, u32[]{:S(2)}) collective-permute-start(bf16[16,16,256]{2,1,0:T(8,128)(2,1)S(1)} %get-tuple-element.46), channel_id=1, source_target_pairs={{0,13},{1,12},{2,15},{3,14},{4,1},{5,0},{6,3},{7,2},{8,5},{9,4},{1... | collective-permute-start | bytes 393224 | tf_op jit(solution)/shard_map/ppermute | solution.py:146
  82.9 14.2 %collective-permute-start.28 = (bf16[16,16,256]{2,1,0:T(8,128)(2,1)S(1)}, bf16[16,16,256]{2,1,0:T(8,128)(2,1)S(1)}, u32[]{:S(2)}, u32[]{:S(2)}) collective-permute-start(bf16[16,16,256]{2,1,0:T(8,128)(2,1)S(1)} %get-tuple-element.45), channel_id=1, source_target_pairs={{0,2},{1,3},{2,0},{3,1},{4,6},{5,7},{6,4},{7,5},{8,10},{9,11},{10,... | collective-permute-start | bytes 393224 | tf_op jit(solution)/shard_map/ppermute | solution.py:146
  83.3 16.7 %collective-permute-start.29 = (bf16[16,16,256]{2,1,0:T(8,128)(2,1)S(1)}, bf16[16,16,256]{2,1,0:T(8,128)(2,1)S(1)}, u32[]{:S(2)}, u32[]{:S(2)}) collective-permute-start(bf16[16,16,256]{2,1,0:T(8,128)(2,1)S(1)} %get-tuple-element.44), channel_id=1, source_target_pairs={{0,6},{1,7},{2,4},{3,5},{4,10},{5,11},{6,8},{7,9},{8,14},{9,15},{1... | collective-permute-start | bytes 393224 | tf_op jit(solution)/shard_map/ppermute | solution.py:146
  88.0 13.9 %collective-permute-start.30 = (bf16[16,16,256]{2,1,0:T(8,128)(2,1)S(1)}, bf16[16,16,256]{2,1,0:T(8,128)(2,1)S(1)}, u32[]{:S(2)}, u32[]{:S(2)}) collective-permute-start(bf16[16,16,256]{2,1,0:T(8,128)(2,1)S(1)} %get-tuple-element.43), channel_id=1, source_target_pairs={{0,10},{1,11},{2,8},{3,9},{4,14},{5,15},{6,12},{7,13},{8,2},{9,3},... | collective-permute-start | bytes 393224 | tf_op jit(solution)/shard_map/ppermute | solution.py:146
  90.6 15.0 %collective-permute-start.31 = (bf16[16,16,256]{2,1,0:T(8,128)(2,1)S(1)}, bf16[16,16,256]{2,1,0:T(8,128)(2,1)S(1)}, u32[]{:S(2)}, u32[]{:S(2)}) collective-permute-start(bf16[16,16,256]{2,1,0:T(8,128)(2,1)S(1)} %get-tuple-element.42), channel_id=1, source_target_pairs={{0,14},{1,15},{2,12},{3,13},{4,2},{5,3},{6,0},{7,1},{8,6},{9,7},{1... | collective-permute-start | bytes 393224 | tf_op jit(solution)/shard_map/ppermute | solution.py:146
  94.4 18.0 %collective-permute-start.32 = (bf16[16,16,256]{2,1,0:T(8,128)(2,1)}, bf16[16,16,256]{2,1,0:T(8,128)(2,1)S(1)}, u32[]{:S(2)}, u32[]{:S(2)}) collective-permute-start(bf16[16,16,256]{2,1,0:T(8,128)(2,1)} %get-tuple-element.41), channel_id=1, source_target_pairs={{0,3},{1,2},{2,1},{3,0},{4,7},{5,6},{6,5},{7,4},{8,11},{9,10},{10,... | collective-permute-start | bytes 393224 | tf_op jit(solution)/shard_map/ppermute | solution.py:146
  97.1 15.3 %collective-permute-start.33 = (bf16[16,16,256]{2,1,0:T(8,128)(2,1)}, bf16[16,16,256]{2,1,0:T(8,128)(2,1)S(1)}, u32[]{:S(2)}, u32[]{:S(2)}) collective-permute-start(bf16[16,16,256]{2,1,0:T(8,128)(2,1)} %get-tuple-element.40), channel_id=1, source_target_pairs={{0,7},{1,6},{2,5},{3,4},{4,11},{5,10},{6,9},{7,8},{8,15},{9,14},{1... | collective-permute-start | bytes 393224 | tf_op jit(solution)/shard_map/ppermute | solution.py:146
  100.0 16.4 %collective-permute-start.34 = (bf16[16,16,256]{2,1,0:T(8,128)(2,1)}, bf16[16,16,256]{2,1,0:T(8,128)(2,1)S(1)}, u32[]{:S(2)}, u32[]{:S(2)}) collective-permute-start(bf16[16,16,256]{2,1,0:T(8,128)(2,1)} %get-tuple-element.39), channel_id=1, source_target_pairs={{0,11},{1,10},{2,9},{3,8},{4,15},{5,14},{6,13},{7,12},{8,3},{9,2},... | collective-permute-start | bytes 393224 | tf_op jit(solution)/shard_map/ppermute | solution.py:146
  101.8 14.6 %collective-permute-start.35 = (bf16[16,16,256]{2,1,0:T(8,128)(2,1)}, bf16[16,16,256]{2,1,0:T(8,128)(2,1)S(1)}, u32[]{:S(2)}, u32[]{:S(2)}) collective-permute-start(bf16[16,16,256]{2,1,0:T(8,128)(2,1)} %get-tuple-element.38), channel_id=1, source_target_pairs={{0,15},{1,14},{2,13},{3,12},{4,3},{5,2},{6,1},{7,0},{8,7},{9,6},{1... | collective-permute-start | bytes 393224 | tf_op jit(solution)/shard_map/ppermute | solution.py:146
  105.6 16.9 %collective-permute-start.6 = (bf16[16,16,256]{2,1,0:T(8,128)(2,1)}, bf16[16,16,256]{2,1,0:T(8,128)(2,1)S(1)}, u32[]{:S(2)}, u32[]{:S(2)}) collective-permute-start(bf16[16,16,256]{2,1,0:T(8,128)(2,1)} %get-tuple-element.36), channel_id=1, source_target_pairs={{0,4},{1,5},{2,6},{3,7},{4,8},{5,9},{6,10},{7,11},{8,12},{9,13},{1... | collective-permute-start | bytes 393224 | tf_op jit(solution)/shard_map/ppermute | solution.py:146
  107.3 31.1 %copy-start.4 = (bf16[16,16,256]{2,1,0:T(8,128)(2,1)S(1)}, bf16[16,16,256]{2,1,0:T(8,128)(2,1)}, u32[]{:S(2)}) copy-start(bf16[16,16,256]{2,1,0:T(8,128)(2,1)} %get-tuple-element.25) | copy-start | bytes 393220
  107.3 31.9 %copy-start.3 = (bf16[16,16,256]{2,1,0:T(8,128)(2,1)S(1)}, bf16[16,16,256]{2,1,0:T(8,128)(2,1)}, u32[]{:S(2)}) copy-start(bf16[16,16,256]{2,1,0:T(8,128)(2,1)} %get-tuple-element.24) | copy-start | bytes 393220
  107.3 36.7 %copy-start.2 = (bf16[16,16,256]{2,1,0:T(8,128)(2,1)S(1)}, bf16[16,16,256]{2,1,0:T(8,128)(2,1)}, u32[]{:S(2)}) copy-start(bf16[16,16,256]{2,1,0:T(8,128)(2,1)} %get-tuple-element.23) | copy-start | bytes 393220
  112.4 13.9 %collective-permute-start.7 = (bf16[16,16,256]{2,1,0:T(8,128)(2,1)}, bf16[16,16,256]{2,1,0:T(8,128)(2,1)S(1)}, u32[]{:S(2)}, u32[]{:S(2)}) collective-permute-start(bf16[16,16,256]{2,1,0:T(8,128)(2,1)} %get-tuple-element.35), channel_id=1, source_target_pairs={{0,8},{1,9},{2,10},{3,11},{4,12},{5,13},{6,14},{7,15},{8,0},{9,1},... | collective-permute-start | bytes 393224 | tf_op jit(solution)/shard_map/ppermute | solution.py:146
  112.4 17.2 %collective-permute-start.8 = (bf16[16,16,256]{2,1,0:T(8,128)(2,1)}, bf16[16,16,256]{2,1,0:T(8,128)(2,1)S(1)}, u32[]{:S(2)}, u32[]{:S(2)}) collective-permute-start(bf16[16,16,256]{2,1,0:T(8,128)(2,1)} %get-tuple-element.34), channel_id=1, source_target_pairs={{0,12},{1,13},{2,14},{3,15},{4,0},{5,1},{6,2},{7,3},{8,4},{9,5},{1... | collective-permute-start | bytes 393224 | tf_op jit(solution)/shard_map/ppermute | solution.py:146
  116.4 15.1 %collective-permute-start.9 = (bf16[16,16,256]{2,1,0:T(8,128)(2,1)}, bf16[16,16,256]{2,1,0:T(8,128)(2,1)S(1)}, u32[]{:S(2)}, u32[]{:S(2)}) collective-permute-start(bf16[16,16,256]{2,1,0:T(8,128)(2,1)} %get-tuple-element.33), channel_id=1, source_target_pairs={{0,1},{1,0},{2,3},{3,2},{4,5},{5,4},{6,7},{7,6},{8,9},{9,8},{10,11... | collective-permute-start | bytes 393224 | tf_op jit(solution)/shard_map/ppermute | solution.py:146
  116.4 18.9 %collective-permute-start.10 = (bf16[16,16,256]{2,1,0:T(8,128)(2,1)}, bf16[16,16,256]{2,1,0:T(8,128)(2,1)S(1)}, u32[]{:S(2)}, u32[]{:S(2)}) collective-permute-start(bf16[16,16,256]{2,1,0:T(8,128)(2,1)} %get-tuple-element.32), channel_id=1, source_target_pairs={{0,5},{1,4},{2,7},{3,6},{4,9},{5,8},{6,11},{7,10},{8,13},{9,12},{1... | collective-permute-start | bytes 393224 | tf_op jit(solution)/shard_map/ppermute | solution.py:146
  122.5 13.3 %collective-permute-start.11 = (bf16[16,16,256]{2,1,0:T(8,128)(2,1)}, bf16[16,16,256]{2,1,0:T(8,128)(2,1)S(1)}, u32[]{:S(2)}, u32[]{:S(2)}) collective-permute-start(bf16[16,16,256]{2,1,0:T(8,128)(2,1)} %get-tuple-element.31), channel_id=1, source_target_pairs={{0,9},{1,8},{2,11},{3,10},{4,13},{5,12},{6,15},{7,14},{8,1},{9,0},... | collective-permute-start | bytes 393224 | tf_op jit(solution)/shard_map/ppermute | solution.py:146
  126.3 12.1 %collective-permute-start.12 = (bf16[16,16,256]{2,1,0:T(8,128)(2,1)}, bf16[16,16,256]{2,1,0:T(8,128)(2,1)S(1)}, u32[]{:S(2)}, u32[]{:S(2)}) collective-permute-start(bf16[16,16,256]{2,1,0:T(8,128)(2,1)} %get-tuple-element.30), channel_id=1, source_target_pairs={{0,13},{1,12},{2,15},{3,14},{4,1},{5,0},{6,3},{7,2},{8,5},{9,4},{1... | collective-permute-start | bytes 393224 | tf_op jit(solution)/shard_map/ppermute | solution.py:146
  129.6 9.7 %collective-permute-start.13 = (bf16[16,16,256]{2,1,0:T(8,128)(2,1)}, bf16[16,16,256]{2,1,0:T(8,128)(2,1)S(1)}, u32[]{:S(2)}, u32[]{:S(2)}) collective-permute-start(bf16[16,16,256]{2,1,0:T(8,128)(2,1)} %get-tuple-element.29), channel_id=1, source_target_pairs={{0,2},{1,3},{2,0},{3,1},{4,6},{5,7},{6,4},{7,5},{8,10},{9,11},{10,... | collective-permute-start | bytes 393224 | tf_op jit(solution)/shard_map/ppermute | solution.py:146
  131.5 12.5 %collective-permute-start.14 = (bf16[16,16,256]{2,1,0:T(8,128)(2,1)}, bf16[16,16,256]{2,1,0:T(8,128)(2,1)S(1)}, u32[]{:S(2)}, u32[]{:S(2)}) collective-permute-start(bf16[16,16,256]{2,1,0:T(8,128)(2,1)} %get-tuple-element.28), channel_id=1, source_target_pairs={{0,6},{1,7},{2,4},{3,5},{4,10},{5,11},{6,8},{7,9},{8,14},{9,15},{1... | collective-permute-start | bytes 393224 | tf_op jit(solution)/shard_map/ppermute | solution.py:146
  135.4 13.1 %collective-permute-start.15 = (bf16[16,16,256]{2,1,0:T(8,128)(2,1)}, bf16[16,16,256]{2,1,0:T(8,128)(2,1)S(1)}, u32[]{:S(2)}, u32[]{:S(2)}) collective-permute-start(bf16[16,16,256]{2,1,0:T(8,128)(2,1)} %get-tuple-element.27), channel_id=1, source_target_pairs={{0,10},{1,11},{2,8},{3,9},{4,14},{5,15},{6,12},{7,13},{8,2},{9,3},... | collective-permute-start | bytes 393224 | tf_op jit(solution)/shard_map/ppermute | solution.py:146
  135.8 21.1 %collective-permute-start.16 = (bf16[16,16,256]{2,1,0:T(8,128)(2,1)}, bf16[16,16,256]{2,1,0:T(8,128)(2,1)S(1)}, u32[]{:S(2)}, u32[]{:S(2)}) collective-permute-start(bf16[16,16,256]{2,1,0:T(8,128)(2,1)} %get-tuple-element.26), channel_id=1, source_target_pairs={{0,14},{1,15},{2,12},{3,13},{4,2},{5,3},{6,0},{7,1},{8,6},{9,7},{1... | collective-permute-start | bytes 393224 | tf_op jit(solution)/shard_map/ppermute | solution.py:146
  138.4 21.2 %collective-permute-start.17 = (bf16[16,16,256]{2,1,0:T(8,128)(2,1)S(1)}, bf16[16,16,256]{2,1,0:T(8,128)(2,1)S(1)}, u32[]{:S(2)}, u32[]{:S(2)}) collective-permute-start(bf16[16,16,256]{2,1,0:T(8,128)(2,1)S(1)} %copy-done.4), channel_id=1, source_target_pairs={{0,3},{1,2},{2,1},{3,0},{4,7},{5,6},{6,5},{7,4},{8,11},{9,10},{10,... | collective-permute-start | bytes 393224 | tf_op jit(solution)/shard_map/ppermute | solution.py:146
  139.2 20.8 %collective-permute-start.18 = (bf16[16,16,256]{2,1,0:T(8,128)(2,1)S(1)}, bf16[16,16,256]{2,1,0:T(8,128)(2,1)S(1)}, u32[]{:S(2)}, u32[]{:S(2)}) collective-permute-start(bf16[16,16,256]{2,1,0:T(8,128)(2,1)S(1)} %copy-done.3), channel_id=1, source_target_pairs={{0,7},{1,6},{2,5},{3,4},{4,11},{5,10},{6,9},{7,8},{8,15},{9,14},{1... | collective-permute-start | bytes 393224 | tf_op jit(solution)/shard_map/ppermute | solution.py:146
  144.0 16.3 %collective-permute-start.19 = (bf16[16,16,256]{2,1,0:T(8,128)(2,1)S(1)}, bf16[16,16,256]{2,1,0:T(8,128)(2,1)S(1)}, u32[]{:S(2)}, u32[]{:S(2)}) collective-permute-start(bf16[16,16,256]{2,1,0:T(8,128)(2,1)S(1)} %copy-done.2), channel_id=1, source_target_pairs={{0,11},{1,10},{2,9},{3,8},{4,15},{5,14},{6,13},{7,12},{8,3},{9,2},... | collective-permute-start | bytes 393224 | tf_op jit(solution)/shard_map/ppermute | solution.py:146
  148.5 11.8 %collective-permute-start.20 = (bf16[16,16,256]{2,1,0:T(8,128)(2,1)S(1)}, bf16[16,16,256]{2,1,0:T(8,128)(2,1)S(1)}, u32[]{:S(2)}, u32[]{:S(2)}) collective-permute-start(bf16[16,16,256]{2,1,0:T(8,128)(2,1)S(1)} %get-tuple-element.22), channel_id=1, source_target_pairs={{0,15},{1,14},{2,13},{3,12},{4,3},{5,2},{6,1},{7,0},{8,7},{9,6},{1... | collective-permute-start | bytes 393224 | tf_op jit(solution)/shard_map/ppermute | solution.py:146
  156.9 12.4 %collective-permute-start.44 = (bf16[16,16,256]{2,1,0:T(8,128)(2,1)S(1)}, bf16[16,16,256]{2,1,0:T(8,128)(2,1)S(1)}, u32[]{:S(2)}, u32[]{:S(2)}) collective-permute-start(bf16[16,16,256]{2,1,0:T(8,128)(2,1)S(1)} %get-tuple-element.21), channel_id=1, source_target_pairs={{0,12},{1,13},{2,14},{3,15},{4,0},{5,1},{6,2},{7,3},{8,4},{9,5},{1... | collective-permute-start | bytes 393224 | tf_op jit(solution)/shard_map/ppermute | solution.py:146
  159.7 12.1 %collective-permute-start.43 = (bf16[16,16,256]{2,1,0:T(8,128)(2,1)S(1)}, bf16[16,16,256]{2,1,0:T(8,128)(2,1)S(1)}, u32[]{:S(2)}, u32[]{:S(2)}) collective-permute-start(bf16[16,16,256]{2,1,0:T(8,128)(2,1)S(1)} %get-tuple-element.20), channel_id=1, source_target_pairs={{0,8},{1,9},{2,10},{3,11},{4,12},{5,13},{6,14},{7,15},{8,0},{9,1},... | collective-permute-start | bytes 393224 | tf_op jit(solution)/shard_map/ppermute | solution.py:146
  160.0 11.7 %collective-permute-start.42 = (bf16[16,16,256]{2,1,0:T(8,128)(2,1)S(1)}, bf16[16,16,256]{2,1,0:T(8,128)(2,1)S(1)}, u32[]{:S(2)}, u32[]{:S(2)}) collective-permute-start(bf16[16,16,256]{2,1,0:T(8,128)(2,1)S(1)} %get-tuple-element.19), channel_id=1, source_target_pairs={{0,4},{1,5},{2,6},{3,7},{4,8},{5,9},{6,10},{7,11},{8,12},{9,13},{1... | collective-permute-start | bytes 393224 | tf_op jit(solution)/shard_map/ppermute | solution.py:146
  164.8 9.0 %collective-permute-start.38 = (bf16[16,16,256]{2,1,0:T(8,128)(2,1)S(1)}, bf16[16,16,256]{2,1,0:T(8,128)(2,1)S(1)}, u32[]{:S(2)}, u32[]{:S(2)}) collective-permute-start(bf16[16,16,256]{2,1,0:T(8,128)(2,1)S(1)} %get-tuple-element.17), channel_id=1, source_target_pairs={{0,12},{1,13},{2,14},{3,15},{4,0},{5,1},{6,2},{7,3},{8,4},{9,5},{1... | collective-permute-start | bytes 393224 | tf_op jit(solution)/shard_map/ppermute | solution.py:146
  168.4 14.4 %collective-permute-start.37 = (bf16[16,16,256]{2,1,0:T(8,128)(2,1)S(1)}, bf16[16,16,256]{2,1,0:T(8,128)(2,1)S(1)}, u32[]{:S(2)}, u32[]{:S(2)}) collective-permute-start(bf16[16,16,256]{2,1,0:T(8,128)(2,1)S(1)} %get-tuple-element.16), channel_id=1, source_target_pairs={{0,8},{1,9},{2,10},{3,11},{4,12},{5,13},{6,14},{7,15},{8,0},{9,1},... | collective-permute-start | bytes 393224 | tf_op jit(solution)/shard_map/ppermute | solution.py:146
  169.3 13.6 %collective-permute-start.36 = (bf16[16,16,256]{2,1,0:T(8,128)(2,1)S(1)}, bf16[16,16,256]{2,1,0:T(8,128)(2,1)S(1)}, u32[]{:S(2)}, u32[]{:S(2)}) collective-permute-start(bf16[16,16,256]{2,1,0:T(8,128)(2,1)S(1)} %get-tuple-element.15), channel_id=1, source_target_pairs={{0,4},{1,5},{2,6},{3,7},{4,8},{5,9},{6,10},{7,11},{8,12},{9,13},{1... | collective-permute-start | bytes 393224 | tf_op jit(solution)/shard_map/ppermute | solution.py:146
  182.9 10.4 %copy-start = (bf16[16,1024,256]{2,1,0:T(8,128)(2,1)S(1)}, bf16[16,1024,256]{2,1,0:T(8,128)(2,1)}, u32[]{:S(2)}) copy-start(bf16[16,1024,256]{2,1,0:T(8,128)(2,1)} %all-gather.2.cloned.1.call-done) | copy-start | bytes 25165828
  189.1 8.7 %collective-permute-start.47 = (bf16[16,1024]{1,0:T(8,128)(2,1)S(1)}, bf16[16,1024]{1,0:T(8,128)(2,1)S(1)}, u32[]{:S(2)}, u32[]{:S(2)}) collective-permute-start(bf16[16,1024]{1,0:T(8,128)(2,1)S(1)} %get-tuple-element.62), channel_id=1, source_target_pairs={{0,4},{1,5},{2,6},{3,7},{4,8},{5,9},{6,10},{7,11},{8,12},{9,13},{1... | collective-permute-start | bytes 98312 | tf_op jit(solution)/shard_map/ppermute | solution.py:146
  189.2 11.5 %collective-permute-start.46 = (bf16[16,1024]{1,0:T(8,128)(2,1)S(1)}, bf16[16,1024]{1,0:T(8,128)(2,1)S(1)}, u32[]{:S(2)}, u32[]{:S(2)}) collective-permute-start(bf16[16,1024]{1,0:T(8,128)(2,1)S(1)} %get-tuple-element.63), channel_id=1, source_target_pairs={{0,8},{1,9},{2,10},{3,11},{4,12},{5,13},{6,14},{7,15},{8,0},{9,1},... | collective-permute-start | bytes 98312 | tf_op jit(solution)/shard_map/ppermute | solution.py:146
  190.5 10.2 %collective-permute-start.45 = (bf16[16,1024]{1,0:T(8,128)(2,1)S(1)}, bf16[16,1024]{1,0:T(8,128)(2,1)S(1)}, u32[]{:S(2)}, u32[]{:S(2)}) collective-permute-start(bf16[16,1024]{1,0:T(8,128)(2,1)S(1)} %get-tuple-element.61), channel_id=1, source_target_pairs={{0,12},{1,13},{2,14},{3,15},{4,0},{5,1},{6,2},{7,3},{8,4},{9,5},{1... | collective-permute-start | bytes 98312 | tf_op jit(solution)/shard_map/ppermute | solution.py:146
  196.0 6.1 %collective-permute-start.41 = (bf16[16,1024]{1,0:T(8,128)(2,1)S(1)}, bf16[16,1024]{1,0:T(8,128)(2,1)S(1)}, u32[]{:S(2)}, u32[]{:S(2)}) collective-permute-start(bf16[16,1024]{1,0:T(8,128)(2,1)S(1)} %get-tuple-element.59), channel_id=1, source_target_pairs={{0,4},{1,5},{2,6},{3,7},{4,8},{5,9},{6,10},{7,11},{8,12},{9,13},{1... | collective-permute-start | bytes 98312 | tf_op jit(solution)/shard_map/ppermute | solution.py:146
  196.3 5.8 %collective-permute-start.40 = (bf16[16,1024]{1,0:T(8,128)(2,1)S(1)}, bf16[16,1024]{1,0:T(8,128)(2,1)S(1)}, u32[]{:S(2)}, u32[]{:S(2)}) collective-permute-start(bf16[16,1024]{1,0:T(8,128)(2,1)S(1)} %get-tuple-element.60), channel_id=1, source_target_pairs={{0,8},{1,9},{2,10},{3,11},{4,12},{5,13},{6,14},{7,15},{8,0},{9,1},... | collective-permute-start | bytes 98312 | tf_op jit(solution)/shard_map/ppermute | solution.py:146
  197.8 4.6 %collective-permute-start.39 = (bf16[16,1024]{1,0:T(8,128)(2,1)S(1)}, bf16[16,1024]{1,0:T(8,128)(2,1)S(1)}, u32[]{:S(2)}, u32[]{:S(2)}) collective-permute-start(bf16[16,1024]{1,0:T(8,128)(2,1)S(1)} %get-tuple-element.58), channel_id=1, source_target_pairs={{0,12},{1,13},{2,14},{3,15},{4,0},{5,1},{6,2},{7,3},{8,4},{9,5},{1... | collective-permute-start | bytes 98312 | tf_op jit(solution)/shard_map/ppermute | solution.py:146
Sparse Core Ops, SparseCore 0:
  10.6 97.8 all-gather.1

commit v2 on v1

--- a/solution.py
+++ b/solution.py
@@ -11,27 +11,26 @@
 
 field_scale = 1.5
 degrees = 5
+window = 5
+early_walkers = 6
+electrons_at = 6
+sums_at = 10
 inner = 4
 
 
-def branch_walkers(walkers, send_walker, slot_row):
-    slots, electrons, orbitals = walkers.shape
-    flat_walkers = walkers.reshape(slots, electrons * orbitals)
+def pick_outgoing(walkers, send_walker):
+    slots = walkers.shape[0]
+    flat_walkers = walkers.reshape(slots, -1)
     send_list = send_walker.reshape(-1)
-    choose_send = (send_list[:, None] == jnp.arange(slots, dtype=jnp.int32)[None, :]).astype(
+    choose = (send_list[:, None] == jnp.arange(slots, dtype=jnp.int32)[None, :]).astype(
         jnp.bfloat16
     )
-    outgoing = jnp.dot(choose_send, flat_walkers, preferred_element_type=jnp.float32).astype(
-        jnp.bfloat16
-    )
-    incoming = lax.all_to_all(outgoing, "chol", split_axis=0, concat_axis=0, tiled=True)
-    choose_recv = (
-        slot_row[:, None] == jnp.arange(incoming.shape[0], dtype=jnp.int32)[None, :]
-    ).astype(jnp.bfloat16)
-    branched = jnp.dot(choose_recv, incoming, preferred_element_type=jnp.float32).astype(
-        jnp.bfloat16
-    )
-    return branched.reshape(slots, electrons, orbitals)
+    return jnp.dot(choose, flat_walkers, preferred_element_type=jnp.float32).astype(jnp.bfloat16)
+
+
+def pick_incoming(incoming, slot_row, names):
+    choose = (slot_row[:, None] == names[None, :]).astype(jnp.bfloat16)
+    return jnp.dot(choose, incoming, preferred_element_type=jnp.float32).astype(jnp.bfloat16)
 
 
 def build_operators(fields, chol_vectors):
@@ -47,7 +46,10 @@
 
 def plain_shards(walkers, fields, chol_vectors, rotated, send_walker, slot_row):
     slots, electrons, orbitals = walkers.shape
-    branched = branch_walkers(walkers, send_walker, slot_row)
+    outgoing = pick_outgoing(walkers, send_walker)
+    incoming = lax.all_to_all(outgoing, "chol", split_axis=0, concat_axis=0, tiled=True)
+    names = jnp.arange(incoming.shape[0], dtype=jnp.int32)
+    branched = pick_incoming(incoming, slot_row, names).reshape(slots, electrons, orbitals)
     operator_rows = build_operators(fields, chol_vectors)
     operator = lax.all_to_all(operator_rows, "chol", split_axis=0, concat_axis=1, tiled=True)
     total = branched.astype(jnp.float32)
@@ -127,62 +129,104 @@
     return outs[0], outs[1:]
 
 
+def after(x, *others):
+    return lax.optimization_barrier((x, others))[0]
+
+
 def plane_shards(chunks, walkers, fields, chol_vectors, rotated, send_walker, slot_row):
     slots, electrons, orbitals = walkers.shape
     nchol, rows, _ = chol_vectors.shape
-    elec_local = rotated.shape[1]
     devices = orbitals // rows
     planes = devices // inner
     me = lax.axis_index("chol")
     plane, spot = me // inner, me % inner
     scale = field_scale / math.sqrt(nchol)
+    everywhere = [(k, m) for m in range(inner) for k in range(planes)]
+    shifts = sorted(range(planes), key=lambda k: -min(k, planes - k))
+    order = [(k, m) for m in range(inner) for k in shifts if (k, m) != (0, 0)]
+    sent = []
 
     def move(x, k, m):
+        if len(sent) >= window:
+            x = after(x, sent[-window])
         route = [
             (p * inner + q, (p + k) % planes * inner + (q ^ m))
             for p in range(planes)
             for q in range(inner)
         ]
-        return lax.ppermute(x, "chol", route)
+        sent.append(lax.ppermute(x, "chol", route))
+        return sent[-1]
 
     column = jnp.stack([fields] + [move(fields, planes - k, 0) for k in range(1, planes)])
     everyone = jnp.stack([column] + [move(column, 0, m) for m in range(1, inner)])
 
-    branched = branch_walkers(walkers, send_walker, slot_row)
-
-    rot_mine = jnp.transpose(rotated, (1, 0, 2))
+    targets = jnp.stack([(plane + k) % planes * inner + (spot ^ m) for k, m in everywhere])
+    sources = jnp.stack([(plane - k) % planes * inner + (spot ^ m) for k, m in everywhere])
+    cap = send_walker.shape[2]
+    picked = pick_outgoing(walkers, send_walker[0][targets]).reshape(devices, cap, -1)
+    outgoing = {at: picked[i] for i, at in enumerate(everywhere)}
+    arrived = {(0, 0): outgoing[0, 0]}
+
+    def send_walkers(count):
+        for at in [at for at in order if at not in arrived][:count]:
+            arrived[at] = move(outgoing[at], *at)
+
+    rot_mine = after(jnp.transpose(rotated, (1, 0, 2)), everyone)
     groups = [[p * inner + q for q in range(inner)] for p in range(planes)]
     rot_plane = lax.all_gather(
         rot_mine, "chol", axis=0, tiled=True, axis_index_groups=groups
     )
-
-    sources = [
-        ((plane - k) % planes) * inner + (spot ^ m) for m in range(inner) for k in range(planes)
-    ]
-    place = jnp.stack(sources + [(plane + k) % planes for k in range(planes)]).astype(jnp.int32)
-
-    per = slots // chunks
-    news, biases = [], []
-    for c in range(chunks):
-        part = everyone[:, :, c * per : (c + 1) * per, :]
+    place = jnp.concatenate([sources, (plane + jnp.arange(planes)) % planes]).astype(jnp.int32)
+
+    def operator_rows(part):
         made = (
             jnp.einsum("mkpg,gij->mkpij", part, chol_vectors, preferred_element_type=jnp.float32)
             * scale
         ).astype(jnp.bfloat16)
-        pieces = [
-            made[m, k] if m == 0 and k == 0 else move(made[m, k], k, m)
-            for m in range(inner)
-            for k in range(planes)
-        ]
-        new, parts = propagate(branched[c * per : (c + 1) * per], pieces, place, planes)
-        news.append(new)
-        held = jnp.stack([parts[0]] + [move(parts[k], k, 0) for k in range(1, planes)])
-        sums = jnp.einsum("kpej,egj->kpg", held, rot_plane, preferred_element_type=jnp.float32)
+        return {(k, m): made[m, k] for k, m in everywhere}
+
+    def propagated(phi, landed):
+        return propagate(phi, [landed[at] for at in everywhere], place, planes)
+
+    def send_electrons(parts):
+        return jnp.stack([parts[0]] + [move(parts[k], k, 0) for k in range(1, planes)])
+
+    def bias_sums(held):
+        return jnp.einsum("kpej,egj->kpg", held, rot_plane, preferred_element_type=jnp.float32)
+
+    def return_sums(sums):
         bias = sums[0]
         for k in range(1, planes):
-            back = move(sums[k].astype(jnp.bfloat16), planes - k, 0)
-            bias = bias + back.astype(jnp.float32)
-        biases.append(bias)
+            bias = bias + move(sums[k].astype(jnp.bfloat16), planes - k, 0).astype(jnp.float32)
+        return bias
+
+    send_walkers(early_walkers)
+    news, biases = [], []
+    first, held, sums, mark = 0, None, None, None
+    branched = None
+    for c, per in enumerate(chunks):
+        part = everyone[:, :, first : first + per, :]
+        made = operator_rows(part if mark is None else after(part, mark))
+        landed = {(0, 0): made[0, 0]}
+        for i, at in enumerate(order):
+            landed[at] = move(made[at], *at)
+            if c == 0:
+                send_walkers(1)
+            if i == 4:
+                mark = landed[at]
+            if c > 0 and i == electrons_at:
+                held = send_electrons(parts)
+            if c > 0 and i == sums_at:
+                biases.append(return_sums(bias_sums(held)))
+        if branched is None:
+            send_walkers(devices)
+            rows_in = jnp.concatenate([arrived[at] for at in everywhere])
+            names = (sources[:, None] * cap + jnp.arange(cap, dtype=jnp.int32)).reshape(-1)
+            branched = pick_incoming(rows_in, slot_row, names).reshape(walkers.shape)
+        new, parts = propagated(branched[first : first + per], landed)
+        news.append(new)
+        first += per
+    biases.append(return_sums(bias_sums(send_electrons(parts))))
     return (jnp.concatenate(news), jnp.concatenate(biases))
 
 
@@ -202,7 +246,9 @@
         rows = chol_vectors.shape[1]
         plane_elec = walkers.shape[1] * inner // devices
         if devices % inner == 0 and rows % 16 == 0 and plane_elec % 16 == 0:
-            body = functools.partial(plane_shards, 2 if walkers.shape[0] % 32 == 0 else 1)
+            slots = walkers.shape[0]
+            head = slots * 5 // 8 if slots % 32 == 0 else slots
+            body = functools.partial(plane_shards, (head, slots - head) if head < slots else (slots,))
         else:
             body = plain_shards
         return body(walkers, fields, chol_vectors, rotated, send_walker, slot_row)

time: 213 us -> 238 us (1.12); the launches traced: 210 us -> 237 us
  waiting for transfers between devices: 47.9 us -> 71.1 us
  starting transfers between devices: 103 us -> 89.4 us
  local copies, waits for them, and re-layouts: 9.61 us -> 23.1 us
  matrix products: 19.6 us -> 23.5 us
    ppermute x48 -> x63, waiting for transfers between devices: 47.8 us -> 71.1 us  [move(): sent.append(lax.ppermute(x, 'chol', route))]
    ppermute x48 -> x63, starting transfers between devices: 97.2 us -> 89.3 us  [move(): sent.append(lax.ppermute(x, 'chol', route))]
    unnamed x25 -> x88, local copies, waits for them, and re-layouts: 4.18 us -> 11.5 us
    concatenate x0 -> x2, local copies, waits for them, and re-layouts: none -> 6.67 us  [the longest x1 6.58 us: plane_shards(): rows_in = jnp.concatenate([arrived[at] for at in everywhere])]
    all_to_all x1 -> x0, starting transfers between devices: 5.42 us -> none  [branch_walkers(): lax.all_to_all(outgoing, 'chol', split_axis=0, concat_axis=0, tiled=True)]
    dot_general x6, matrix products: 19.6 us -> 23.5 us  [the longest x2 12.5 us: operator_rows(): jnp.einsum('mkpg,gij->mkpij', part, chol_vectors, preferred_element_type=...]
    all_to_all x2 -> x0, local copies, waits for them, and re-layouts: 2.96 us -> none  [branch_walkers(): lax.all_to_all(outgoing, 'chol', split_axis=0, concat_axis=0, tiled=True)]
  transfers between devices with their start and end apart: 50 -> 64, of which waited for: 11 -> 20; matrix products, arithmetic and copies ran while one was open for 11% -> 17% of each run, Pallas kernels for 4% -> 4%
where the time goes in v2:
time: 238 us; the launch traced here: 237 us
  starting transfers between devices  89.4 us (38%)
  waiting for transfers between devices  71.1 us (30%)
  matrix products  23.5 us (10%)
  local copies, waits for them, and re-layouts  23.1 us (10%)
  between operations  14.9 us (6%)
  Pallas kernels  9.1 us (4%)
  other arithmetic  6.29 us (3%)
    ppermute x63, starting transfers between devices, move(): sent.append(lax.ppermute(x, 'chol', route))  89.3 us
    ppermute x63, waiting for transfers between devices, move(): sent.append(lax.ppermute(x, 'chol', route))  71.1 us
    dot_general x2, matrix products, operator_rows(): jnp.einsum('mkpg,gij->mkpij', part, chol_vectors, preferred_element_type=...  12.5 us
    unnamed x88, local copies, waits for them, and re-layouts  11.5 us
    pallas_call x2, Pallas kernels, propagate(): pl.pallas_call(functools.partial(propagate_kernel, len(pieces), planes, r...  9.1 us
    dot_general x2, matrix products, bias_sums(): jnp.einsum('kpej,egj->kpg', held, rot_plane, preferred_element_type=jnp.f...  8.83 us
    concatenate x1, local copies, waits for them, and re-layouts, plane_shards(): rows_in = jnp.concatenate([arrived[at] for at in everywhere])  6.58 us
  transfers between devices with their start and end apart: 64, of which 20 were waited for; matrix products, arithmetic and copies ran while one was open for 17% of the time, Pallas kernels for 4%

profile of v2, /device:TPU:0, one launch (start us, length us, event | category | flops | bytes accessed | tf_op | source)
XLA Modules:
  0.0 237.4 jit_solution(18284303416089090087)
XLA Ops:
  7.2 3.1 %collective-permute-start = (bf16[32,1024]{1,0:T(8,128)(2,1)}, bf16[32,1024]{1,0:T(8,128)(2,1)S(1)}, u32[]{:S(2)}, u32[]{:S(2)}) collective-permute-start(bf16[32,1024]{1,0:T(8,128)(2,1)} %param.7), channel_id=1, source_target_pairs={{0,4},{1,5},{2,6},{3,7},{4,8},{5,9},{6,10},{7,11},{8,12},{9,13},{1... | collective-permute-start | bytes 196616 | tf_op jit(solution)/shard_map/ppermute | solution.py:157
  10.3 2.6 %collective-permute-start.2 = (bf16[32,1024]{1,0:T(8,128)(2,1)}, bf16[32,1024]{1,0:T(8,128)(2,1)S(1)}, u32[]{:S(2)}, u32[]{:S(2)}) collective-permute-start(bf16[32,1024]{1,0:T(8,128)(2,1)} %param.7), channel_id=1, source_target_pairs={{0,8},{1,9},{2,10},{3,11},{4,12},{5,13},{6,14},{7,15},{8,0},{9,1},... | collective-permute-start | bytes 196616 | tf_op jit(solution)/shard_map/ppermute | solution.py:157
  12.9 1.3 collective-permute-start.4
  15.1 2.5 %collective-permute-done.2 = bf16[32,1024]{1,0:T(8,128)(2,1)S(1)} collective-permute-done((bf16[32,1024]{1,0:T(8,128)(2,1)}, bf16[32,1024]{1,0:T(8,128)(2,1)S(1)}, u32[]{:S(2)}, u32[]{:S(2)}) %collective-permute-start.2) | collective-permute-done | bytes 65568 | tf_op jit(solution)/shard_map/ppermute | solution.py:157
  18.8 1.7 collective-permute-start.8
  20.9 3.2 %copy.64 = bf16[1024,4,256]{2,0,1:T(8,128)(2,1)} copy(bf16[1024,4,256]{2,1,0:T(4,128)(2,1)} %param.9) | data formatting | bytes 4194304 | tf_op args[3]
  24.1 3.0 %collective-permute-done.8 = bf16[4,32,1024]{2,1,0:T(8,128)(2,1)S(1)} collective-permute-done((bf16[4,32,1024]{2,1,0:T(8,128)(2,1)S(1)}, bf16[4,32,1024]{2,1,0:T(8,128)(2,1)S(1)}, u32[]{:S(2)}, u32[]{:S(2)}) %collective-permute-start.8) | collective-permute-done | bytes 262176 | tf_op jit(solution)/shard_map/ppermute | solution.py:157
  27.1 6.0 %collective-permute-done.10 = bf16[4,32,1024]{2,1,0:T(8,128)(2,1)S(1)} collective-permute-done((bf16[4,32,1024]{2,1,0:T(8,128)(2,1)S(1)}, bf16[4,32,1024]{2,1,0:T(8,128)(2,1)S(1)}, u32[]{:S(2)}, u32[]{:S(2)}) %collective-permute-start.10) | collective-permute-done | bytes 262176 | tf_op jit(solution)/shard_map/ppermute | solution.py:157
  35.5 1.5 fusion.32
  37.8 2.8 %collective-permute-start.1 = (bf16[2,16384]{1,0:T(2,128)(2,1)S(1)}, bf16[2,16384]{1,0:T(2,128)(2,1)S(1)}, u32[]{:S(2)}, u32[]{:S(2)}) collective-permute-start(bf16[2,16384]{1,0:T(2,128)(2,1)S(1)} %get-tuple-element.72), channel_id=1, source_target_pairs={{0,4},{1,5},{2,6},{3,7},{4,8},{5,9},{6,10},{7,11},{8,12},{9,13},{1... | collective-permute-start | bytes 196616 | tf_op jit(solution)/shard_map/ppermute | solution.py:157
  40.6 4.0 %collective-permute-done.3 = bf16[2,16384]{1,0:T(2,128)(2,1)S(1)} collective-permute-done((bf16[2,16384]{1,0:T(2,128)(2,1)S(1)}, bf16[2,16384]{1,0:T(2,128)(2,1)S(1)}, u32[]{:S(2)}, u32[]{:S(2)}) %collective-permute-start.3) | collective-permute-done | bytes 65568 | tf_op jit(solution)/shard_map/ppermute | solution.py:157
  44.5 1.4 collective-permute-start.6
  45.9 1.4 collective-permute-start.9
  47.5 6.0 %fusion.6 = f32[4,4,20,16,256]{4,2,3,1,0:T(8,128)S(1)} fusion(bf16[1024,16,256,1,1]{2,1,0,4,3:T(8,128)(2,1)} %bitcast.211, bf16[4,4,32,1024]{3,2,1,0:T(8,128)(2,1)S(1)} %pad_maximum_fusion), kind=kOutput, calls=%fused_computation.9 | convolution fusion | flops 2684354560 | bytes 14417920 | tf_op jit(solution)/shard_map/mkpg,gij->mkpij/dot_general | solution.py:183
  53.5 1.5 fusion.8
  55.7 3.9 %collective-permute-start.17 = (bf16[2,16384]{1,0:T(2,128)(2,1)S(1)}, bf16[2,16384]{1,0:T(2,128)(2,1)S(1)}, u32[]{:S(2)}, u32[]{:S(2)}) collective-permute-start(bf16[2,16384]{1,0:T(2,128)(2,1)S(1)} %get-tuple-element.84), channel_id=1, source_target_pairs={{0,10},{1,11},{2,8},{3,9},{4,14},{5,15},{6,12},{7,13},{8,2},{9,3},... | collective-permute-start | bytes 196616 | tf_op jit(solution)/shard_map/ppermute | solution.py:157
  59.6 1.0 slice_bitcast_fusion.10
  61.2 2.1 collective-permute-start.13
  65.7 1.9 collective-permute-start.22
  67.6 1.8 collective-permute-start.24
  70.0 15.5 %collective-permute-done.15.refs_2_ = bf16[20,16,256]{2,1,0:T(8,128)(2,1)S(1)} collective-permute-done((bf16[20,16,256]{2,1,0:T(8,128)(2,1)S(1)}, bf16[20,16,256]{2,1,0:T(8,128)(2,1)S(1)}, u32[]{:S(2)}, u32[]{:S(2)}) %collective-permute-start.15) | collective-permute-done | bytes 163872 | tf_op jit(solution)/shard_map/ppermute | solution.py:157
  85.5 4.7 %collective-permute-start.19 = (bf16[2,16384]{1,0:T(2,128)(2,1)}, bf16[2,16384]{1,0:T(2,128)(2,1)S(1)}, u32[]{:S(2)}, u32[]{:S(2)}) collective-permute-start(bf16[2,16384]{1,0:T(2,128)(2,1)} %get-tuple-element.86), channel_id=1, source_target_pairs={{0,14},{1,15},{2,12},{3,13},{4,2},{5,3},{6,0},{7,1},{8,6},{9,7},{1... | collective-permute-start | bytes 196616 | tf_op jit(solution)/shard_map/ppermute | solution.py:157
  90.5 2.2 collective-permute-done.16
  92.7 2.0 collective-permute-start.28
  95.3 1.1 collective-permute-start.23
  96.5 2.2 collective-permute-start.25
  98.7 6.5 %fusion.4 = f32[4,4,12,16,256]{4,2,3,1,0:T(8,128)S(1)} fusion(bf16[1024,16,256,1,1]{2,1,0,4,3:T(8,128)(2,1)} %bitcast.212, bf16[4,4,12,1024]{3,2,1,0:T(8,128)(2,1)S(1)} %slice.307), kind=kOutput, calls=%fused_computation.7 | convolution fusion | flops 1610612736 | bytes 11927552 | tf_op jit(solution)/shard_map/mkpg,gij->mkpij/dot_general | solution.py:183
  105.3 2.7 %collective-permute-done.25 = bf16[2,16384]{1,0:T(2,128)(2,1)S(1)} collective-permute-done((bf16[2,16384]{1,0:T(2,128)(2,1)}, bf16[2,16384]{1,0:T(2,128)(2,1)S(1)}, u32[]{:S(2)}, u32[]{:S(2)}) %collective-permute-start.25) | collective-permute-done | bytes 65568 | tf_op jit(solution)/shard_map/ppermute | solution.py:157
  108.6 2.0 collective-permute-start.30
  110.6 2.8 %collective-permute-start.31 = (bf16[20,16,256]{2,1,0:T(8,128)(2,1)S(1)}, bf16[20,16,256]{2,1,0:T(8,128)(2,1)S(1)}, u32[]{:S(2)}, u32[]{:S(2)}) collective-permute-start(bf16[20,16,256]{2,1,0:T(8,128)(2,1)S(1)} %get-tuple-element.98), channel_id=1, source_target_pairs={{0,14},{1,15},{2,12},{3,13},{4,2},{5,3},{6,0},{7,1},{8,6},{9,7},{1... | collective-permute-start | bytes 491528 | tf_op jit(solution)/shard_map/ppermute | solution.py:157
  114.3 1.7 fusion.9
  116.1 3.2 %collective-permute-start.27 = (bf16[2,16384]{1,0:T(2,128)(2,1)S(1)}, bf16[2,16384]{1,0:T(2,128)(2,1)S(1)}, u32[]{:S(2)}, u32[]{:S(2)}) collective-permute-start(bf16[2,16384]{1,0:T(2,128)(2,1)S(1)} %copy-done.21), channel_id=1, source_target_pairs={{0,15},{1,14},{2,13},{3,12},{4,3},{5,2},{6,1},{7,0},{8,7},{9,6},{1... | collective-permute-start | bytes 196616 | tf_op jit(solution)/shard_map/ppermute | solution.py:157
  119.3 2.5 %collective-permute-done.31.refs_11_ = bf16[20,16,256]{2,1,0:T(8,128)(2,1)S(1)} collective-permute-done((bf16[20,16,256]{2,1,0:T(8,128)(2,1)S(1)}, bf16[20,16,256]{2,1,0:T(8,128)(2,1)S(1)}, u32[]{:S(2)}, u32[]{:S(2)}) %collective-permute-start.31) | collective-permute-done | bytes 163872 | tf_op jit(solution)/shard_map/ppermute | solution.py:157
  121.8 2.0 collective-permute-done.21
  123.8 6.2 %collective-permute-start.35 = (bf16[20,16,256]{2,1,0:T(8,128)(2,1)}, bf16[20,16,256]{2,1,0:T(8,128)(2,1)S(1)}, u32[]{:S(2)}, u32[]{:S(2)}) collective-permute-start(bf16[20,16,256]{2,1,0:T(8,128)(2,1)} %get-tuple-element.102), channel_id=1, source_target_pairs={{0,15},{1,14},{2,13},{3,12},{4,3},{5,2},{6,1},{7,0},{8,7},{9,6},{1... | collective-permute-start | bytes 491528 | tf_op jit(solution)/shard_map/ppermute | solution.py:157
  130.0 1.1 slice_bitcast_fusion.19
  131.8 6.6 %concatenate.37 = bf16[32,16384]{1,0:T(8,128)(2,1)} concatenate(bf16[2,16384]{1,0:T(2,128)(2,1)S(1)} %copy-done.10, bf16[2,16384]{1,0:T(2,128)(2,1)S(1)} %copy-done.23, bf16[2,16384]{1,0:T(2,128)(2,1)S(1)} %copy-done.20, bf16[2,16384]{1,0:T(2,128)(2,1)S(1)} %copy-done.27, bf16[2,16384]{1,0:T(2,128)(2,1)} %collective-permute-done.7, bf16[2,16384]{1,0:T(2,128)(2,1)S(1)} %copy-done.29, ...), dimensions={0} | concatenate | bytes 2097152 | tf_op jit(solution)/shard_map/concatenate | solution.py:223
  138.4 1.0 collective-permute-start.38
  140.2 3.6 %collective-permute-start.41 = (bf16[12,16,256]{2,1,0:T(8,128)(2,1)}, bf16[12,16,256]{2,1,0:T(8,128)(2,1)S(1)}, u32[]{:S(2)}, u32[]{:S(2)}) collective-permute-start(bf16[12,16,256]{2,1,0:T(8,128)(2,1)} %get-tuple-element.110), channel_id=1, source_target_pairs={{0,9},{1,8},{2,11},{3,10},{4,13},{5,12},{6,15},{7,14},{8,1},{9,0},... | collective-permute-start | bytes 294920 | tf_op jit(solution)/shard_map/ppermute | solution.py:157
  143.8 1.7 convolution_convert_fusion
  146.5 5.5 %shard_map.77 = (bf16[20,64,256]{2,1,0:T(8,128)(2,1)S(1)}, bf16[20,16,256]{2,1,0:T(8,128)(2,1)S(1)}, bf16[20,16,256]{2,1,0:T(8,128)(2,1)S(1)}, bf16[20,16,256]{2,1,0:T(8,128)(2,1)S(1)}, bf16[20,16,256]{2,1,0:T(8,128)(2,1)S(1)}) custom-call(s32[20]{0:T(128)S(1)} %concatenate.36.place_ref, bf16[20,64,256]{2,1,0:T(8,128)(2,1)S(1)} %slice.332.phi_ref, ...), custom_call_target="tpu_custom_call" | custom-call | flops 838860800 | bytes 4587520 | tf_op jit(solution)/shard_map/pallas_call | solution.py:111
  152.0 1.7 collective-permute-done.41.refs_6_
  155.0 2.5 %collective-permute-start.47 = (bf16[20,16,256]{2,1,0:T(8,128)(2,1)S(1)}, bf16[20,16,256]{2,1,0:T(8,128)(2,1)S(1)}, u32[]{:S(2)}, u32[]{:S(2)}) collective-permute-start(bf16[20,16,256]{2,1,0:T(8,128)(2,1)S(1)} %get-tuple-element.118), channel_id=1, source_target_pairs={{0,4},{1,5},{2,6},{3,7},{4,8},{5,9},{6,10},{7,11},{8,12},{9,13},{1... | collective-permute-start | bytes 491528 | tf_op jit(solution)/shard_map/ppermute | solution.py:157
  158.1 1.3 collective-permute-start.49
  160.8 1.6 collective-permute-start.42
  162.4 8.8 %collective-permute-done.36.refs_1_ = bf16[12,16,256]{2,1,0:T(8,128)(2,1)S(1)} collective-permute-done((bf16[12,16,256]{2,1,0:T(8,128)(2,1)S(1)}, bf16[12,16,256]{2,1,0:T(8,128)(2,1)S(1)}, u32[]{:S(2)}, u32[]{:S(2)}) %collective-permute-start.36) | collective-permute-done | bytes 98336 | tf_op jit(solution)/shard_map/ppermute | solution.py:157
  171.2 2.6 %collective-permute-done.42.refs_7_ = bf16[12,16,256]{2,1,0:T(8,128)(2,1)S(1)} collective-permute-done((bf16[12,16,256]{2,1,0:T(8,128)(2,1)S(1)}, bf16[12,16,256]{2,1,0:T(8,128)(2,1)S(1)}, u32[]{:S(2)}, u32[]{:S(2)}) %collective-permute-start.42) | collective-permute-done | bytes 98336 | tf_op jit(solution)/shard_map/ppermute | solution.py:157
  173.8 3.0 %collective-permute-start.46 = (bf16[12,16,256]{2,1,0:T(8,128)(2,1)}, bf16[12,16,256]{2,1,0:T(8,128)(2,1)S(1)}, u32[]{:S(2)}, u32[]{:S(2)}) collective-permute-start(bf16[12,16,256]{2,1,0:T(8,128)(2,1)} %get-tuple-element.116), channel_id=1, source_target_pairs={{0,10},{1,11},{2,8},{3,9},{4,14},{5,15},{6,12},{7,13},{8,2},{9,3},... | collective-permute-start | bytes 294920 | tf_op jit(solution)/shard_map/ppermute | solution.py:157
  176.8 1.5 collective-permute-start.44
  178.3 1.8 collective-permute-start.48
  180.2 6.2 %fusion.33 = (bf16[4,20,1024]{2,1,0:T(8,128)(2,1)S(1)}, f32[4,20,1024]{2,1,0:T(8,128)S(1)}) fusion(bf16[16,1024,256]{2,1,0:T(8,128)(2,1)} %all-gather.2.cloned.1.call-done, bf16[4,20,16,256]{3,2,1,0:T(8,128)(2,1)S(1)} %pad_maximum_fusion.2), kind=kOutput, calls=%fused_computation.90 | convolution fusion | flops 671170560 | bytes 9535488 | tf_op jit(solution)/shard_map/kpej,egj->kpg/dot_general | solution.py:195
  186.6 2.6 %collective-permute-start.54 = (bf16[20,1024]{1,0:T(8,128)(2,1)S(1)}, bf16[20,1024]{1,0:T(8,128)(2,1)S(1)}, u32[]{:S(2)}, u32[]{:S(2)}) collective-permute-start(bf16[20,1024]{1,0:T(8,128)(2,1)S(1)} %get-tuple-element.128), channel_id=1, source_target_pairs={{0,12},{1,13},{2,14},{3,15},{4,0},{5,1},{6,2},{7,3},{8,4},{9,5},{1... | collective-permute-start | bytes 122888 | tf_op jit(solution)/shard_map/ppermute | solution.py:157
  190.1 5.0 %collective-permute-start.53 = (bf16[12,16,256]{2,1,0:T(8,128)(2,1)S(1)}, bf16[12,16,256]{2,1,0:T(8,128)(2,1)S(1)}, u32[]{:S(2)}, u32[]{:S(2)}) collective-permute-start(bf16[12,16,256]{2,1,0:T(8,128)(2,1)S(1)} %copy-done.14), channel_id=1, source_target_pairs={{0,11},{1,10},{2,9},{3,8},{4,15},{5,14},{6,13},{7,12},{8,3},{9,2},... | collective-permute-start | bytes 294920 | tf_op jit(solution)/shard_map/ppermute | solution.py:157
  195.1 2.5 %collective-permute-start.55 = (bf16[12,16,256]{2,1,0:T(8,128)(2,1)S(1)}, bf16[12,16,256]{2,1,0:T(8,128)(2,1)S(1)}, u32[]{:S(2)}, u32[]{:S(2)}) collective-permute-start(bf16[12,16,256]{2,1,0:T(8,128)(2,1)S(1)} %copy-done.12), channel_id=1, source_target_pairs={{0,15},{1,14},{2,13},{3,12},{4,3},{5,2},{6,1},{7,0},{8,7},{9,6},{1... | collective-permute-start | bytes 294920 | tf_op jit(solution)/shard_map/ppermute | solution.py:157
  198.9 4.3 %collective-permute-done.53.refs_14_ = bf16[12,16,256]{2,1,0:T(8,128)(2,1)S(1)} collective-permute-done((bf16[12,16,256]{2,1,0:T(8,128)(2,1)S(1)}, bf16[12,16,256]{2,1,0:T(8,128)(2,1)S(1)}, u32[]{:S(2)}, u32[]{:S(2)}) %collective-permute-start.53) | collective-permute-done | bytes 98336 | tf_op jit(solution)/shard_map/ppermute | solution.py:157
  203.2 1.7 collective-permute-done.51.refs_12_
  204.9 3.6 %shard_map.78 = (bf16[12,64,256]{2,1,0:T(8,128)(2,1)S(1)}, bf16[12,16,256]{2,1,0:T(8,128)(2,1)S(1)}, bf16[12,16,256]{2,1,0:T(8,128)(2,1)S(1)}, bf16[12,16,256]{2,1,0:T(8,128)(2,1)S(1)}, bf16[12,16,256]{2,1,0:T(8,128)(2,1)S(1)}) custom-call(s32[20]{0:T(128)S(1)} %concatenate.36.place_ref, bf16[12,64,256]{2,1,0:T(8,128)(2,1)S(1)} %slice.333.phi_ref, ...), custom_call_target="tpu_custom_call" | custom-call | flops 503316480 | bytes 2752512 | tf_op jit(solution)/shard_map/pallas_call | solution.py:111
  208.9 2.7 %collective-permute-start.58 = (bf16[12,16,256]{2,1,0:T(8,128)(2,1)S(1)}, bf16[12,16,256]{2,1,0:T(8,128)(2,1)S(1)}, u32[]{:S(2)}, u32[]{:S(2)}) collective-permute-start(bf16[12,16,256]{2,1,0:T(8,128)(2,1)S(1)} %get-tuple-element.136), channel_id=1, source_target_pairs={{0,8},{1,9},{2,10},{3,11},{4,12},{5,13},{6,14},{7,15},{8,0},{9,1},... | collective-permute-start | bytes 294920 | tf_op jit(solution)/shard_map/ppermute | solution.py:157
  211.7 1.6 collective-permute-done.59
  213.3 7.5 %collective-permute-done.58 = bf16[12,16,256]{2,1,0:T(8,128)(2,1)S(1)} collective-permute-done((bf16[12,16,256]{2,1,0:T(8,128)(2,1)S(1)}, bf16[12,16,256]{2,1,0:T(8,128)(2,1)S(1)}, u32[]{:S(2)}, u32[]{:S(2)}) %collective-permute-start.58) | collective-permute-done | bytes 98336 | tf_op jit(solution)/shard_map/ppermute | solution.py:157
  220.8 2.6 %fusion.34 = (bf16[4,12,1024]{2,1,0:T(8,128)(2,1)S(1)}, f32[4,12,1024]{2,1,0:T(8,128)S(1)}) fusion(bf16[16,1024,256]{2,1,0:T(8,128)(2,1)S(1)} %copy-done.6, bf16[4,12,16,256]{3,2,1,0:T(8,128)(2,1)S(1)} %pad_maximum_fusion.3), kind=kOutput, calls=%fused_computation.91 | convolution fusion | flops 402702336 | bytes 9076736 | tf_op jit(solution)/shard_map/kpej,egj->kpg/dot_general | solution.py:195
  223.8 3.6 %collective-permute-start.60 = (bf16[12,1024]{1,0:T(8,128)(2,1)S(1)}, bf16[12,1024]{1,0:T(8,128)(2,1)S(1)}, u32[]{:S(2)}, u32[]{:S(2)}) collective-permute-start(bf16[12,1024]{1,0:T(8,128)(2,1)S(1)} %get-tuple-element.139), channel_id=1, source_target_pairs={{0,12},{1,13},{2,14},{3,15},{4,0},{5,1},{6,2},{7,3},{8,4},{9,5},{1... | collective-permute-start | bytes 73736 | tf_op jit(solution)/shard_map/ppermute | solution.py:157
  227.4 1.1 pad_maximum_fusion.1
  228.4 0.9 collective-permute-done.62
  (194 shorter events, 22.4 us)
Async XLA Ops:
  7.2 173.0 %all-gather.2.cloned.1.call-start = ((), (), s32[]{:S(2)}) async-start(), calls=%async_computation | async-start | bytes 10485760 | tf_op jit(solution)/shard_map/all_gather | solution.py:176
  7.2 7.8 %collective-permute-start = (bf16[32,1024]{1,0:T(8,128)(2,1)}, bf16[32,1024]{1,0:T(8,128)(2,1)S(1)}, u32[]{:S(2)}, u32[]{:S(2)}) collective-permute-start(bf16[32,1024]{1,0:T(8,128)(2,1)} %param.7), channel_id=1, source_target_pairs={{0,4},{1,5},{2,6},{3,7},{4,8},{5,9},{6,10},{7,11},{8,12},{9,13},{1... | collective-permute-start | bytes 196616 | tf_op jit(solution)/shard_map/ppermute | solution.py:157
  10.3 7.3 %collective-permute-start.2 = (bf16[32,1024]{1,0:T(8,128)(2,1)}, bf16[32,1024]{1,0:T(8,128)(2,1)S(1)}, u32[]{:S(2)}, u32[]{:S(2)}) collective-permute-start(bf16[32,1024]{1,0:T(8,128)(2,1)} %param.7), channel_id=1, source_target_pairs={{0,8},{1,9},{2,10},{3,11},{4,12},{5,13},{6,14},{7,15},{8,0},{9,1},... | collective-permute-start | bytes 196616 | tf_op jit(solution)/shard_map/ppermute | solution.py:157
  12.9 4.9 %collective-permute-start.4 = (bf16[32,1024]{1,0:T(8,128)(2,1)}, bf16[32,1024]{1,0:T(8,128)(2,1)S(1)}, u32[]{:S(2)}, u32[]{:S(2)}) collective-permute-start(bf16[32,1024]{1,0:T(8,128)(2,1)} %param.7), channel_id=1, source_target_pairs={{0,12},{1,13},{2,14},{3,15},{4,0},{5,1},{6,2},{7,3},{8,4},{9,5},{1... | collective-permute-start | bytes 196616 | tf_op jit(solution)/shard_map/ppermute | solution.py:157
  18.7 5.4 %collective-permute-start.5 = (bf16[4,32,1024]{2,1,0:T(8,128)(2,1)S(1)}, bf16[4,32,1024]{2,1,0:T(8,128)(2,1)S(1)}, u32[]{:S(2)}, u32[]{:S(2)}) collective-permute-start(bf16[4,32,1024]{2,1,0:T(8,128)(2,1)S(1)} %get-tuple-element.76), channel_id=1, source_target_pairs={{0,1},{1,0},{2,3},{3,2},{4,5},{5,4},{6,7},{7,6},{8,9},{9,8},{10,11... | collective-permute-start | bytes 786440 | tf_op jit(solution)/shard_map/ppermute | solution.py:157
  18.8 8.3 %collective-permute-start.8 = (bf16[4,32,1024]{2,1,0:T(8,128)(2,1)S(1)}, bf16[4,32,1024]{2,1,0:T(8,128)(2,1)S(1)}, u32[]{:S(2)}, u32[]{:S(2)}) collective-permute-start(bf16[4,32,1024]{2,1,0:T(8,128)(2,1)S(1)} %get-tuple-element.76), channel_id=1, source_target_pairs={{0,3},{1,2},{2,1},{3,0},{4,7},{5,6},{6,5},{7,4},{8,11},{9,10},{10,... | collective-permute-start | bytes 786440 | tf_op jit(solution)/shard_map/ppermute | solution.py:157
  20.5 12.6 %collective-permute-start.10 = (bf16[4,32,1024]{2,1,0:T(8,128)(2,1)S(1)}, bf16[4,32,1024]{2,1,0:T(8,128)(2,1)S(1)}, u32[]{:S(2)}, u32[]{:S(2)}) collective-permute-start(bf16[4,32,1024]{2,1,0:T(8,128)(2,1)S(1)} %get-tuple-element.76), channel_id=1, source_target_pairs={{0,2},{1,3},{2,0},{3,1},{4,6},{5,7},{6,4},{7,5},{8,10},{9,11},{10,... | collective-permute-start | bytes 786440 | tf_op jit(solution)/shard_map/ppermute | solution.py:157
  37.0 7.6 %collective-permute-start.3 = (bf16[2,16384]{1,0:T(2,128)(2,1)S(1)}, bf16[2,16384]{1,0:T(2,128)(2,1)S(1)}, u32[]{:S(2)}, u32[]{:S(2)}) collective-permute-start(bf16[2,16384]{1,0:T(2,128)(2,1)S(1)} %get-tuple-element.73), channel_id=1, source_target_pairs={{0,8},{1,9},{2,10},{3,11},{4,12},{5,13},{6,14},{7,15},{8,0},{9,1},... | collective-permute-start | bytes 196616 | tf_op jit(solution)/shard_map/ppermute | solution.py:157
  37.8 25.5 %collective-permute-start.1 = (bf16[2,16384]{1,0:T(2,128)(2,1)S(1)}, bf16[2,16384]{1,0:T(2,128)(2,1)S(1)}, u32[]{:S(2)}, u32[]{:S(2)}) collective-permute-start(bf16[2,16384]{1,0:T(2,128)(2,1)S(1)} %get-tuple-element.72), channel_id=1, source_target_pairs={{0,4},{1,5},{2,6},{3,7},{4,8},{5,9},{6,10},{7,11},{8,12},{9,13},{1... | collective-permute-start | bytes 196616 | tf_op jit(solution)/shard_map/ppermute | solution.py:157
  44.5 16.0 %collective-permute-start.12 = (bf16[2,16384]{1,0:T(2,128)(2,1)S(1)}, bf16[2,16384]{1,0:T(2,128)(2,1)S(1)}, u32[]{:S(2)}, u32[]{:S(2)}) collective-permute-start(bf16[2,16384]{1,0:T(2,128)(2,1)S(1)} %get-tuple-element.79), channel_id=1, source_target_pairs={{0,13},{1,12},{2,15},{3,14},{4,1},{5,0},{6,3},{7,2},{8,5},{9,4},{1... | collective-permute-start | bytes 196616 | tf_op jit(solution)/shard_map/ppermute | solution.py:157
  44.5 10.5 %collective-permute-start.6 = (bf16[2,16384]{1,0:T(2,128)(2,1)S(1)}, bf16[2,16384]{1,0:T(2,128)(2,1)S(1)}, u32[]{:S(2)}, u32[]{:S(2)}) collective-permute-start(bf16[2,16384]{1,0:T(2,128)(2,1)S(1)} %get-tuple-element.74), channel_id=1, source_target_pairs={{0,12},{1,13},{2,14},{3,15},{4,0},{5,1},{6,2},{7,3},{8,4},{9,5},{1... | collective-permute-start | bytes 196616 | tf_op jit(solution)/shard_map/ppermute | solution.py:157
  45.9 9.2 %collective-permute-start.9 = (bf16[2,16384]{1,0:T(2,128)(2,1)S(1)}, bf16[2,16384]{1,0:T(2,128)(2,1)S(1)}, u32[]{:S(2)}, u32[]{:S(2)}) collective-permute-start(bf16[2,16384]{1,0:T(2,128)(2,1)S(1)} %get-tuple-element.77), channel_id=1, source_target_pairs={{0,5},{1,4},{2,7},{3,6},{4,9},{5,8},{6,11},{7,10},{8,13},{9,12},{1... | collective-permute-start | bytes 196616 | tf_op jit(solution)/shard_map/ppermute | solution.py:157
  47.4 16.6 %collective-permute-start.11 = (bf16[2,16384]{1,0:T(2,128)(2,1)S(1)}, bf16[2,16384]{1,0:T(2,128)(2,1)S(1)}, u32[]{:S(2)}, u32[]{:S(2)}) collective-permute-start(bf16[2,16384]{1,0:T(2,128)(2,1)S(1)} %get-tuple-element.78), channel_id=1, source_target_pairs={{0,9},{1,8},{2,11},{3,10},{4,13},{5,12},{6,15},{7,14},{8,1},{9,0},... | collective-permute-start | bytes 196616 | tf_op jit(solution)/shard_map/ppermute | solution.py:157
  55.0 12.5 %collective-permute-start.7 = (bf16[2,16384]{1,0:T(2,128)(2,1)S(1)}, bf16[2,16384]{1,0:T(2,128)(2,1)}, u32[]{:S(2)}, u32[]{:S(2)}) collective-permute-start(bf16[2,16384]{1,0:T(2,128)(2,1)S(1)} %get-tuple-element.75), channel_id=1, source_target_pairs={{0,1},{1,0},{2,3},{3,2},{4,5},{5,4},{6,7},{7,6},{8,9},{9,8},{10,11... | collective-permute-start | bytes 196616 | tf_op jit(solution)/shard_map/ppermute | solution.py:157
  55.7 9.4 %collective-permute-start.17 = (bf16[2,16384]{1,0:T(2,128)(2,1)S(1)}, bf16[2,16384]{1,0:T(2,128)(2,1)S(1)}, u32[]{:S(2)}, u32[]{:S(2)}) collective-permute-start(bf16[2,16384]{1,0:T(2,128)(2,1)S(1)} %get-tuple-element.84), channel_id=1, source_target_pairs={{0,10},{1,11},{2,8},{3,9},{4,14},{5,15},{6,12},{7,13},{8,2},{9,3},... | collective-permute-start | bytes 196616 | tf_op jit(solution)/shard_map/ppermute | solution.py:157
  61.2 8.2 %collective-permute-start.13 = (bf16[20,16,256]{2,1,0:T(8,128)(2,1)S(1)}, bf16[20,16,256]{2,1,0:T(8,128)(2,1)S(1)}, u32[]{:S(2)}, u32[]{:S(2)}) collective-permute-start(bf16[20,16,256]{2,1,0:T(8,128)(2,1)S(1)} %get-tuple-element.80), channel_id=1, source_target_pairs={{0,12},{1,13},{2,14},{3,15},{4,0},{5,1},{6,2},{7,3},{8,4},{9,5},{1... | collective-permute-start | bytes 491528 | tf_op jit(solution)/shard_map/ppermute | solution.py:157
  63.9 21.6 %collective-permute-start.15 = (bf16[20,16,256]{2,1,0:T(8,128)(2,1)S(1)}, bf16[20,16,256]{2,1,0:T(8,128)(2,1)S(1)}, u32[]{:S(2)}, u32[]{:S(2)}) collective-permute-start(bf16[20,16,256]{2,1,0:T(8,128)(2,1)S(1)} %get-tuple-element.82), channel_id=1, source_target_pairs={{0,8},{1,9},{2,10},{3,11},{4,12},{5,13},{6,14},{7,15},{8,0},{9,1},... | collective-permute-start | bytes 491528 | tf_op jit(solution)/shard_map/ppermute | solution.py:157
  64.6 20.8 %collective-permute-start.18 = (bf16[20,16,256]{2,1,0:T(8,128)(2,1)S(1)}, bf16[20,16,256]{2,1,0:T(8,128)(2,1)S(1)}, u32[]{:S(2)}, u32[]{:S(2)}) collective-permute-start(bf16[20,16,256]{2,1,0:T(8,128)(2,1)S(1)} %get-tuple-element.85), channel_id=1, source_target_pairs={{0,4},{1,5},{2,6},{3,7},{4,8},{5,9},{6,10},{7,11},{8,12},{9,13},{1... | collective-permute-start | bytes 491528 | tf_op jit(solution)/shard_map/ppermute | solution.py:157
  65.7 29.6 %collective-permute-start.22 = (bf16[20,16,256]{2,1,0:T(8,128)(2,1)S(1)}, bf16[20,16,256]{2,1,0:T(8,128)(2,1)S(1)}, u32[]{:S(2)}, u32[]{:S(2)}) collective-permute-start(bf16[20,16,256]{2,1,0:T(8,128)(2,1)S(1)} %get-tuple-element.89), channel_id=1, source_target_pairs={{0,5},{1,4},{2,7},{3,6},{4,9},{5,8},{6,11},{7,10},{8,13},{9,12},{1... | collective-permute-start | bytes 491528 | tf_op jit(solution)/shard_map/ppermute | solution.py:157
  67.6 28.9 %collective-permute-start.24 = (bf16[20,16,256]{2,1,0:T(8,128)(2,1)S(1)}, bf16[20,16,256]{2,1,0:T(8,128)(2,1)S(1)}, u32[]{:S(2)}, u32[]{:S(2)}) collective-permute-start(bf16[20,16,256]{2,1,0:T(8,128)(2,1)S(1)} %get-tuple-element.91), channel_id=1, source_target_pairs={{0,9},{1,8},{2,11},{3,10},{4,13},{5,12},{6,15},{7,14},{8,1},{9,0},... | collective-permute-start | bytes 491528 | tf_op jit(solution)/shard_map/ppermute | solution.py:157
  69.4 23.3 %collective-permute-start.14 = (bf16[2,16384]{1,0:T(2,128)(2,1)}, bf16[2,16384]{1,0:T(2,128)(2,1)}, u32[]{:S(2)}, u32[]{:S(2)}) collective-permute-start(bf16[2,16384]{1,0:T(2,128)(2,1)} %get-tuple-element.81), channel_id=1, source_target_pairs={{0,2},{1,3},{2,0},{3,1},{4,6},{5,7},{6,4},{7,5},{8,10},{9,11},{10,... | collective-permute-start | bytes 196616 | tf_op jit(solution)/shard_map/ppermute | solution.py:157
  85.4 7.2 %collective-permute-start.16 = (bf16[2,16384]{1,0:T(2,128)(2,1)}, bf16[2,16384]{1,0:T(2,128)(2,1)S(1)}, u32[]{:S(2)}, u32[]{:S(2)}) collective-permute-start(bf16[2,16384]{1,0:T(2,128)(2,1)} %get-tuple-element.83), channel_id=1, source_target_pairs={{0,6},{1,7},{2,4},{3,5},{4,10},{5,11},{6,8},{7,9},{8,14},{9,15},{1... | collective-permute-start | bytes 196616 | tf_op jit(solution)/shard_map/ppermute | solution.py:157
  85.5 9.2 %collective-permute-start.19 = (bf16[2,16384]{1,0:T(2,128)(2,1)}, bf16[2,16384]{1,0:T(2,128)(2,1)S(1)}, u32[]{:S(2)}, u32[]{:S(2)}) collective-permute-start(bf16[2,16384]{1,0:T(2,128)(2,1)} %get-tuple-element.86), channel_id=1, source_target_pairs={{0,14},{1,15},{2,12},{3,13},{4,2},{5,3},{6,0},{7,1},{8,6},{9,7},{1... | collective-permute-start | bytes 196616 | tf_op jit(solution)/shard_map/ppermute | solution.py:157
  92.7 23.4 %collective-permute-start.26 = (bf16[20,16,256]{2,1,0:T(8,128)(2,1)S(1)}, bf16[20,16,256]{2,1,0:T(8,128)(2,1)S(1)}, u32[]{:S(2)}, u32[]{:S(2)}) collective-permute-start(bf16[20,16,256]{2,1,0:T(8,128)(2,1)S(1)} %get-tuple-element.93), channel_id=1, source_target_pairs={{0,13},{1,12},{2,15},{3,14},{4,1},{5,0},{6,3},{7,2},{8,5},{9,4},{1... | collective-permute-start | bytes 491528 | tf_op jit(solution)/shard_map/ppermute | solution.py:157
  92.7 38.4 %collective-permute-start.28 = (bf16[20,16,256]{2,1,0:T(8,128)(2,1)S(1)}, bf16[20,16,256]{2,1,0:T(8,128)(2,1)S(1)}, u32[]{:S(2)}, u32[]{:S(2)}) collective-permute-start(bf16[20,16,256]{2,1,0:T(8,128)(2,1)S(1)} %get-tuple-element.95), channel_id=1, source_target_pairs={{0,10},{1,11},{2,8},{3,9},{4,14},{5,15},{6,12},{7,13},{8,2},{9,3},... | collective-permute-start | bytes 491528 | tf_op jit(solution)/shard_map/ppermute | solution.py:157
  95.3 18.1 %collective-permute-start.20 = (bf16[20,16,256]{2,1,0:T(8,128)(2,1)S(1)}, bf16[20,16,256]{2,1,0:T(8,128)(2,1)S(1)}, u32[]{:S(2)}, u32[]{:S(2)}) collective-permute-start(bf16[20,16,256]{2,1,0:T(8,128)(2,1)S(1)} %get-tuple-element.87), channel_id=1, source_target_pairs={{0,1},{1,0},{2,3},{3,2},{4,5},{5,4},{6,7},{7,6},{8,9},{9,8},{10,11... | collective-permute-start | bytes 491528 | tf_op jit(solution)/shard_map/ppermute | solution.py:157
  95.3 15.3 %collective-permute-start.23 = (bf16[2,16384]{1,0:T(2,128)(2,1)}, bf16[2,16384]{1,0:T(2,128)(2,1)S(1)}, u32[]{:S(2)}, u32[]{:S(2)}) collective-permute-start(bf16[2,16384]{1,0:T(2,128)(2,1)} %get-tuple-element.90), channel_id=1, source_target_pairs={{0,7},{1,6},{2,5},{3,4},{4,11},{5,10},{6,9},{7,8},{8,15},{9,14},{1... | collective-permute-start | bytes 196616 | tf_op jit(solution)/shard_map/ppermute | solution.py:157
  96.5 11.5 %collective-permute-start.25 = (bf16[2,16384]{1,0:T(2,128)(2,1)}, bf16[2,16384]{1,0:T(2,128)(2,1)S(1)}, u32[]{:S(2)}, u32[]{:S(2)}) collective-permute-start(bf16[2,16384]{1,0:T(2,128)(2,1)} %get-tuple-element.92), channel_id=1, source_target_pairs={{0,11},{1,10},{2,9},{3,8},{4,15},{5,14},{6,13},{7,12},{8,3},{9,2},... | collective-permute-start | bytes 196616 | tf_op jit(solution)/shard_map/ppermute | solution.py:157
  108.6 10.7 %collective-permute-start.30 = (bf16[20,16,256]{2,1,0:T(8,128)(2,1)S(1)}, bf16[20,16,256]{2,1,0:T(8,128)(2,1)S(1)}, u32[]{:S(2)}, u32[]{:S(2)}) collective-permute-start(bf16[20,16,256]{2,1,0:T(8,128)(2,1)S(1)} %get-tuple-element.97), channel_id=1, source_target_pairs={{0,6},{1,7},{2,4},{3,5},{4,10},{5,11},{6,8},{7,9},{8,14},{9,15},{1... | collective-permute-start | bytes 491528 | tf_op jit(solution)/shard_map/ppermute | solution.py:157
  110.6 11.2 %collective-permute-start.31 = (bf16[20,16,256]{2,1,0:T(8,128)(2,1)S(1)}, bf16[20,16,256]{2,1,0:T(8,128)(2,1)S(1)}, u32[]{:S(2)}, u32[]{:S(2)}) collective-permute-start(bf16[20,16,256]{2,1,0:T(8,128)(2,1)S(1)} %get-tuple-element.98), channel_id=1, source_target_pairs={{0,14},{1,15},{2,12},{3,13},{4,2},{5,3},{6,0},{7,1},{8,6},{9,7},{1... | collective-permute-start | bytes 491528 | tf_op jit(solution)/shard_map/ppermute | solution.py:157
  113.4 10.3 %collective-permute-start.21 = (bf16[2,16384]{1,0:T(2,128)(2,1)S(1)}, bf16[2,16384]{1,0:T(2,128)(2,1)S(1)}, u32[]{:S(2)}, u32[]{:S(2)}) collective-permute-start(bf16[2,16384]{1,0:T(2,128)(2,1)S(1)} %copy-done.32), channel_id=1, source_target_pairs={{0,3},{1,2},{2,1},{3,0},{4,7},{5,6},{6,5},{7,4},{8,11},{9,10},{10,... | collective-permute-start | bytes 196616 | tf_op jit(solution)/shard_map/ppermute | solution.py:157
  116.1 15.1 %collective-permute-start.27 = (bf16[2,16384]{1,0:T(2,128)(2,1)S(1)}, bf16[2,16384]{1,0:T(2,128)(2,1)S(1)}, u32[]{:S(2)}, u32[]{:S(2)}) collective-permute-start(bf16[2,16384]{1,0:T(2,128)(2,1)S(1)} %copy-done.21), channel_id=1, source_target_pairs={{0,15},{1,14},{2,13},{3,12},{4,3},{5,2},{6,1},{7,0},{8,7},{9,6},{1... | collective-permute-start | bytes 196616 | tf_op jit(solution)/shard_map/ppermute | solution.py:157
  119.3 19.1 %collective-permute-start.33 = (bf16[20,16,256]{2,1,0:T(8,128)(2,1)}, bf16[20,16,256]{2,1,0:T(8,128)(2,1)S(1)}, u32[]{:S(2)}, u32[]{:S(2)}) collective-permute-start(bf16[20,16,256]{2,1,0:T(8,128)(2,1)} %get-tuple-element.100), channel_id=1, source_target_pairs={{0,7},{1,6},{2,5},{3,4},{4,11},{5,10},{6,9},{7,8},{8,15},{9,14},{1... | collective-permute-start | bytes 491528 | tf_op jit(solution)/shard_map/ppermute | solution.py:157
  121.8 17.6 %collective-permute-start.32 = (bf16[20,16,256]{2,1,0:T(8,128)(2,1)}, bf16[20,16,256]{2,1,0:T(8,128)(2,1)S(1)}, u32[]{:S(2)}, u32[]{:S(2)}) collective-permute-start(bf16[20,16,256]{2,1,0:T(8,128)(2,1)} %get-tuple-element.99), channel_id=1, source_target_pairs={{0,3},{1,2},{2,1},{3,0},{4,7},{5,6},{6,5},{7,4},{8,11},{9,10},{10,... | collective-permute-start | bytes 491528 | tf_op jit(solution)/shard_map/ppermute | solution.py:157
  123.8 16.5 %collective-permute-start.35 = (bf16[20,16,256]{2,1,0:T(8,128)(2,1)}, bf16[20,16,256]{2,1,0:T(8,128)(2,1)S(1)}, u32[]{:S(2)}, u32[]{:S(2)}) collective-permute-start(bf16[20,16,256]{2,1,0:T(8,128)(2,1)} %get-tuple-element.102), channel_id=1, source_target_pairs={{0,15},{1,14},{2,13},{3,12},{4,3},{5,2},{6,1},{7,0},{8,7},{9,6},{1... | collective-permute-start | bytes 491528 | tf_op jit(solution)/shard_map/ppermute | solution.py:157
  131.1 14.7 %collective-permute-start.29 = (bf16[20,16,256]{2,1,0:T(8,128)(2,1)}, bf16[20,16,256]{2,1,0:T(8,128)(2,1)S(1)}, u32[]{:S(2)}, u32[]{:S(2)}) collective-permute-start(bf16[20,16,256]{2,1,0:T(8,128)(2,1)} %get-tuple-element.96), channel_id=1, source_target_pairs={{0,2},{1,3},{2,0},{3,1},{4,6},{5,7},{6,4},{7,5},{8,10},{9,11},{10,... | collective-permute-start | bytes 491528 | tf_op jit(solution)/shard_map/ppermute | solution.py:157
  131.2 14.8 %collective-permute-start.34 = (bf16[20,16,256]{2,1,0:T(8,128)(2,1)S(1)}, bf16[20,16,256]{2,1,0:T(8,128)(2,1)S(1)}, u32[]{:S(2)}, u32[]{:S(2)}) collective-permute-start(bf16[20,16,256]{2,1,0:T(8,128)(2,1)S(1)} %copy-done.11), channel_id=1, source_target_pairs={{0,11},{1,10},{2,9},{3,8},{4,15},{5,14},{6,13},{7,12},{8,3},{9,2},... | collective-permute-start | bytes 491528 | tf_op jit(solution)/shard_map/ppermute | solution.py:157
  138.4 16.6 %collective-permute-start.38 = (bf16[12,16,256]{2,1,0:T(8,128)(2,1)}, bf16[12,16,256]{2,1,0:T(8,128)(2,1)S(1)}, u32[]{:S(2)}, u32[]{:S(2)}) collective-permute-start(bf16[12,16,256]{2,1,0:T(8,128)(2,1)} %get-tuple-element.107), channel_id=1, source_target_pairs={{0,12},{1,13},{2,14},{3,15},{4,0},{5,1},{6,2},{7,3},{8,4},{9,5},{1... | collective-permute-start | bytes 294920 | tf_op jit(solution)/shard_map/ppermute | solution.py:157
  139.4 18.1 %collective-permute-start.40 = (bf16[12,16,256]{2,1,0:T(8,128)(2,1)}, bf16[12,16,256]{2,1,0:T(8,128)(2,1)S(1)}, u32[]{:S(2)}, u32[]{:S(2)}) collective-permute-start(bf16[12,16,256]{2,1,0:T(8,128)(2,1)} %get-tuple-element.109), channel_id=1, source_target_pairs={{0,5},{1,4},{2,7},{3,6},{4,9},{5,8},{6,11},{7,10},{8,13},{9,12},{1... | collective-permute-start | bytes 294920 | tf_op jit(solution)/shard_map/ppermute | solution.py:157
  140.2 13.5 %collective-permute-start.41 = (bf16[12,16,256]{2,1,0:T(8,128)(2,1)}, bf16[12,16,256]{2,1,0:T(8,128)(2,1)S(1)}, u32[]{:S(2)}, u32[]{:S(2)}) collective-permute-start(bf16[12,16,256]{2,1,0:T(8,128)(2,1)} %get-tuple-element.110), channel_id=1, source_target_pairs={{0,9},{1,8},{2,11},{3,10},{4,13},{5,12},{6,15},{7,14},{8,1},{9,0},... | collective-permute-start | bytes 294920 | tf_op jit(solution)/shard_map/ppermute | solution.py:157
  145.8 14.3 %collective-permute-start.37 = (bf16[12,16,256]{2,1,0:T(8,128)(2,1)}, bf16[12,16,256]{2,1,0:T(8,128)(2,1)S(1)}, u32[]{:S(2)}, u32[]{:S(2)}) collective-permute-start(bf16[12,16,256]{2,1,0:T(8,128)(2,1)} %get-tuple-element.106), channel_id=1, source_target_pairs={{0,8},{1,9},{2,10},{3,11},{4,12},{5,13},{6,14},{7,15},{8,0},{9,1},... | collective-permute-start | bytes 294920 | tf_op jit(solution)/shard_map/ppermute | solution.py:157
  154.4 22.4 %collective-permute-start.43 = (bf16[20,16,256]{2,1,0:T(8,128)(2,1)S(1)}, bf16[20,16,256]{2,1,0:T(8,128)(2,1)S(1)}, u32[]{:S(2)}, u32[]{:S(2)}) collective-permute-start(bf16[20,16,256]{2,1,0:T(8,128)(2,1)S(1)} %get-tuple-element.113), channel_id=1, source_target_pairs={{0,8},{1,9},{2,10},{3,11},{4,12},{5,13},{6,14},{7,15},{8,0},{9,1},... | collective-permute-start | bytes 491528 | tf_op jit(solution)/shard_map/ppermute | solution.py:157
  155.0 23.3 %collective-permute-start.47 = (bf16[20,16,256]{2,1,0:T(8,128)(2,1)S(1)}, bf16[20,16,256]{2,1,0:T(8,128)(2,1)S(1)}, u32[]{:S(2)}, u32[]{:S(2)}) collective-permute-start(bf16[20,16,256]{2,1,0:T(8,128)(2,1)S(1)} %get-tuple-element.118), channel_id=1, source_target_pairs={{0,4},{1,5},{2,6},{3,7},{4,8},{5,9},{6,10},{7,11},{8,12},{9,13},{1... | collective-permute-start | bytes 491528 | tf_op jit(solution)/shard_map/ppermute | solution.py:157
  158.1 21.9 %collective-permute-start.49 = (bf16[20,16,256]{2,1,0:T(8,128)(2,1)S(1)}, bf16[20,16,256]{2,1,0:T(8,128)(2,1)S(1)}, u32[]{:S(2)}, u32[]{:S(2)}) collective-permute-start(bf16[20,16,256]{2,1,0:T(8,128)(2,1)S(1)} %get-tuple-element.122), channel_id=1, source_target_pairs={{0,12},{1,13},{2,14},{3,15},{4,0},{5,1},{6,2},{7,3},{8,4},{9,5},{1... | collective-permute-start | bytes 491528 | tf_op jit(solution)/shard_map/ppermute | solution.py:157
  159.5 11.7 %collective-permute-start.36 = (bf16[12,16,256]{2,1,0:T(8,128)(2,1)S(1)}, bf16[12,16,256]{2,1,0:T(8,128)(2,1)S(1)}, u32[]{:S(2)}, u32[]{:S(2)}) collective-permute-start(bf16[12,16,256]{2,1,0:T(8,128)(2,1)S(1)} %copy-done.18), channel_id=1, source_target_pairs={{0,4},{1,5},{2,6},{3,7},{4,8},{5,9},{6,10},{7,11},{8,12},{9,13},{1... | collective-permute-start | bytes 294920 | tf_op jit(solution)/shard_map/ppermute | solution.py:157
  160.8 13.0 %collective-permute-start.42 = (bf16[12,16,256]{2,1,0:T(8,128)(2,1)S(1)}, bf16[12,16,256]{2,1,0:T(8,128)(2,1)S(1)}, u32[]{:S(2)}, u32[]{:S(2)}) collective-permute-start(bf16[12,16,256]{2,1,0:T(8,128)(2,1)S(1)} %copy-done.17), channel_id=1, source_target_pairs={{0,13},{1,12},{2,15},{3,14},{4,1},{5,0},{6,3},{7,2},{8,5},{9,4},{1... | collective-permute-start | bytes 294920 | tf_op jit(solution)/shard_map/ppermute | solution.py:157
  171.2 18.0 %collective-permute-start.39 = (bf16[12,16,256]{2,1,0:T(8,128)(2,1)}, bf16[12,16,256]{2,1,0:T(8,128)(2,1)S(1)}, u32[]{:S(2)}, u32[]{:S(2)}) collective-permute-start(bf16[12,16,256]{2,1,0:T(8,128)(2,1)} %get-tuple-element.108), channel_id=1, source_target_pairs={{0,1},{1,0},{2,3},{3,2},{4,5},{5,4},{6,7},{7,6},{8,9},{9,8},{10,11... | collective-permute-start | bytes 294920 | tf_op jit(solution)/shard_map/ppermute | solution.py:157
  173.8 12.7 %collective-permute-start.46 = (bf16[12,16,256]{2,1,0:T(8,128)(2,1)}, bf16[12,16,256]{2,1,0:T(8,128)(2,1)S(1)}, u32[]{:S(2)}, u32[]{:S(2)}) collective-permute-start(bf16[12,16,256]{2,1,0:T(8,128)(2,1)} %get-tuple-element.116), channel_id=1, source_target_pairs={{0,10},{1,11},{2,8},{3,9},{4,14},{5,15},{6,12},{7,13},{8,2},{9,3},... | collective-permute-start | bytes 294920 | tf_op jit(solution)/shard_map/ppermute | solution.py:157
  176.8 13.3 %collective-permute-start.44 = (bf16[12,16,256]{2,1,0:T(8,128)(2,1)}, bf16[12,16,256]{2,1,0:T(8,128)(2,1)S(1)}, u32[]{:S(2)}, u32[]{:S(2)}) collective-permute-start(bf16[12,16,256]{2,1,0:T(8,128)(2,1)} %get-tuple-element.114), channel_id=1, source_target_pairs={{0,2},{1,3},{2,0},{3,1},{4,6},{5,7},{6,4},{7,5},{8,10},{9,11},{10,... | collective-permute-start | bytes 294920 | tf_op jit(solution)/shard_map/ppermute | solution.py:157
  178.3 11.8 %collective-permute-start.48 = (bf16[12,16,256]{2,1,0:T(8,128)(2,1)}, bf16[12,16,256]{2,1,0:T(8,128)(2,1)S(1)}, u32[]{:S(2)}, u32[]{:S(2)}) collective-permute-start(bf16[12,16,256]{2,1,0:T(8,128)(2,1)} %get-tuple-element.119), channel_id=1, source_target_pairs={{0,14},{1,15},{2,12},{3,13},{4,2},{5,3},{6,0},{7,1},{8,6},{9,7},{1... | collective-permute-start | bytes 294920 | tf_op jit(solution)/shard_map/ppermute | solution.py:157
  186.5 8.6 %collective-permute-start.50 = (bf16[20,1024]{1,0:T(8,128)(2,1)S(1)}, bf16[20,1024]{1,0:T(8,128)(2,1)S(1)}, u32[]{:S(2)}, u32[]{:S(2)}) collective-permute-start(bf16[20,1024]{1,0:T(8,128)(2,1)S(1)} %get-tuple-element.124), channel_id=1, source_target_pairs={{0,8},{1,9},{2,10},{3,11},{4,12},{5,13},{6,14},{7,15},{8,0},{9,1},... | collective-permute-start | bytes 122888 | tf_op jit(solution)/shard_map/ppermute | solution.py:157
  186.6 8.6 %collective-permute-start.54 = (bf16[20,1024]{1,0:T(8,128)(2,1)S(1)}, bf16[20,1024]{1,0:T(8,128)(2,1)S(1)}, u32[]{:S(2)}, u32[]{:S(2)}) collective-permute-start(bf16[20,1024]{1,0:T(8,128)(2,1)S(1)} %get-tuple-element.128), channel_id=1, source_target_pairs={{0,12},{1,13},{2,14},{3,15},{4,0},{5,1},{6,2},{7,3},{8,4},{9,5},{1... | collective-permute-start | bytes 122888 | tf_op jit(solution)/shard_map/ppermute | solution.py:157
  189.2 8.8 %collective-permute-start.45 = (bf16[12,16,256]{2,1,0:T(8,128)(2,1)S(1)}, bf16[12,16,256]{2,1,0:T(8,128)(2,1)S(1)}, u32[]{:S(2)}, u32[]{:S(2)}) collective-permute-start(bf16[12,16,256]{2,1,0:T(8,128)(2,1)S(1)} %copy-done.16), channel_id=1, source_target_pairs={{0,6},{1,7},{2,4},{3,5},{4,10},{5,11},{6,8},{7,9},{8,14},{9,15},{1... | collective-permute-start | bytes 294920 | tf_op jit(solution)/shard_map/ppermute | solution.py:157
  190.1 8.8 %collective-permute-start.52 = (bf16[12,16,256]{2,1,0:T(8,128)(2,1)S(1)}, bf16[12,16,256]{2,1,0:T(8,128)(2,1)S(1)}, u32[]{:S(2)}, u32[]{:S(2)}) collective-permute-start(bf16[12,16,256]{2,1,0:T(8,128)(2,1)S(1)} %copy-done.15), channel_id=1, source_target_pairs={{0,7},{1,6},{2,5},{3,4},{4,11},{5,10},{6,9},{7,8},{8,15},{9,14},{1... | collective-permute-start | bytes 294920 | tf_op jit(solution)/shard_map/ppermute | solution.py:157
  190.1 13.1 %collective-permute-start.53 = (bf16[12,16,256]{2,1,0:T(8,128)(2,1)S(1)}, bf16[12,16,256]{2,1,0:T(8,128)(2,1)S(1)}, u32[]{:S(2)}, u32[]{:S(2)}) collective-permute-start(bf16[12,16,256]{2,1,0:T(8,128)(2,1)S(1)} %copy-done.14), channel_id=1, source_target_pairs={{0,11},{1,10},{2,9},{3,8},{4,15},{5,14},{6,13},{7,12},{8,3},{9,2},... | collective-permute-start | bytes 294920 | tf_op jit(solution)/shard_map/ppermute | solution.py:157
  195.1 9.8 %collective-permute-start.51 = (bf16[12,16,256]{2,1,0:T(8,128)(2,1)S(1)}, bf16[12,16,256]{2,1,0:T(8,128)(2,1)S(1)}, u32[]{:S(2)}, u32[]{:S(2)}) collective-permute-start(bf16[12,16,256]{2,1,0:T(8,128)(2,1)S(1)} %copy-done.13), channel_id=1, source_target_pairs={{0,3},{1,2},{2,1},{3,0},{4,7},{5,6},{6,5},{7,4},{8,11},{9,10},{10,... | collective-permute-start | bytes 294920 | tf_op jit(solution)/shard_map/ppermute | solution.py:157
  195.1 9.8 %collective-permute-start.55 = (bf16[12,16,256]{2,1,0:T(8,128)(2,1)S(1)}, bf16[12,16,256]{2,1,0:T(8,128)(2,1)S(1)}, u32[]{:S(2)}, u32[]{:S(2)}) collective-permute-start(bf16[12,16,256]{2,1,0:T(8,128)(2,1)S(1)} %copy-done.12), channel_id=1, source_target_pairs={{0,15},{1,14},{2,13},{3,12},{4,3},{5,2},{6,1},{7,0},{8,7},{9,6},{1... | collective-permute-start | bytes 294920 | tf_op jit(solution)/shard_map/ppermute | solution.py:157
  198.0 13.7 %collective-permute-start.56 = (bf16[20,1024]{1,0:T(8,128)(2,1)S(1)}, bf16[20,1024]{1,0:T(8,128)(2,1)S(1)}, u32[]{:S(2)}, u32[]{:S(2)}) collective-permute-start(bf16[20,1024]{1,0:T(8,128)(2,1)S(1)} %get-tuple-element.131), channel_id=1, source_target_pairs={{0,4},{1,5},{2,6},{3,7},{4,8},{5,9},{6,10},{7,11},{8,12},{9,13},{1... | collective-permute-start | bytes 122888 | tf_op jit(solution)/shard_map/ppermute | solution.py:157
  208.5 4.8 %collective-permute-start.59 = (bf16[12,16,256]{2,1,0:T(8,128)(2,1)S(1)}, bf16[12,16,256]{2,1,0:T(8,128)(2,1)S(1)}, u32[]{:S(2)}, u32[]{:S(2)}) collective-permute-start(bf16[12,16,256]{2,1,0:T(8,128)(2,1)S(1)} %get-tuple-element.138), channel_id=1, source_target_pairs={{0,12},{1,13},{2,14},{3,15},{4,0},{5,1},{6,2},{7,3},{8,4},{9,5},{1... | collective-permute-start | bytes 294920 | tf_op jit(solution)/shard_map/ppermute | solution.py:157
  208.9 11.8 %collective-permute-start.58 = (bf16[12,16,256]{2,1,0:T(8,128)(2,1)S(1)}, bf16[12,16,256]{2,1,0:T(8,128)(2,1)S(1)}, u32[]{:S(2)}, u32[]{:S(2)}) collective-permute-start(bf16[12,16,256]{2,1,0:T(8,128)(2,1)S(1)} %get-tuple-element.136), channel_id=1, source_target_pairs={{0,8},{1,9},{2,10},{3,11},{4,12},{5,13},{6,14},{7,15},{8,0},{9,1},... | collective-permute-start | bytes 294920 | tf_op jit(solution)/shard_map/ppermute | solution.py:157
  211.7 9.1 %collective-permute-start.57 = (bf16[12,16,256]{2,1,0:T(8,128)(2,1)S(1)}, bf16[12,16,256]{2,1,0:T(8,128)(2,1)S(1)}, u32[]{:S(2)}, u32[]{:S(2)}) collective-permute-start(bf16[12,16,256]{2,1,0:T(8,128)(2,1)S(1)} %get-tuple-element.134), channel_id=1, source_target_pairs={{0,4},{1,5},{2,6},{3,7},{4,8},{5,9},{6,10},{7,11},{8,12},{9,13},{1... | collective-permute-start | bytes 294920 | tf_op jit(solution)/shard_map/ppermute | solution.py:157
  223.5 5.9 %collective-permute-start.62 = (bf16[12,1024]{1,0:T(8,128)(2,1)S(1)}, bf16[12,1024]{1,0:T(8,128)(2,1)S(1)}, u32[]{:S(2)}, u32[]{:S(2)}) collective-permute-start(bf16[12,1024]{1,0:T(8,128)(2,1)S(1)} %get-tuple-element.141), channel_id=1, source_target_pairs={{0,4},{1,5},{2,6},{3,7},{4,8},{5,9},{6,10},{7,11},{8,12},{9,13},{1... | collective-permute-start | bytes 73736 | tf_op jit(solution)/shard_map/ppermute | solution.py:157
  223.6 5.8 %collective-permute-start.61 = (bf16[12,1024]{1,0:T(8,128)(2,1)S(1)}, bf16[12,1024]{1,0:T(8,128)(2,1)S(1)}, u32[]{:S(2)}, u32[]{:S(2)}) collective-permute-start(bf16[12,1024]{1,0:T(8,128)(2,1)S(1)} %get-tuple-element.140), channel_id=1, source_target_pairs={{0,8},{1,9},{2,10},{3,11},{4,12},{5,13},{6,14},{7,15},{8,0},{9,1},... | collective-permute-start | bytes 73736 | tf_op jit(solution)/shard_map/ppermute | solution.py:157
  223.8 6.1 %collective-permute-start.60 = (bf16[12,1024]{1,0:T(8,128)(2,1)S(1)}, bf16[12,1024]{1,0:T(8,128)(2,1)S(1)}, u32[]{:S(2)}, u32[]{:S(2)}) collective-permute-start(bf16[12,1024]{1,0:T(8,128)(2,1)S(1)} %get-tuple-element.139), channel_id=1, source_target_pairs={{0,12},{1,13},{2,14},{3,15},{4,0},{5,1},{6,2},{7,3},{8,4},{9,5},{1... | collective-permute-start | bytes 73736 | tf_op jit(solution)/shard_map/ppermute | solution.py:157
  (42 other events, 613.5 us)
Sparse Core Ops, SparseCore 0:
  33.4 64.6 all-gather.1

commit v3 on v1

--- a/solution.py
+++ b/solution.py
@@ -127,6 +127,10 @@
     return outs[0], outs[1:]
 
 
+def after(x, *others):
+    return lax.optimization_barrier((x, others))[0]
+
+
 def plane_shards(chunks, walkers, fields, chol_vectors, rotated, send_walker, slot_row):
     slots, electrons, orbitals = walkers.shape
     nchol, rows, _ = chol_vectors.shape
@@ -150,40 +154,63 @@
 
     branched = branch_walkers(walkers, send_walker, slot_row)
 
-    rot_mine = jnp.transpose(rotated, (1, 0, 2))
-    groups = [[p * inner + q for q in range(inner)] for p in range(planes)]
-    rot_plane = lax.all_gather(
-        rot_mine, "chol", axis=0, tiled=True, axis_index_groups=groups
-    )
+    rot_mine = after(jnp.transpose(rotated, (1, 0, 2)), everyone)
+    rot_pair = jnp.concatenate([rot_mine, move(rot_mine, 0, 1)])
 
     sources = [
         ((plane - k) % planes) * inner + (spot ^ m) for m in range(inner) for k in range(planes)
     ]
     place = jnp.stack(sources + [(plane + k) % planes for k in range(planes)]).astype(jnp.int32)
 
-    per = slots // chunks
-    news, biases = [], []
-    for c in range(chunks):
-        part = everyone[:, :, c * per : (c + 1) * per, :]
-        made = (
-            jnp.einsum("mkpg,gij->mkpij", part, chol_vectors, preferred_element_type=jnp.float32)
-            * scale
-        ).astype(jnp.bfloat16)
-        pieces = [
-            made[m, k] if m == 0 and k == 0 else move(made[m, k], k, m)
-            for m in range(inner)
-            for k in range(planes)
+    pairs = [(k, m) for m in range(0, inner, 2) for k in range(planes)]
+    quarter = electrons // devices
+
+    def send_electrons(parts):
+        both = parts.reshape(planes, -1, 2, 2 * quarter, orbitals)
+        side = {
+            m: lax.dynamic_index_in_dim(both, (spot ^ m) // 2, 2, keepdims=False)
+            for m in range(0, inner, 2)
+        }
+        held = [side[m][k] if (k, m) == (0, 0) else move(side[m][k], k, m) for k, m in pairs]
+        held = jnp.stack(held).reshape(len(pairs), -1, 2, quarter, orbitals)
+        lanes = [
+            lax.dynamic_index_in_dim(held, (spot + odd) % 2, 2, keepdims=False) for odd in range(2)
         ]
-        new, parts = propagate(branched[c * per : (c + 1) * per], pieces, place, planes)
+        return jnp.concatenate(lanes, 2)
+
+    def return_sums(sums):
+        bias = sums[0]
+        for at, (k, m) in enumerate(pairs[1:], 1):
+            back = move(sums[at].astype(jnp.bfloat16), (planes - k) % planes, m)
+            bias = bias + back.astype(jnp.float32)
+        return bias
+
+    def bias_sums(held):
+        return jnp.einsum("rpej,egj->rpg", held, rot_pair, preferred_element_type=jnp.float32)
+
+    def operator_rows(first, per):
+        part = everyone[:, :, first : first + per, :]
+        made = jnp.einsum(
+            "mkpg,gij->mkpij", part, chol_vectors, preferred_element_type=jnp.float32
+        )
+        return (made * scale).astype(jnp.bfloat16)
+
+    starts = [sum(chunks[:c]) for c in range(len(chunks))]
+    made = [operator_rows(*x) for x in zip(starts, chunks)]
+    made = lax.optimization_barrier(made)
+    order = [(k, m) for m in range(inner) for k in range(planes) if (k, m) != (0, 0)]
+    news, parts = [], []
+    for c, per in enumerate(chunks):
+        landed = {(0, 0): made[c][0, 0]}
+        for k, m in order:
+            landed[k, m] = move(made[c][m, k], k, m)
+        pieces = [landed[k, m] for m in range(inner) for k in range(planes)]
+        phi = branched[starts[c] : starts[c] + per]
+        new, part = propagate(phi, pieces, place, planes)
         news.append(new)
-        held = jnp.stack([parts[0]] + [move(parts[k], k, 0) for k in range(1, planes)])
-        sums = jnp.einsum("kpej,egj->kpg", held, rot_plane, preferred_element_type=jnp.float32)
-        bias = sums[0]
-        for k in range(1, planes):
-            back = move(sums[k].astype(jnp.bfloat16), planes - k, 0)
-            bias = bias + back.astype(jnp.float32)
-        biases.append(bias)
-    return (jnp.concatenate(news), jnp.concatenate(biases))
+        parts.append(jnp.stack(part))
+    bias = return_sums(bias_sums(send_electrons(jnp.concatenate(parts, 1))))
+    return (jnp.concatenate(news), bias)
 
 
 def solution(mesh):
@@ -202,7 +229,10 @@
         rows = chol_vectors.shape[1]
         plane_elec = walkers.shape[1] * inner // devices
         if devices % inner == 0 and rows % 16 == 0 and plane_elec % 16 == 0:
-            body = functools.partial(plane_shards, 2 if walkers.shape[0] % 32 == 0 else 1)
+            slots = walkers.shape[0]
+            head = slots * 4 // 8
+            chunks = (head, slots - head) if slots % 32 == 0 else (slots,)
+            body = functools.partial(plane_shards, chunks)
         else:
             body = plain_shards
         return body(walkers, fields, chol_vectors, rotated, send_walker, slot_row)

time: 213 us -> 195 us (0.915); the launches traced: 210 us -> 195 us
  between operations: 14.4 us -> 1.07 us
  matrix products: 19.6 us -> 15.5 us
  waiting for transfers between devices: 47.9 us -> 44.5 us
  local copies, waits for them, and re-layouts: 9.61 us -> 12.4 us
    dot_general x4 -> x3, matrix products: 18.7 us -> 13.3 us  [the longest x2 9.8 us: operator_rows(): jnp.einsum('mkpg,gij->mkpij', part, chol_vectors, preferred_element_type=...]
    ppermute x48 -> x51, waiting for transfers between devices: 47.8 us -> 44.5 us  [move(): return lax.ppermute(x, 'chol', route)]
    ppermute x48 -> x51, starting transfers between devices: 97.2 us -> 100 us  [move(): return lax.ppermute(x, 'chol', route)]
    unnamed x25 -> x18, local copies, waits for them, and re-layouts: 4.18 us -> 6.07 us
    convert_element_type x2 -> x1, other arithmetic: 4.63 us -> 4.61 us  [operator_rows(): return (made * scale).astype(jnp.bfloat16)]
  transfers between devices with their start and end apart: 50 -> 52, of which waited for: 11 -> 16; matrix products, arithmetic and copies ran while one was open for 11% -> 14% of each run, Pallas kernels for 4% -> 5%
where the time goes in v3:
time: 195 us
  starting transfers between devices  105 us (54%)
  waiting for transfers between devices  44.5 us (23%)
  matrix products  15.5 us (8%)
  local copies, waits for them, and re-layouts  12.4 us (6%)
  Pallas kernels  9.1 us (5%)
  other arithmetic  7.55 us (4%)
    ppermute x51, starting transfers between devices, move(): return lax.ppermute(x, 'chol', route)  100 us
    ppermute x51, waiting for transfers between devices, move(): return lax.ppermute(x, 'chol', route)  44.5 us
    dot_general x2, matrix products, operator_rows(): jnp.einsum('mkpg,gij->mkpij', part, chol_vectors, preferred_element_type=...  9.8 us
    pallas_call x2, Pallas kernels, propagate(): pl.pallas_call(functools.partial(propagate_kernel, len(pieces), planes, r...  9.1 us
    unnamed x18, local copies, waits for them, and re-layouts  6.07 us
    convert_element_type x1, other arithmetic, operator_rows(): return (made * scale).astype(jnp.bfloat16)  4.61 us
    all_to_all x1, starting transfers between devices, branch_walkers(): lax.all_to_all(outgoing, 'chol', split_axis=0, concat_axis=0, tiled=True)  4.35 us
  transfers between devices with their start and end apart: 52, of which 16 were waited for; matrix products, arithmetic and copies ran while one was open for 14% of the time, Pallas kernels for 5%

profile of v3, /device:TPU:0, one launch (start us, length us, event | category | flops | bytes accessed | tf_op | source)
XLA Modules:
  0.0 194.8 jit_solution(18114141753388431683)
XLA Ops:
  0.6 5.1 %collective-permute-start = (bf16[32,1024]{1,0:T(8,128)(2,1)}, bf16[32,1024]{1,0:T(8,128)(2,1)S(1)}, u32[]{:S(2)}, u32[]{:S(2)}) collective-permute-start(bf16[32,1024]{1,0:T(8,128)(2,1)} %param.7), channel_id=1, source_target_pairs={{0,12},{1,13},{2,14},{3,15},{4,0},{5,1},{6,2},{7,3},{8,4},{9,5},{1... | collective-permute-start | bytes 196616 | tf_op jit(solution)/shard_map/ppermute | solution.py:150
  5.7 1.0 collective-permute-start.2
  6.7 1.8 copy.53
  9.4 3.0 %collective-permute-done.1 = bf16[32,1024]{1,0:T(8,128)(2,1)S(1)} collective-permute-done((bf16[32,1024]{1,0:T(8,128)(2,1)}, bf16[32,1024]{1,0:T(8,128)(2,1)S(1)}, u32[]{:S(2)}, u32[]{:S(2)}) %collective-permute-start.1) | collective-permute-done | bytes 65568 | tf_op jit(solution)/shard_map/ppermute | solution.py:150
  12.4 0.9 fusion.23
  13.4 1.6 collective-permute-start.4
  15.7 1.5 all_to_all.8
  17.2 4.3 %all-to-all-start = ((bf16[16,2,16384]{2,1,0:T(2,128)(2,1)}), bf16[16,2,16384]{2,1,0:T(2,128)(2,1)}, u32[]{:S(2)}, u32[]{:S(2)}) async-start(bf16[16,2,16384]{2,1,0:T(2,128)(2,1)} %all_to_all.8), calls=%async_computation | async-start | bytes 2097152 | tf_op jit(solution)/shard_map/all_to_all | solution.py:27
  21.6 1.0 collective-permute-done.4
  22.6 6.9 %collective-permute-done.5 = bf16[4,32,1024]{2,1,0:T(8,128)(2,1)S(1)} collective-permute-done((bf16[4,32,1024]{2,1,0:T(8,128)(2,1)S(1)}, bf16[4,32,1024]{2,1,0:T(8,128)(2,1)S(1)}, u32[]{:S(2)}, u32[]{:S(2)}) %collective-permute-start.5) | collective-permute-done | bytes 262176 | tf_op jit(solution)/shard_map/ppermute | solution.py:150
  29.6 6.6 %fusion = f32[4,4,16,16,256]{4,2,3,1,0:T(8,128)S(1)} fusion(bf16[1024,16,256,1,1]{2,1,0,4,3:T(8,128)(2,1)} %bitcast.223, bf16[4,4,32,1024]{3,2,1,0:T(8,128)(2,1)S(1)} %pad_maximum_fusion), kind=kOutput, calls=%fused_computation.2 | convolution fusion | flops 2147483648 | bytes 13107200 | tf_op jit(solution)/shard_map/mkpg,gij->mkpij/dot_general | solution.py:193
  36.2 3.2 %fusion.2 = f32[4,4,16,16,256]{4,2,3,1,0:T(8,128)S(1)} fusion(bf16[1024,16,256,1,1]{2,1,0,4,3:T(8,128)(2,1)S(1)} %bitcast.226, bf16[4,4,32,1024]{3,2,1,0:T(8,128)(2,1)S(1)} %pad_maximum_fusion), kind=kOutput, calls=%fused_computation.4 | convolution fusion | flops 2147483648 | bytes 13107200 | tf_op jit(solution)/shard_map/mkpg,gij->mkpij/dot_general | solution.py:193
  39.5 4.6 %fusion.7 = (bf16[4,4,16,16,256]{4,3,2,1,0:T(8,128)(2,1)S(1)}, bf16[4,4,16,16,256]{4,3,2,1,0:T(8,128)(2,1)S(1)}) fusion(f32[4,4,16,16,256]{4,2,3,1,0:T(8,128)S(1)} %fusion, f32[4,4,16,16,256]{4,2,3,1,0:T(8,128)S(1)} %fusion.2), kind=kLoop, calls=%fused_computation.11 | loop fusion | flops 4194304 | bytes 12582912 | tf_op jit(solution)/shard_map/convert_element_type | solution.py:196
  44.3 1.4 collective-permute-start.11
  45.7 2.5 %collective-permute-start.12 = (bf16[16,16,256]{2,1,0:T(8,128)(2,1)S(1)}, bf16[16,16,256]{2,1,0:T(8,128)(2,1)S(1)}, u32[]{:S(2)}, u32[]{:S(2)}) collective-permute-start(bf16[16,16,256]{2,1,0:T(8,128)(2,1)S(1)} %get-tuple-element.36), channel_id=1, source_target_pairs={{0,13},{1,12},{2,15},{3,14},{4,1},{5,0},{6,3},{7,2},{8,5},{9,4},{1... | collective-permute-start | bytes 393224 | tf_op jit(solution)/shard_map/ppermute | solution.py:150
  48.2 3.1 %collective-permute-start.13 = (bf16[16,16,256]{2,1,0:T(8,128)(2,1)S(1)}, bf16[16,16,256]{2,1,0:T(8,128)(2,1)S(1)}, u32[]{:S(2)}, u32[]{:S(2)}) collective-permute-start(bf16[16,16,256]{2,1,0:T(8,128)(2,1)S(1)} %get-tuple-element.35), channel_id=1, source_target_pairs={{0,2},{1,3},{2,0},{3,1},{4,6},{5,7},{6,4},{7,5},{8,10},{9,11},{10,... | collective-permute-start | bytes 393224 | tf_op jit(solution)/shard_map/ppermute | solution.py:150
  51.3 1.2 collective-permute-start.15
  52.5 2.4 %collective-permute-done.11.refs_6_ = bf16[16,16,256]{2,1,0:T(8,128)(2,1)S(1)} collective-permute-done((bf16[16,16,256]{2,1,0:T(8,128)(2,1)S(1)}, bf16[16,16,256]{2,1,0:T(8,128)(2,1)S(1)}, u32[]{:S(2)}, u32[]{:S(2)}) %collective-permute-start.11) | collective-permute-done | bytes 131104 | tf_op jit(solution)/shard_map/ppermute | solution.py:150
  54.9 6.8 %collective-permute-start.16 = (bf16[16,16,256]{2,1,0:T(8,128)(2,1)S(1)}, bf16[16,16,256]{2,1,0:T(8,128)(2,1)S(1)}, u32[]{:S(2)}, u32[]{:S(2)}) collective-permute-start(bf16[16,16,256]{2,1,0:T(8,128)(2,1)S(1)} %get-tuple-element.32), channel_id=1, source_target_pairs={{0,14},{1,15},{2,12},{3,13},{4,2},{5,3},{6,0},{7,1},{8,6},{9,7},{1... | collective-permute-start | bytes 393224 | tf_op jit(solution)/shard_map/ppermute | solution.py:150
  61.7 1.9 collective-permute-start.17
  63.6 2.9 %collective-permute-start.18 = (bf16[16,16,256]{2,1,0:T(8,128)(2,1)S(1)}, bf16[16,16,256]{2,1,0:T(8,128)(2,1)S(1)}, u32[]{:S(2)}, u32[]{:S(2)}) collective-permute-start(bf16[16,16,256]{2,1,0:T(8,128)(2,1)S(1)} %get-tuple-element.30), channel_id=1, source_target_pairs={{0,7},{1,6},{2,5},{3,4},{4,11},{5,10},{6,9},{7,8},{8,15},{9,14},{1... | collective-permute-start | bytes 393224 | tf_op jit(solution)/shard_map/ppermute | solution.py:150
  66.4 2.3 %collective-permute-start.19 = (bf16[16,16,256]{2,1,0:T(8,128)(2,1)S(1)}, bf16[16,16,256]{2,1,0:T(8,128)(2,1)S(1)}, u32[]{:S(2)}, u32[]{:S(2)}) collective-permute-start(bf16[16,16,256]{2,1,0:T(8,128)(2,1)S(1)} %get-tuple-element.29), channel_id=1, source_target_pairs={{0,11},{1,10},{2,9},{3,8},{4,15},{5,14},{6,13},{7,12},{8,3},{9,2},... | collective-permute-start | bytes 393224 | tf_op jit(solution)/shard_map/ppermute | solution.py:150
  69.3 4.4 %collective-permute-start.20 = (bf16[16,16,256]{2,1,0:T(8,128)(2,1)S(1)}, bf16[16,16,256]{2,1,0:T(8,128)(2,1)S(1)}, u32[]{:S(2)}, u32[]{:S(2)}) collective-permute-start(bf16[16,16,256]{2,1,0:T(8,128)(2,1)S(1)} %get-tuple-element.28), channel_id=1, source_target_pairs={{0,15},{1,14},{2,13},{3,12},{4,3},{5,2},{6,1},{7,0},{8,7},{9,6},{1... | collective-permute-start | bytes 393224 | tf_op jit(solution)/shard_map/ppermute | solution.py:150
  73.6 1.1 slice_bitcast_fusion.5
  74.7 4.5 %collective-permute-start.6 = (bf16[16,16,256]{2,1,0:T(8,128)(2,1)S(1)}, bf16[16,16,256]{2,1,0:T(8,128)(2,1)S(1)}, u32[]{:S(2)}, u32[]{:S(2)}) collective-permute-start(bf16[16,16,256]{2,1,0:T(8,128)(2,1)S(1)} %get-tuple-element.42), channel_id=1, source_target_pairs={{0,4},{1,5},{2,6},{3,7},{4,8},{5,9},{6,10},{7,11},{8,12},{9,13},{1... | collective-permute-start | bytes 393224 | tf_op jit(solution)/shard_map/ppermute | solution.py:150
  79.2 2.4 %collective-permute-start.8 = (bf16[16,16,256]{2,1,0:T(8,128)(2,1)S(1)}, bf16[16,16,256]{2,1,0:T(8,128)(2,1)S(1)}, u32[]{:S(2)}, u32[]{:S(2)}) collective-permute-start(bf16[16,16,256]{2,1,0:T(8,128)(2,1)S(1)} %get-tuple-element.40), channel_id=1, source_target_pairs={{0,12},{1,13},{2,14},{3,15},{4,0},{5,1},{6,2},{7,3},{8,4},{9,5},{1... | collective-permute-start | bytes 393224 | tf_op jit(solution)/shard_map/ppermute | solution.py:150
  81.6 5.2 %collective-permute-done.19.refs_14_ = bf16[16,16,256]{2,1,0:T(8,128)(2,1)S(1)} collective-permute-done((bf16[16,16,256]{2,1,0:T(8,128)(2,1)S(1)}, bf16[16,16,256]{2,1,0:T(8,128)(2,1)S(1)}, u32[]{:S(2)}, u32[]{:S(2)}) %collective-permute-start.19) | collective-permute-done | bytes 131104 | tf_op jit(solution)/shard_map/ppermute | solution.py:150
  86.9 3.3 %collective-permute-start.21 = (bf16[16,16,256]{2,1,0:T(8,128)(2,1)S(1)}, bf16[16,16,256]{2,1,0:T(8,128)(2,1)S(1)}, u32[]{:S(2)}, u32[]{:S(2)}) collective-permute-start(bf16[16,16,256]{2,1,0:T(8,128)(2,1)S(1)} %get-tuple-element.58), channel_id=1, source_target_pairs={{0,4},{1,5},{2,6},{3,7},{4,8},{5,9},{6,10},{7,11},{8,12},{9,13},{1... | collective-permute-start | bytes 393224 | tf_op jit(solution)/shard_map/ppermute | solution.py:150
  90.2 3.4 %collective-permute-start.22 = (bf16[16,16,256]{2,1,0:T(8,128)(2,1)}, bf16[16,16,256]{2,1,0:T(8,128)(2,1)S(1)}, u32[]{:S(2)}, u32[]{:S(2)}) collective-permute-start(bf16[16,16,256]{2,1,0:T(8,128)(2,1)} %get-tuple-element.57), channel_id=1, source_target_pairs={{0,8},{1,9},{2,10},{3,11},{4,12},{5,13},{6,14},{7,15},{8,0},{9,1},... | collective-permute-start | bytes 393224 | tf_op jit(solution)/shard_map/ppermute | solution.py:150
  93.7 2.1 %collective-permute-start.23 = (bf16[16,16,256]{2,1,0:T(8,128)(2,1)}, bf16[16,16,256]{2,1,0:T(8,128)(2,1)S(1)}, u32[]{:S(2)}, u32[]{:S(2)}) collective-permute-start(bf16[16,16,256]{2,1,0:T(8,128)(2,1)} %get-tuple-element.56), channel_id=1, source_target_pairs={{0,12},{1,13},{2,14},{3,15},{4,0},{5,1},{6,2},{7,3},{8,4},{9,5},{1... | collective-permute-start | bytes 393224 | tf_op jit(solution)/shard_map/ppermute | solution.py:150
  95.8 1.7 collective-permute-done.21.refs_1_
  97.5 5.5 %collective-permute-start.26 = (bf16[16,16,256]{2,1,0:T(8,128)(2,1)}, bf16[16,16,256]{2,1,0:T(8,128)(2,1)S(1)}, u32[]{:S(2)}, u32[]{:S(2)}) collective-permute-start(bf16[16,16,256]{2,1,0:T(8,128)(2,1)} %get-tuple-element.53), channel_id=1, source_target_pairs={{0,9},{1,8},{2,11},{3,10},{4,13},{5,12},{6,15},{7,14},{8,1},{9,0},... | collective-permute-start | bytes 393224 | tf_op jit(solution)/shard_map/ppermute | solution.py:150
  103.0 3.2 %copy.67 = bf16[1024,4,256]{2,0,1:T(8,128)(2,1)} copy(bf16[1024,4,256]{2,1,0:T(4,128)(2,1)} %param.9) | data formatting | bytes 4194304 | tf_op args[3]
  106.3 2.2 %all_to_all.10 = bf16[32,16384]{1,0:T(8,128)(2,1)} reshape(bf16[16,2,16384]{2,1,0:T(2,128)(2,1)} %all-to-all-done) | data formatting | bytes 2097152 | tf_op jit(solution)/shard_map/all_to_all | solution.py:27
  108.6 2.8 %collective-permute-start.28 = (bf16[16,16,256]{2,1,0:T(8,128)(2,1)S(1)}, bf16[16,16,256]{2,1,0:T(8,128)(2,1)S(1)}, u32[]{:S(2)}, u32[]{:S(2)}) collective-permute-start(bf16[16,16,256]{2,1,0:T(8,128)(2,1)S(1)} %get-tuple-element.51), channel_id=1, source_target_pairs={{0,2},{1,3},{2,0},{3,1},{4,6},{5,7},{6,4},{7,5},{8,10},{9,11},{10,... | collective-permute-start | bytes 393224 | tf_op jit(solution)/shard_map/ppermute | solution.py:150
  111.3 1.6 collective-permute-start.29
  113.6 6.4 %collective-permute-start.31 = (bf16[16,16,256]{2,1,0:T(8,128)(2,1)S(1)}, bf16[16,16,256]{2,1,0:T(8,128)(2,1)S(1)}, u32[]{:S(2)}, u32[]{:S(2)}) collective-permute-start(bf16[16,16,256]{2,1,0:T(8,128)(2,1)S(1)} %get-tuple-element.48), channel_id=1, source_target_pairs={{0,14},{1,15},{2,12},{3,13},{4,2},{5,3},{6,0},{7,1},{8,6},{9,7},{1... | collective-permute-start | bytes 393224 | tf_op jit(solution)/shard_map/ppermute | solution.py:150
  120.1 1.7 convolution_convert_fusion
  121.9 1.9 collective-permute-start.33
  123.8 6.6 %collective-permute-start.34 = (bf16[16,16,256]{2,1,0:T(8,128)(2,1)}, bf16[16,16,256]{2,1,0:T(8,128)(2,1)S(1)}, u32[]{:S(2)}, u32[]{:S(2)}) collective-permute-start(bf16[16,16,256]{2,1,0:T(8,128)(2,1)} %get-tuple-element.45), channel_id=1, source_target_pairs={{0,11},{1,10},{2,9},{3,8},{4,15},{5,14},{6,13},{7,12},{8,3},{9,2},... | collective-permute-start | bytes 393224 | tf_op jit(solution)/shard_map/ppermute | solution.py:150
  130.4 2.9 %collective-permute-start.43 = (bf16[4,1024,256]{2,1,0:T(8,128)(2,1)}, bf16[4,1024,256]{2,1,0:T(8,128)(2,1)}, u32[]{:S(2)}, u32[]{:S(2)}) collective-permute-start(bf16[4,1024,256]{2,1,0:T(8,128)(2,1)} %bitcast.203), channel_id=1, source_target_pairs={{0,1},{1,0},{2,3},{3,2},{4,5},{5,4},{6,7},{7,6},{8,9},{9,8},{10,11... | collective-permute-start | bytes 6291464 | tf_op jit(solution)/shard_map/ppermute | solution.py:150
  133.6 4.6 %shard_map.77 = (bf16[16,64,256]{2,1,0:T(8,128)(2,1)S(1)}, bf16[16,16,256]{2,1,0:T(8,128)(2,1)S(1)}, bf16[16,16,256]{2,1,0:T(8,128)(2,1)S(1)}, bf16[16,16,256]{2,1,0:T(8,128)(2,1)S(1)}, bf16[16,16,256]{2,1,0:T(8,128)(2,1)S(1)}) custom-call(s32[20]{0:T(128)S(1)} %stack.169.place_ref, bf16[16,64,256]{2,1,0:T(8,128)(2,1)S(1)} %bitcast.193, ...), custom_call_target="tpu_custom_call" | custom-call | flops 671088640 | bytes 3670016 | tf_op jit(solution)/shard_map/pallas_call | solution.py:109
  138.2 1.4 collective-permute-done.35.refs_15_
  139.7 4.5 %shard_map.78 = (bf16[16,64,256]{2,1,0:T(8,128)(2,1)S(1)}, bf16[16,16,256]{2,1,0:T(8,128)(2,1)S(1)}, bf16[16,16,256]{2,1,0:T(8,128)(2,1)S(1)}, bf16[16,16,256]{2,1,0:T(8,128)(2,1)S(1)}, bf16[16,16,256]{2,1,0:T(8,128)(2,1)S(1)}) custom-call(s32[20]{0:T(128)S(1)} %stack.169.place_ref, bf16[16,64,256]{2,1,0:T(8,128)(2,1)S(1)} %bitcast.192, ...), custom_call_target="tpu_custom_call" | custom-call | flops 671088640 | bytes 3670016 | tf_op jit(solution)/shard_map/pallas_call | solution.py:109
  145.1 1.1 collective-permute-start.36
  146.2 1.3 collective-permute-start.37
  147.5 2.2 %collective-permute-start.38 = (bf16[32,8,256]{2,1,0:T(8,128)(2,1)S(1)}, bf16[32,8,256]{2,1,0:T(8,128)(2,1)S(1)}, u32[]{:S(2)}, u32[]{:S(2)}) collective-permute-start(bf16[32,8,256]{2,1,0:T(8,128)(2,1)S(1)} %get-tuple-element.69), channel_id=1, source_target_pairs={{0,12},{1,13},{2,14},{3,15},{4,0},{5,1},{6,2},{7,3},{8,4},{9,5},{1... | collective-permute-start | bytes 393224 | tf_op jit(solution)/shard_map/ppermute | solution.py:150
  149.8 2.2 %collective-permute-start.39 = (bf16[32,8,256]{2,1,0:T(8,128)(2,1)}, bf16[32,8,256]{2,1,0:T(8,128)(2,1)S(1)}, u32[]{:S(2)}, u32[]{:S(2)}) collective-permute-start(bf16[32,8,256]{2,1,0:T(8,128)(2,1)} %get-tuple-element.65), channel_id=1, source_target_pairs={{0,2},{1,3},{2,0},{3,1},{4,6},{5,7},{6,4},{7,5},{8,10},{9,11},{10,... | collective-permute-start | bytes 393224 | tf_op jit(solution)/shard_map/ppermute | solution.py:150
  152.0 1.4 collective-permute-done.36
  153.4 2.1 %collective-permute-start.40 = (bf16[32,8,256]{2,1,0:T(8,128)(2,1)}, bf16[32,8,256]{2,1,0:T(8,128)(2,1)S(1)}, u32[]{:S(2)}, u32[]{:S(2)}) collective-permute-start(bf16[32,8,256]{2,1,0:T(8,128)(2,1)} %get-tuple-element.64), channel_id=1, source_target_pairs={{0,6},{1,7},{2,4},{3,5},{4,10},{5,11},{6,8},{7,9},{8,14},{9,15},{1... | collective-permute-start | bytes 393224 | tf_op jit(solution)/shard_map/ppermute | solution.py:150
  155.5 3.4 %collective-permute-done.37 = bf16[32,8,256]{2,1,0:T(8,128)(2,1)S(1)} collective-permute-done((bf16[32,8,256]{2,1,0:T(8,128)(2,1)S(1)}, bf16[32,8,256]{2,1,0:T(8,128)(2,1)S(1)}, u32[]{:S(2)}, u32[]{:S(2)}) %collective-permute-start.37) | collective-permute-done | bytes 131104 | tf_op jit(solution)/shard_map/ppermute | solution.py:150
  158.9 0.9 collective-permute-start.41
  159.9 4.4 %collective-permute-start.42 = (bf16[32,8,256]{2,1,0:T(8,128)(2,1)S(1)}, bf16[32,8,256]{2,1,0:T(8,128)(2,1)S(1)}, u32[]{:S(2)}, u32[]{:S(2)}) collective-permute-start(bf16[32,8,256]{2,1,0:T(8,128)(2,1)S(1)} %get-tuple-element.62), channel_id=1, source_target_pairs={{0,14},{1,15},{2,12},{3,13},{4,2},{5,3},{6,0},{7,1},{8,6},{9,7},{1... | collective-permute-start | bytes 393224 | tf_op jit(solution)/shard_map/ppermute | solution.py:150
  164.5 6.3 %collective-permute-done.41 = bf16[32,8,256]{2,1,0:T(8,128)(2,1)S(1)} collective-permute-done((bf16[32,8,256]{2,1,0:T(8,128)(2,1)}, bf16[32,8,256]{2,1,0:T(8,128)(2,1)S(1)}, u32[]{:S(2)}, u32[]{:S(2)}) %collective-permute-start.41) | collective-permute-done | bytes 131104 | tf_op jit(solution)/shard_map/ppermute | solution.py:150
  170.8 2.7 %collective-permute-done.42 = bf16[32,8,256]{2,1,0:T(8,128)(2,1)S(1)} collective-permute-done((bf16[32,8,256]{2,1,0:T(8,128)(2,1)S(1)}, bf16[32,8,256]{2,1,0:T(8,128)(2,1)S(1)}, u32[]{:S(2)}, u32[]{:S(2)}) %collective-permute-start.42) | collective-permute-done | bytes 131104 | tf_op jit(solution)/shard_map/ppermute | solution.py:150
  173.8 3.5 %fusion.25 = (bf16[8,32,1024]{2,1,0:T(8,128)(2,1)S(1)}, f32[8,32,1024]{2,1,0:T(8,128)S(1)}) fusion(bf16[4,1024,256]{2,1,0:T(8,128)(2,1)} %collective-permute-done.43, bf16[4,1024,256]{2,1,0:T(8,128)(2,1)} %bitcast.204, bf16[8,32,4,256]{3,1,2,0:T(8,128)(2,1)S(1)} %get-tuple-element.61, bf16[8,32,4,256]{3,1,2,0:T(8,128)(2,1)S(1)} %get-tuple-element.60), kind=kOutput, calls=%fused_computation.97 | convolution fusion | flops 1076625408 | bytes 6815744 | tf_op jit(solution)/shard_map/rpej,egj->rpg/dot_general | solution.py:189
  177.3 1.0 collective-permute-start.44
  178.4 1.0 collective-permute-start.45
  179.4 1.3 collective-permute-start.47
  180.7 4.0 %collective-permute-start.48 = (bf16[32,1024]{1,0:T(8,128)(2,1)S(1)}, bf16[32,1024]{1,0:T(8,128)(2,1)S(1)}, u32[]{:S(2)}, u32[]{:S(2)}) collective-permute-start(bf16[32,1024]{1,0:T(8,128)(2,1)S(1)} %get-tuple-element.75), channel_id=1, source_target_pairs={{0,14},{1,15},{2,12},{3,13},{4,2},{5,3},{6,0},{7,1},{8,6},{9,7},{1... | collective-permute-start | bytes 196616 | tf_op jit(solution)/shard_map/ppermute | solution.py:150
  184.7 2.4 %collective-permute-done.45 = bf16[32,1024]{1,0:T(8,128)(2,1)S(1)} collective-permute-done((bf16[32,1024]{1,0:T(8,128)(2,1)S(1)}, bf16[32,1024]{1,0:T(8,128)(2,1)S(1)}, u32[]{:S(2)}, u32[]{:S(2)}) %collective-permute-start.45) | collective-permute-done | bytes 65568 | tf_op jit(solution)/shard_map/ppermute | solution.py:150
  187.1 1.1 pad_maximum_fusion.1
  188.2 3.6 %collective-permute-done.49 = bf16[32,1024]{1,0:T(8,128)(2,1)S(1)} collective-permute-done((bf16[32,1024]{1,0:T(8,128)(2,1)S(1)}, bf16[32,1024]{1,0:T(8,128)(2,1)S(1)}, u32[]{:S(2)}, u32[]{:S(2)}) %collective-permute-start.49) | collective-permute-done | bytes 65568 | tf_op jit(solution)/shard_map/ppermute | solution.py:150
  191.8 2.3 %collective-permute-done.50 = bf16[32,1024]{1,0:T(8,128)(2,1)S(1)} collective-permute-done((bf16[32,1024]{1,0:T(8,128)(2,1)S(1)}, bf16[32,1024]{1,0:T(8,128)(2,1)S(1)}, u32[]{:S(2)}, u32[]{:S(2)}) %collective-permute-start.50) | collective-permute-done | bytes 65568 | tf_op jit(solution)/shard_map/ppermute | solution.py:150
  (91 shorter events, 6.0 us)
Async XLA Ops:
  0.6 8.8 %collective-permute-start = (bf16[32,1024]{1,0:T(8,128)(2,1)}, bf16[32,1024]{1,0:T(8,128)(2,1)S(1)}, u32[]{:S(2)}, u32[]{:S(2)}) collective-permute-start(bf16[32,1024]{1,0:T(8,128)(2,1)} %param.7), channel_id=1, source_target_pairs={{0,12},{1,13},{2,14},{3,15},{4,0},{5,1},{6,2},{7,3},{8,4},{9,5},{1... | collective-permute-start | bytes 196616 | tf_op jit(solution)/shard_map/ppermute | solution.py:150
  5.7 6.7 %collective-permute-start.1 = (bf16[32,1024]{1,0:T(8,128)(2,1)}, bf16[32,1024]{1,0:T(8,128)(2,1)S(1)}, u32[]{:S(2)}, u32[]{:S(2)}) collective-permute-start(bf16[32,1024]{1,0:T(8,128)(2,1)} %param.7), channel_id=1, source_target_pairs={{0,8},{1,9},{2,10},{3,11},{4,12},{5,13},{6,14},{7,15},{8,0},{9,1},... | collective-permute-start | bytes 196616 | tf_op jit(solution)/shard_map/ppermute | solution.py:150
  5.7 6.7 %collective-permute-start.2 = (bf16[32,1024]{1,0:T(8,128)(2,1)}, bf16[32,1024]{1,0:T(8,128)(2,1)S(1)}, u32[]{:S(2)}, u32[]{:S(2)}) collective-permute-start(bf16[32,1024]{1,0:T(8,128)(2,1)} %param.7), channel_id=1, source_target_pairs={{0,4},{1,5},{2,6},{3,7},{4,8},{5,9},{6,10},{7,11},{8,12},{9,13},{1... | collective-permute-start | bytes 196616 | tf_op jit(solution)/shard_map/ppermute | solution.py:150
  13.3 8.3 %collective-permute-start.3 = (bf16[4,32,1024]{2,1,0:T(8,128)(2,1)S(1)}, bf16[4,32,1024]{2,1,0:T(8,128)(2,1)S(1)}, u32[]{:S(2)}, u32[]{:S(2)}) collective-permute-start(bf16[4,32,1024]{2,1,0:T(8,128)(2,1)S(1)} %get-tuple-element.80), channel_id=1, source_target_pairs={{0,1},{1,0},{2,3},{3,2},{4,5},{5,4},{6,7},{7,6},{8,9},{9,8},{10,11... | collective-permute-start | bytes 786440 | tf_op jit(solution)/shard_map/ppermute | solution.py:150
  13.4 9.2 %collective-permute-start.4 = (bf16[4,32,1024]{2,1,0:T(8,128)(2,1)S(1)}, bf16[4,32,1024]{2,1,0:T(8,128)(2,1)S(1)}, u32[]{:S(2)}, u32[]{:S(2)}) collective-permute-start(bf16[4,32,1024]{2,1,0:T(8,128)(2,1)S(1)} %get-tuple-element.80), channel_id=1, source_target_pairs={{0,2},{1,3},{2,0},{3,1},{4,6},{5,7},{6,4},{7,5},{8,10},{9,11},{10,... | collective-permute-start | bytes 786440 | tf_op jit(solution)/shard_map/ppermute | solution.py:150
  15.0 14.5 %collective-permute-start.5 = (bf16[4,32,1024]{2,1,0:T(8,128)(2,1)S(1)}, bf16[4,32,1024]{2,1,0:T(8,128)(2,1)S(1)}, u32[]{:S(2)}, u32[]{:S(2)}) collective-permute-start(bf16[4,32,1024]{2,1,0:T(8,128)(2,1)S(1)} %get-tuple-element.80), channel_id=1, source_target_pairs={{0,3},{1,2},{2,1},{3,0},{4,7},{5,6},{6,5},{7,4},{8,11},{9,10},{10,... | collective-permute-start | bytes 786440 | tf_op jit(solution)/shard_map/ppermute | solution.py:150
  17.2 89.1 %all-to-all-start = ((bf16[16,2,16384]{2,1,0:T(2,128)(2,1)}), bf16[16,2,16384]{2,1,0:T(2,128)(2,1)}, u32[]{:S(2)}, u32[]{:S(2)}) async-start(bf16[16,2,16384]{2,1,0:T(2,128)(2,1)} %all_to_all.8), calls=%async_computation | async-start | bytes 2097152 | tf_op jit(solution)/shard_map/all_to_all | solution.py:27
  29.5 6.7 %slice-start = ((s8[8388608]{0:T(1024)(128)(4,1)}), s8[4194304]{0:T(1024)(128)(4,1)S(1)}, s32[]{:S(2)}) async-start(s8[8388608]{0:T(1024)(128)(4,1)} %bitcast.224), calls=%async_computation.1 | async-start | bytes 8388608
  29.6 6.6 %slice-start.1 = ((s8[8388608]{0:T(1024)(128)(4,1)}), s8[4194304]{0:T(1024)(128)(4,1)S(1)}, s32[]{:S(2)}) async-start(s8[8388608]{0:T(1024)(128)(4,1)} %bitcast.224), calls=%async_computation.2 | async-start | bytes 8388608
  44.2 7.0 %collective-permute-start.10 = (bf16[16,16,256]{2,1,0:T(8,128)(2,1)S(1)}, bf16[16,16,256]{2,1,0:T(8,128)(2,1)S(1)}, u32[]{:S(2)}, u32[]{:S(2)}) collective-permute-start(bf16[16,16,256]{2,1,0:T(8,128)(2,1)S(1)} %get-tuple-element.38), channel_id=1, source_target_pairs={{0,5},{1,4},{2,7},{3,6},{4,9},{5,8},{6,11},{7,10},{8,13},{9,12},{1... | collective-permute-start | bytes 393224 | tf_op jit(solution)/shard_map/ppermute | solution.py:150
  44.3 10.6 %collective-permute-start.11 = (bf16[16,16,256]{2,1,0:T(8,128)(2,1)S(1)}, bf16[16,16,256]{2,1,0:T(8,128)(2,1)S(1)}, u32[]{:S(2)}, u32[]{:S(2)}) collective-permute-start(bf16[16,16,256]{2,1,0:T(8,128)(2,1)S(1)} %get-tuple-element.37), channel_id=1, source_target_pairs={{0,9},{1,8},{2,11},{3,10},{4,13},{5,12},{6,15},{7,14},{8,1},{9,0},... | collective-permute-start | bytes 393224 | tf_op jit(solution)/shard_map/ppermute | solution.py:150
  45.7 16.0 %collective-permute-start.12 = (bf16[16,16,256]{2,1,0:T(8,128)(2,1)S(1)}, bf16[16,16,256]{2,1,0:T(8,128)(2,1)S(1)}, u32[]{:S(2)}, u32[]{:S(2)}) collective-permute-start(bf16[16,16,256]{2,1,0:T(8,128)(2,1)S(1)} %get-tuple-element.36), channel_id=1, source_target_pairs={{0,13},{1,12},{2,15},{3,14},{4,1},{5,0},{6,3},{7,2},{8,5},{9,4},{1... | collective-permute-start | bytes 393224 | tf_op jit(solution)/shard_map/ppermute | solution.py:150
  48.2 15.3 %collective-permute-start.13 = (bf16[16,16,256]{2,1,0:T(8,128)(2,1)S(1)}, bf16[16,16,256]{2,1,0:T(8,128)(2,1)S(1)}, u32[]{:S(2)}, u32[]{:S(2)}) collective-permute-start(bf16[16,16,256]{2,1,0:T(8,128)(2,1)S(1)} %get-tuple-element.35), channel_id=1, source_target_pairs={{0,2},{1,3},{2,0},{3,1},{4,6},{5,7},{6,4},{7,5},{8,10},{9,11},{10,... | collective-permute-start | bytes 393224 | tf_op jit(solution)/shard_map/ppermute | solution.py:150
  51.3 15.1 %collective-permute-start.14 = (bf16[16,16,256]{2,1,0:T(8,128)(2,1)S(1)}, bf16[16,16,256]{2,1,0:T(8,128)(2,1)S(1)}, u32[]{:S(2)}, u32[]{:S(2)}) collective-permute-start(bf16[16,16,256]{2,1,0:T(8,128)(2,1)S(1)} %get-tuple-element.34), channel_id=1, source_target_pairs={{0,6},{1,7},{2,4},{3,5},{4,10},{5,11},{6,8},{7,9},{8,14},{9,15},{1... | collective-permute-start | bytes 393224 | tf_op jit(solution)/shard_map/ppermute | solution.py:150
  51.3 18.0 %collective-permute-start.15 = (bf16[16,16,256]{2,1,0:T(8,128)(2,1)S(1)}, bf16[16,16,256]{2,1,0:T(8,128)(2,1)S(1)}, u32[]{:S(2)}, u32[]{:S(2)}) collective-permute-start(bf16[16,16,256]{2,1,0:T(8,128)(2,1)S(1)} %get-tuple-element.33), channel_id=1, source_target_pairs={{0,10},{1,11},{2,8},{3,9},{4,14},{5,15},{6,12},{7,13},{8,2},{9,3},... | collective-permute-start | bytes 393224 | tf_op jit(solution)/shard_map/ppermute | solution.py:150
  54.9 19.8 %collective-permute-start.16 = (bf16[16,16,256]{2,1,0:T(8,128)(2,1)S(1)}, bf16[16,16,256]{2,1,0:T(8,128)(2,1)S(1)}, u32[]{:S(2)}, u32[]{:S(2)}) collective-permute-start(bf16[16,16,256]{2,1,0:T(8,128)(2,1)S(1)} %get-tuple-element.32), channel_id=1, source_target_pairs={{0,14},{1,15},{2,12},{3,13},{4,2},{5,3},{6,0},{7,1},{8,6},{9,7},{1... | collective-permute-start | bytes 393224 | tf_op jit(solution)/shard_map/ppermute | solution.py:150
  61.7 17.5 %collective-permute-start.17 = (bf16[16,16,256]{2,1,0:T(8,128)(2,1)S(1)}, bf16[16,16,256]{2,1,0:T(8,128)(2,1)S(1)}, u32[]{:S(2)}, u32[]{:S(2)}) collective-permute-start(bf16[16,16,256]{2,1,0:T(8,128)(2,1)S(1)} %get-tuple-element.31), channel_id=1, source_target_pairs={{0,3},{1,2},{2,1},{3,0},{4,7},{5,6},{6,5},{7,4},{8,11},{9,10},{10,... | collective-permute-start | bytes 393224 | tf_op jit(solution)/shard_map/ppermute | solution.py:150
  63.6 15.6 %collective-permute-start.18 = (bf16[16,16,256]{2,1,0:T(8,128)(2,1)S(1)}, bf16[16,16,256]{2,1,0:T(8,128)(2,1)S(1)}, u32[]{:S(2)}, u32[]{:S(2)}) collective-permute-start(bf16[16,16,256]{2,1,0:T(8,128)(2,1)S(1)} %get-tuple-element.30), channel_id=1, source_target_pairs={{0,7},{1,6},{2,5},{3,4},{4,11},{5,10},{6,9},{7,8},{8,15},{9,14},{1... | collective-permute-start | bytes 393224 | tf_op jit(solution)/shard_map/ppermute | solution.py:150
  66.4 20.4 %collective-permute-start.19 = (bf16[16,16,256]{2,1,0:T(8,128)(2,1)S(1)}, bf16[16,16,256]{2,1,0:T(8,128)(2,1)S(1)}, u32[]{:S(2)}, u32[]{:S(2)}) collective-permute-start(bf16[16,16,256]{2,1,0:T(8,128)(2,1)S(1)} %get-tuple-element.29), channel_id=1, source_target_pairs={{0,11},{1,10},{2,9},{3,8},{4,15},{5,14},{6,13},{7,12},{8,3},{9,2},... | collective-permute-start | bytes 393224 | tf_op jit(solution)/shard_map/ppermute | solution.py:150
  69.3 17.7 %collective-permute-start.20 = (bf16[16,16,256]{2,1,0:T(8,128)(2,1)S(1)}, bf16[16,16,256]{2,1,0:T(8,128)(2,1)S(1)}, u32[]{:S(2)}, u32[]{:S(2)}) collective-permute-start(bf16[16,16,256]{2,1,0:T(8,128)(2,1)S(1)} %get-tuple-element.28), channel_id=1, source_target_pairs={{0,15},{1,14},{2,13},{3,12},{4,3},{5,2},{6,1},{7,0},{8,7},{9,6},{1... | collective-permute-start | bytes 393224 | tf_op jit(solution)/shard_map/ppermute | solution.py:150
  74.7 45.4 %copy-start = (s32[32]{0:T(128)S(1)}, s32[32]{0:T(128)}, u32[]{:S(2)}) copy-start(s32[32]{0:T(128)} %param.11) | copy-start | bytes 388
  74.7 15.5 %collective-permute-start.6 = (bf16[16,16,256]{2,1,0:T(8,128)(2,1)S(1)}, bf16[16,16,256]{2,1,0:T(8,128)(2,1)S(1)}, u32[]{:S(2)}, u32[]{:S(2)}) collective-permute-start(bf16[16,16,256]{2,1,0:T(8,128)(2,1)S(1)} %get-tuple-element.42), channel_id=1, source_target_pairs={{0,4},{1,5},{2,6},{3,7},{4,8},{5,9},{6,10},{7,11},{8,12},{9,13},{1... | collective-permute-start | bytes 393224 | tf_op jit(solution)/shard_map/ppermute | solution.py:150
  79.2 14.5 %collective-permute-start.7 = (bf16[16,16,256]{2,1,0:T(8,128)(2,1)S(1)}, bf16[16,16,256]{2,1,0:T(8,128)(2,1)S(1)}, u32[]{:S(2)}, u32[]{:S(2)}) collective-permute-start(bf16[16,16,256]{2,1,0:T(8,128)(2,1)S(1)} %get-tuple-element.41), channel_id=1, source_target_pairs={{0,8},{1,9},{2,10},{3,11},{4,12},{5,13},{6,14},{7,15},{8,0},{9,1},... | collective-permute-start | bytes 393224 | tf_op jit(solution)/shard_map/ppermute | solution.py:150
  79.2 16.5 %collective-permute-start.8 = (bf16[16,16,256]{2,1,0:T(8,128)(2,1)S(1)}, bf16[16,16,256]{2,1,0:T(8,128)(2,1)S(1)}, u32[]{:S(2)}, u32[]{:S(2)}) collective-permute-start(bf16[16,16,256]{2,1,0:T(8,128)(2,1)S(1)} %get-tuple-element.40), channel_id=1, source_target_pairs={{0,12},{1,13},{2,14},{3,15},{4,0},{5,1},{6,2},{7,3},{8,4},{9,5},{1... | collective-permute-start | bytes 393224 | tf_op jit(solution)/shard_map/ppermute | solution.py:150
  86.8 9.0 %collective-permute-start.9 = (bf16[16,16,256]{2,1,0:T(8,128)(2,1)S(1)}, bf16[16,16,256]{2,1,0:T(8,128)(2,1)S(1)}, u32[]{:S(2)}, u32[]{:S(2)}) collective-permute-start(bf16[16,16,256]{2,1,0:T(8,128)(2,1)S(1)} %get-tuple-element.39), channel_id=1, source_target_pairs={{0,1},{1,0},{2,3},{3,2},{4,5},{5,4},{6,7},{7,6},{8,9},{9,8},{10,11... | collective-permute-start | bytes 393224 | tf_op jit(solution)/shard_map/ppermute | solution.py:150
  86.9 10.6 %collective-permute-start.21 = (bf16[16,16,256]{2,1,0:T(8,128)(2,1)S(1)}, bf16[16,16,256]{2,1,0:T(8,128)(2,1)S(1)}, u32[]{:S(2)}, u32[]{:S(2)}) collective-permute-start(bf16[16,16,256]{2,1,0:T(8,128)(2,1)S(1)} %get-tuple-element.58), channel_id=1, source_target_pairs={{0,4},{1,5},{2,6},{3,7},{4,8},{5,9},{6,10},{7,11},{8,12},{9,13},{1... | collective-permute-start | bytes 393224 | tf_op jit(solution)/shard_map/ppermute | solution.py:150
  90.2 18.4 %collective-permute-start.22 = (bf16[16,16,256]{2,1,0:T(8,128)(2,1)}, bf16[16,16,256]{2,1,0:T(8,128)(2,1)S(1)}, u32[]{:S(2)}, u32[]{:S(2)}) collective-permute-start(bf16[16,16,256]{2,1,0:T(8,128)(2,1)} %get-tuple-element.57), channel_id=1, source_target_pairs={{0,8},{1,9},{2,10},{3,11},{4,12},{5,13},{6,14},{7,15},{8,0},{9,1},... | collective-permute-start | bytes 393224 | tf_op jit(solution)/shard_map/ppermute | solution.py:150
  93.7 14.9 %collective-permute-start.23 = (bf16[16,16,256]{2,1,0:T(8,128)(2,1)}, bf16[16,16,256]{2,1,0:T(8,128)(2,1)S(1)}, u32[]{:S(2)}, u32[]{:S(2)}) collective-permute-start(bf16[16,16,256]{2,1,0:T(8,128)(2,1)} %get-tuple-element.56), channel_id=1, source_target_pairs={{0,12},{1,13},{2,14},{3,15},{4,0},{5,1},{6,2},{7,3},{8,4},{9,5},{1... | collective-permute-start | bytes 393224 | tf_op jit(solution)/shard_map/ppermute | solution.py:150
  95.7 15.6 %collective-permute-start.24 = (bf16[16,16,256]{2,1,0:T(8,128)(2,1)}, bf16[16,16,256]{2,1,0:T(8,128)(2,1)S(1)}, u32[]{:S(2)}, u32[]{:S(2)}) collective-permute-start(bf16[16,16,256]{2,1,0:T(8,128)(2,1)} %get-tuple-element.55), channel_id=1, source_target_pairs={{0,1},{1,0},{2,3},{3,2},{4,5},{5,4},{6,7},{7,6},{8,9},{9,8},{10,11... | collective-permute-start | bytes 393224 | tf_op jit(solution)/shard_map/ppermute | solution.py:150
  95.7 17.2 %collective-permute-start.25 = (bf16[16,16,256]{2,1,0:T(8,128)(2,1)}, bf16[16,16,256]{2,1,0:T(8,128)(2,1)S(1)}, u32[]{:S(2)}, u32[]{:S(2)}) collective-permute-start(bf16[16,16,256]{2,1,0:T(8,128)(2,1)} %get-tuple-element.54), channel_id=1, source_target_pairs={{0,5},{1,4},{2,7},{3,6},{4,9},{5,8},{6,11},{7,10},{8,13},{9,12},{1... | collective-permute-start | bytes 393224 | tf_op jit(solution)/shard_map/ppermute | solution.py:150
  97.5 16.1 %collective-permute-start.26 = (bf16[16,16,256]{2,1,0:T(8,128)(2,1)}, bf16[16,16,256]{2,1,0:T(8,128)(2,1)S(1)}, u32[]{:S(2)}, u32[]{:S(2)}) collective-permute-start(bf16[16,16,256]{2,1,0:T(8,128)(2,1)} %get-tuple-element.53), channel_id=1, source_target_pairs={{0,9},{1,8},{2,11},{3,10},{4,13},{5,12},{6,15},{7,14},{8,1},{9,0},... | collective-permute-start | bytes 393224 | tf_op jit(solution)/shard_map/ppermute | solution.py:150
  108.6 13.2 %collective-permute-start.27 = (bf16[16,16,256]{2,1,0:T(8,128)(2,1)}, bf16[16,16,256]{2,1,0:T(8,128)(2,1)S(1)}, u32[]{:S(2)}, u32[]{:S(2)}) collective-permute-start(bf16[16,16,256]{2,1,0:T(8,128)(2,1)} %get-tuple-element.52), channel_id=1, source_target_pairs={{0,13},{1,12},{2,15},{3,14},{4,1},{5,0},{6,3},{7,2},{8,5},{9,4},{1... | collective-permute-start | bytes 393224 | tf_op jit(solution)/shard_map/ppermute | solution.py:150
  108.6 13.3 %collective-permute-start.28 = (bf16[16,16,256]{2,1,0:T(8,128)(2,1)S(1)}, bf16[16,16,256]{2,1,0:T(8,128)(2,1)S(1)}, u32[]{:S(2)}, u32[]{:S(2)}) collective-permute-start(bf16[16,16,256]{2,1,0:T(8,128)(2,1)S(1)} %get-tuple-element.51), channel_id=1, source_target_pairs={{0,2},{1,3},{2,0},{3,1},{4,6},{5,7},{6,4},{7,5},{8,10},{9,11},{10,... | collective-permute-start | bytes 393224 | tf_op jit(solution)/shard_map/ppermute | solution.py:150
  111.3 12.4 %collective-permute-start.29 = (bf16[16,16,256]{2,1,0:T(8,128)(2,1)S(1)}, bf16[16,16,256]{2,1,0:T(8,128)(2,1)S(1)}, u32[]{:S(2)}, u32[]{:S(2)}) collective-permute-start(bf16[16,16,256]{2,1,0:T(8,128)(2,1)S(1)} %get-tuple-element.50), channel_id=1, source_target_pairs={{0,6},{1,7},{2,4},{3,5},{4,10},{5,11},{6,8},{7,9},{8,14},{9,15},{1... | collective-permute-start | bytes 393224 | tf_op jit(solution)/shard_map/ppermute | solution.py:150
  113.0 17.4 %collective-permute-start.30 = (bf16[16,16,256]{2,1,0:T(8,128)(2,1)S(1)}, bf16[16,16,256]{2,1,0:T(8,128)(2,1)S(1)}, u32[]{:S(2)}, u32[]{:S(2)}) collective-permute-start(bf16[16,16,256]{2,1,0:T(8,128)(2,1)S(1)} %get-tuple-element.49), channel_id=1, source_target_pairs={{0,10},{1,11},{2,8},{3,9},{4,14},{5,15},{6,12},{7,13},{8,2},{9,3},... | collective-permute-start | bytes 393224 | tf_op jit(solution)/shard_map/ppermute | solution.py:150
  113.6 16.7 %collective-permute-start.31 = (bf16[16,16,256]{2,1,0:T(8,128)(2,1)S(1)}, bf16[16,16,256]{2,1,0:T(8,128)(2,1)S(1)}, u32[]{:S(2)}, u32[]{:S(2)}) collective-permute-start(bf16[16,16,256]{2,1,0:T(8,128)(2,1)S(1)} %get-tuple-element.48), channel_id=1, source_target_pairs={{0,14},{1,15},{2,12},{3,13},{4,2},{5,3},{6,0},{7,1},{8,6},{9,7},{1... | collective-permute-start | bytes 393224 | tf_op jit(solution)/shard_map/ppermute | solution.py:150
  121.8 16.4 %collective-permute-start.32 = (bf16[16,16,256]{2,1,0:T(8,128)(2,1)}, bf16[16,16,256]{2,1,0:T(8,128)(2,1)S(1)}, u32[]{:S(2)}, u32[]{:S(2)}) collective-permute-start(bf16[16,16,256]{2,1,0:T(8,128)(2,1)} %get-tuple-element.47), channel_id=1, source_target_pairs={{0,3},{1,2},{2,1},{3,0},{4,7},{5,6},{6,5},{7,4},{8,11},{9,10},{10,... | collective-permute-start | bytes 393224 | tf_op jit(solution)/shard_map/ppermute | solution.py:150
  121.9 16.3 %collective-permute-start.33 = (bf16[16,16,256]{2,1,0:T(8,128)(2,1)}, bf16[16,16,256]{2,1,0:T(8,128)(2,1)S(1)}, u32[]{:S(2)}, u32[]{:S(2)}) collective-permute-start(bf16[16,16,256]{2,1,0:T(8,128)(2,1)} %get-tuple-element.46), channel_id=1, source_target_pairs={{0,7},{1,6},{2,5},{3,4},{4,11},{5,10},{6,9},{7,8},{8,15},{9,14},{1... | collective-permute-start | bytes 393224 | tf_op jit(solution)/shard_map/ppermute | solution.py:150
  123.8 14.5 %collective-permute-start.34 = (bf16[16,16,256]{2,1,0:T(8,128)(2,1)}, bf16[16,16,256]{2,1,0:T(8,128)(2,1)S(1)}, u32[]{:S(2)}, u32[]{:S(2)}) collective-permute-start(bf16[16,16,256]{2,1,0:T(8,128)(2,1)} %get-tuple-element.45), channel_id=1, source_target_pairs={{0,11},{1,10},{2,9},{3,8},{4,15},{5,14},{6,13},{7,12},{8,3},{9,2},... | collective-permute-start | bytes 393224 | tf_op jit(solution)/shard_map/ppermute | solution.py:150
  130.4 9.3 %collective-permute-start.35 = (bf16[16,16,256]{2,1,0:T(8,128)(2,1)}, bf16[16,16,256]{2,1,0:T(8,128)(2,1)S(1)}, u32[]{:S(2)}, u32[]{:S(2)}) collective-permute-start(bf16[16,16,256]{2,1,0:T(8,128)(2,1)} %get-tuple-element.44), channel_id=1, source_target_pairs={{0,15},{1,14},{2,13},{3,12},{4,3},{5,2},{6,1},{7,0},{8,7},{9,6},{1... | collective-permute-start | bytes 393224 | tf_op jit(solution)/shard_map/ppermute | solution.py:150
  130.4 43.4 %collective-permute-start.43 = (bf16[4,1024,256]{2,1,0:T(8,128)(2,1)}, bf16[4,1024,256]{2,1,0:T(8,128)(2,1)}, u32[]{:S(2)}, u32[]{:S(2)}) collective-permute-start(bf16[4,1024,256]{2,1,0:T(8,128)(2,1)} %bitcast.203), channel_id=1, source_target_pairs={{0,1},{1,0},{2,3},{3,2},{4,5},{5,4},{6,7},{7,6},{8,9},{9,8},{10,11... | collective-permute-start | bytes 6291464 | tf_op jit(solution)/shard_map/ppermute | solution.py:150
  145.1 8.3 %collective-permute-start.36 = (bf16[32,8,256]{2,1,0:T(8,128)(2,1)S(1)}, bf16[32,8,256]{2,1,0:T(8,128)(2,1)S(1)}, u32[]{:S(2)}, u32[]{:S(2)}) collective-permute-start(bf16[32,8,256]{2,1,0:T(8,128)(2,1)S(1)} %get-tuple-element.67), channel_id=1, source_target_pairs={{0,4},{1,5},{2,6},{3,7},{4,8},{5,9},{6,10},{7,11},{8,12},{9,13},{1... | collective-permute-start | bytes 393224 | tf_op jit(solution)/shard_map/ppermute | solution.py:150
  146.2 12.7 %collective-permute-start.37 = (bf16[32,8,256]{2,1,0:T(8,128)(2,1)S(1)}, bf16[32,8,256]{2,1,0:T(8,128)(2,1)S(1)}, u32[]{:S(2)}, u32[]{:S(2)}) collective-permute-start(bf16[32,8,256]{2,1,0:T(8,128)(2,1)S(1)} %get-tuple-element.66), channel_id=1, source_target_pairs={{0,8},{1,9},{2,10},{3,11},{4,12},{5,13},{6,14},{7,15},{8,0},{9,1},... | collective-permute-start | bytes 393224 | tf_op jit(solution)/shard_map/ppermute | solution.py:150
  147.5 12.3 %collective-permute-start.38 = (bf16[32,8,256]{2,1,0:T(8,128)(2,1)S(1)}, bf16[32,8,256]{2,1,0:T(8,128)(2,1)S(1)}, u32[]{:S(2)}, u32[]{:S(2)}) collective-permute-start(bf16[32,8,256]{2,1,0:T(8,128)(2,1)S(1)} %get-tuple-element.69), channel_id=1, source_target_pairs={{0,12},{1,13},{2,14},{3,15},{4,0},{5,1},{6,2},{7,3},{8,4},{9,5},{1... | collective-permute-start | bytes 393224 | tf_op jit(solution)/shard_map/ppermute | solution.py:150
  149.8 14.6 %collective-permute-start.39 = (bf16[32,8,256]{2,1,0:T(8,128)(2,1)}, bf16[32,8,256]{2,1,0:T(8,128)(2,1)S(1)}, u32[]{:S(2)}, u32[]{:S(2)}) collective-permute-start(bf16[32,8,256]{2,1,0:T(8,128)(2,1)} %get-tuple-element.65), channel_id=1, source_target_pairs={{0,2},{1,3},{2,0},{3,1},{4,6},{5,7},{6,4},{7,5},{8,10},{9,11},{10,... | collective-permute-start | bytes 393224 | tf_op jit(solution)/shard_map/ppermute | solution.py:150
  153.4 11.0 %collective-permute-start.40 = (bf16[32,8,256]{2,1,0:T(8,128)(2,1)}, bf16[32,8,256]{2,1,0:T(8,128)(2,1)S(1)}, u32[]{:S(2)}, u32[]{:S(2)}) collective-permute-start(bf16[32,8,256]{2,1,0:T(8,128)(2,1)} %get-tuple-element.64), channel_id=1, source_target_pairs={{0,6},{1,7},{2,4},{3,5},{4,10},{5,11},{6,8},{7,9},{8,14},{9,15},{1... | collective-permute-start | bytes 393224 | tf_op jit(solution)/shard_map/ppermute | solution.py:150
  158.9 11.9 %collective-permute-start.41 = (bf16[32,8,256]{2,1,0:T(8,128)(2,1)}, bf16[32,8,256]{2,1,0:T(8,128)(2,1)S(1)}, u32[]{:S(2)}, u32[]{:S(2)}) collective-permute-start(bf16[32,8,256]{2,1,0:T(8,128)(2,1)} %get-tuple-element.63), channel_id=1, source_target_pairs={{0,10},{1,11},{2,8},{3,9},{4,14},{5,15},{6,12},{7,13},{8,2},{9,3},... | collective-permute-start | bytes 393224 | tf_op jit(solution)/shard_map/ppermute | solution.py:150
  159.9 13.7 %collective-permute-start.42 = (bf16[32,8,256]{2,1,0:T(8,128)(2,1)S(1)}, bf16[32,8,256]{2,1,0:T(8,128)(2,1)S(1)}, u32[]{:S(2)}, u32[]{:S(2)}) collective-permute-start(bf16[32,8,256]{2,1,0:T(8,128)(2,1)S(1)} %get-tuple-element.62), channel_id=1, source_target_pairs={{0,14},{1,15},{2,12},{3,13},{4,2},{5,3},{6,0},{7,1},{8,6},{9,7},{1... | collective-permute-start | bytes 393224 | tf_op jit(solution)/shard_map/ppermute | solution.py:150
  177.3 7.4 %collective-permute-start.44 = (bf16[32,1024]{1,0:T(8,128)(2,1)S(1)}, bf16[32,1024]{1,0:T(8,128)(2,1)S(1)}, u32[]{:S(2)}, u32[]{:S(2)}) collective-permute-start(bf16[32,1024]{1,0:T(8,128)(2,1)S(1)} %get-tuple-element.72), channel_id=1, source_target_pairs={{0,12},{1,13},{2,14},{3,15},{4,0},{5,1},{6,2},{7,3},{8,4},{9,5},{1... | collective-permute-start | bytes 196616 | tf_op jit(solution)/shard_map/ppermute | solution.py:150
  178.4 8.8 %collective-permute-start.45 = (bf16[32,1024]{1,0:T(8,128)(2,1)S(1)}, bf16[32,1024]{1,0:T(8,128)(2,1)S(1)}, u32[]{:S(2)}, u32[]{:S(2)}) collective-permute-start(bf16[32,1024]{1,0:T(8,128)(2,1)S(1)} %get-tuple-element.78), channel_id=1, source_target_pairs={{0,8},{1,9},{2,10},{3,11},{4,12},{5,13},{6,14},{7,15},{8,0},{9,1},... | collective-permute-start | bytes 196616 | tf_op jit(solution)/shard_map/ppermute | solution.py:150
  179.4 8.8 %collective-permute-start.46 = (bf16[32,1024]{1,0:T(8,128)(2,1)S(1)}, bf16[32,1024]{1,0:T(8,128)(2,1)S(1)}, u32[]{:S(2)}, u32[]{:S(2)}) collective-permute-start(bf16[32,1024]{1,0:T(8,128)(2,1)S(1)} %get-tuple-element.77), channel_id=1, source_target_pairs={{0,4},{1,5},{2,6},{3,7},{4,8},{5,9},{6,10},{7,11},{8,12},{9,13},{1... | collective-permute-start | bytes 196616 | tf_op jit(solution)/shard_map/ppermute | solution.py:150
  179.4 8.8 %collective-permute-start.47 = (bf16[32,1024]{1,0:T(8,128)(2,1)S(1)}, bf16[32,1024]{1,0:T(8,128)(2,1)S(1)}, u32[]{:S(2)}, u32[]{:S(2)}) collective-permute-start(bf16[32,1024]{1,0:T(8,128)(2,1)S(1)} %get-tuple-element.76), channel_id=1, source_target_pairs={{0,2},{1,3},{2,0},{3,1},{4,6},{5,7},{6,4},{7,5},{8,10},{9,11},{10,... | collective-permute-start | bytes 196616 | tf_op jit(solution)/shard_map/ppermute | solution.py:150
  180.7 7.5 %collective-permute-start.48 = (bf16[32,1024]{1,0:T(8,128)(2,1)S(1)}, bf16[32,1024]{1,0:T(8,128)(2,1)S(1)}, u32[]{:S(2)}, u32[]{:S(2)}) collective-permute-start(bf16[32,1024]{1,0:T(8,128)(2,1)S(1)} %get-tuple-element.75), channel_id=1, source_target_pairs={{0,14},{1,15},{2,12},{3,13},{4,2},{5,3},{6,0},{7,1},{8,6},{9,7},{1... | collective-permute-start | bytes 196616 | tf_op jit(solution)/shard_map/ppermute | solution.py:150
  184.7 7.1 %collective-permute-start.49 = (bf16[32,1024]{1,0:T(8,128)(2,1)S(1)}, bf16[32,1024]{1,0:T(8,128)(2,1)S(1)}, u32[]{:S(2)}, u32[]{:S(2)}) collective-permute-start(bf16[32,1024]{1,0:T(8,128)(2,1)S(1)} %get-tuple-element.74), channel_id=1, source_target_pairs={{0,10},{1,11},{2,8},{3,9},{4,14},{5,15},{6,12},{7,13},{8,2},{9,3},... | collective-permute-start | bytes 196616 | tf_op jit(solution)/shard_map/ppermute | solution.py:150
  187.1 7.0 %collective-permute-start.50 = (bf16[32,1024]{1,0:T(8,128)(2,1)S(1)}, bf16[32,1024]{1,0:T(8,128)(2,1)S(1)}, u32[]{:S(2)}, u32[]{:S(2)}) collective-permute-start(bf16[32,1024]{1,0:T(8,128)(2,1)S(1)} %get-tuple-element.73), channel_id=1, source_target_pairs={{0,6},{1,7},{2,4},{3,5},{4,10},{5,11},{6,8},{7,9},{8,14},{9,15},{1... | collective-permute-start | bytes 196616 | tf_op jit(solution)/shard_map/ppermute | solution.py:150

commit v4 on v3

--- a/solution.py
+++ b/solution.py
@@ -11,6 +11,7 @@
 
 field_scale = 1.5
 degrees = 5
+next_rows_at = 8
 inner = 4
 
 
@@ -103,7 +104,7 @@
     slots, electrons, orbitals = phi.shape
     rows = pieces[0].shape[1]
     elec = electrons // planes
-    block = 4 if slots % 4 == 0 else 1
+    block = 8 if slots % 8 == 0 else 1
     spec = lambda height: pl.BlockSpec((block, height, orbitals), lambda i: (i, 0, 0))
     shape = lambda height: jax.ShapeDtypeStruct((slots, height, orbitals), jnp.bfloat16)
     outs = pl.pallas_call(
@@ -197,13 +198,15 @@
 
     starts = [sum(chunks[:c]) for c in range(len(chunks))]
     made = [operator_rows(*x) for x in zip(starts, chunks)]
-    made = lax.optimization_barrier(made)
     order = [(k, m) for m in range(inner) for k in range(planes) if (k, m) != (0, 0)]
     news, parts = [], []
     for c, per in enumerate(chunks):
         landed = {(0, 0): made[c][0, 0]}
-        for k, m in order:
-            landed[k, m] = move(made[c][m, k], k, m)
+        for at, (k, m) in enumerate(order):
+            piece = made[c][m, k]
+            if c == 0 and len(chunks) > 1 and at >= next_rows_at:
+                piece = after(piece, made[1])
+            landed[k, m] = move(piece, k, m)
         pieces = [landed[k, m] for m in range(inner) for k in range(planes)]
         phi = branched[starts[c] : starts[c] + per]
         new, part = propagate(phi, pieces, place, planes)

time: 195 us -> 193 us (0.990)
  starting transfers between devices: 105 us -> 97.9 us
  waiting for transfers between devices: 44.5 us -> 49.7 us
    ppermute x51, starting transfers between devices: 100 us -> 93.6 us  [move(): return lax.ppermute(x, 'chol', route)]
    ppermute x51, waiting for transfers between devices: 44.5 us -> 49.7 us  [move(): return lax.ppermute(x, 'chol', route)]
    convert_element_type x1 -> x2, other arithmetic: 4.61 us -> 4.63 us  [operator_rows(): return (made * scale).astype(jnp.bfloat16)]
  transfers between devices with their start and end apart: 52 -> 52, of which waited for: 16 -> 15; matrix products, arithmetic and copies ran while one was open for 14% -> 14% of each run, Pallas kernels for 5% -> 4%
where the time goes in v4:
time: 193 us
  starting transfers between devices  97.9 us (51%)
  waiting for transfers between devices  49.7 us (26%)
  matrix products  15.5 us (8%)
  local copies, waits for them, and re-layouts  12.4 us (6%)
  Pallas kernels  8.41 us (4%)
  other arithmetic  7.57 us (4%)
    ppermute x51, starting transfers between devices, move(): return lax.ppermute(x, 'chol', route)  93.6 us
    ppermute x51, waiting for transfers between devices, move(): return lax.ppermute(x, 'chol', route)  49.7 us
    dot_general x2, matrix products, operator_rows(): jnp.einsum('mkpg,gij->mkpij', part, chol_vectors, preferred_element_type=...  9.8 us
    pallas_call x2, Pallas kernels, propagate(): pl.pallas_call(functools.partial(propagate_kernel, len(pieces), planes, r...  8.41 us
    unnamed x18, local copies, waits for them, and re-layouts  6.08 us
    convert_element_type x2, other arithmetic, operator_rows(): return (made * scale).astype(jnp.bfloat16)  4.63 us
    all_to_all x1, starting transfers between devices, branch_walkers(): lax.all_to_all(outgoing, 'chol', split_axis=0, concat_axis=0, tiled=True)  4.34 us
  transfers between devices with their start and end apart: 52, of which 15 were waited for; matrix products, arithmetic and copies ran while one was open for 14% of the time, Pallas kernels for 4%

profile of v4, /device:TPU:0, one launch (start us, length us, event | category | flops | bytes accessed | tf_op | source)
XLA Modules:
  0.0 192.6 jit_solution(3279970179428177674)
XLA Ops:
  0.6 5.1 %collective-permute-start = (bf16[32,1024]{1,0:T(8,128)(2,1)}, bf16[32,1024]{1,0:T(8,128)(2,1)S(1)}, u32[]{:S(2)}, u32[]{:S(2)}) collective-permute-start(bf16[32,1024]{1,0:T(8,128)(2,1)} %param.7), channel_id=1, source_target_pairs={{0,12},{1,13},{2,14},{3,15},{4,0},{5,1},{6,2},{7,3},{8,4},{9,5},{1... | collective-permute-start | bytes 196616 | tf_op jit(solution)/shard_map/ppermute | solution.py:151
  5.7 1.0 collective-permute-start.2
  6.7 1.8 copy.53
  9.4 3.0 %collective-permute-done.1 = bf16[32,1024]{1,0:T(8,128)(2,1)S(1)} collective-permute-done((bf16[32,1024]{1,0:T(8,128)(2,1)}, bf16[32,1024]{1,0:T(8,128)(2,1)S(1)}, u32[]{:S(2)}, u32[]{:S(2)}) %collective-permute-start.1) | collective-permute-done | bytes 65568 | tf_op jit(solution)/shard_map/ppermute | solution.py:151
  12.4 0.9 fusion.23
  13.4 1.6 collective-permute-start.4
  15.7 1.5 all_to_all.8
  17.2 4.3 %all-to-all-start = ((bf16[16,2,16384]{2,1,0:T(2,128)(2,1)}), bf16[16,2,16384]{2,1,0:T(2,128)(2,1)}, u32[]{:S(2)}, u32[]{:S(2)}) async-start(bf16[16,2,16384]{2,1,0:T(2,128)(2,1)} %all_to_all.8), calls=%async_computation | async-start | bytes 2097152 | tf_op jit(solution)/shard_map/all_to_all | solution.py:28
  21.6 1.0 collective-permute-done.4
  22.6 6.9 %collective-permute-done.5 = bf16[4,32,1024]{2,1,0:T(8,128)(2,1)S(1)} collective-permute-done((bf16[4,32,1024]{2,1,0:T(8,128)(2,1)S(1)}, bf16[4,32,1024]{2,1,0:T(8,128)(2,1)S(1)}, u32[]{:S(2)}, u32[]{:S(2)}) %collective-permute-start.5) | collective-permute-done | bytes 262176 | tf_op jit(solution)/shard_map/ppermute | solution.py:151
  29.6 6.6 %fusion.2 = f32[4,4,16,16,256]{4,2,3,1,0:T(8,128)S(1)} fusion(bf16[1024,16,256,1,1]{2,1,0,4,3:T(8,128)(2,1)} %bitcast.223, bf16[4,4,32,1024]{3,2,1,0:T(8,128)(2,1)S(1)} %pad_maximum_fusion), kind=kOutput, calls=%fused_computation.4 | convolution fusion | flops 2147483648 | bytes 13107200 | tf_op jit(solution)/shard_map/mkpg,gij->mkpij/dot_general | solution.py:194
  36.2 3.2 %fusion = f32[4,4,16,16,256]{4,2,3,1,0:T(8,128)S(1)} fusion(bf16[1024,16,256,1,1]{2,1,0,4,3:T(8,128)(2,1)S(1)} %bitcast.226, bf16[4,4,32,1024]{3,2,1,0:T(8,128)(2,1)S(1)} %pad_maximum_fusion), kind=kOutput, calls=%fused_computation.2 | convolution fusion | flops 2147483648 | bytes 13107200 | tf_op jit(solution)/shard_map/mkpg,gij->mkpij/dot_general | solution.py:194
  39.5 2.3 %fusion.8 = bf16[4,4,16,16,256]{4,3,2,1,0:T(8,128)(2,1)S(1)} fusion(f32[4,4,16,16,256]{4,2,3,1,0:T(8,128)S(1)} %fusion.2), kind=kLoop, calls=%fused_computation.13 | loop fusion | flops 2097152 | bytes 6291456 | tf_op jit(solution)/shard_map/convert_element_type | solution.py:197
  42.0 2.3 %fusion.7 = bf16[4,4,16,16,256]{4,3,2,1,0:T(8,128)(2,1)S(1)} fusion(f32[4,4,16,16,256]{4,2,3,1,0:T(8,128)S(1)} %fusion), kind=kLoop, calls=%fused_computation.11 | loop fusion | flops 2097152 | bytes 6291456 | tf_op jit(solution)/shard_map/convert_element_type | solution.py:197
  44.6 2.3 %collective-permute-start.15 = (bf16[16,16,256]{2,1,0:T(8,128)(2,1)S(1)}, bf16[16,16,256]{2,1,0:T(8,128)(2,1)S(1)}, u32[]{:S(2)}, u32[]{:S(2)}) collective-permute-start(bf16[16,16,256]{2,1,0:T(8,128)(2,1)S(1)} %get-tuple-element.21), channel_id=1, source_target_pairs={{0,10},{1,11},{2,8},{3,9},{4,14},{5,15},{6,12},{7,13},{8,2},{9,3},... | collective-permute-start | bytes 393224 | tf_op jit(solution)/shard_map/ppermute | solution.py:151
  47.0 3.1 %collective-permute-start.16 = (bf16[16,16,256]{2,1,0:T(8,128)(2,1)S(1)}, bf16[16,16,256]{2,1,0:T(8,128)(2,1)S(1)}, u32[]{:S(2)}, u32[]{:S(2)}) collective-permute-start(bf16[16,16,256]{2,1,0:T(8,128)(2,1)S(1)} %get-tuple-element.22), channel_id=1, source_target_pairs={{0,14},{1,15},{2,12},{3,13},{4,2},{5,3},{6,0},{7,1},{8,6},{9,7},{1... | collective-permute-start | bytes 393224 | tf_op jit(solution)/shard_map/ppermute | solution.py:151
  51.1 2.0 %collective-permute-done.14.refs_9_ = bf16[16,16,256]{2,1,0:T(8,128)(2,1)S(1)} collective-permute-done((bf16[16,16,256]{2,1,0:T(8,128)(2,1)S(1)}, bf16[16,16,256]{2,1,0:T(8,128)(2,1)S(1)}, u32[]{:S(2)}, u32[]{:S(2)}) %collective-permute-start.14) | collective-permute-done | bytes 131104 | tf_op jit(solution)/shard_map/ppermute | solution.py:151
  53.1 5.9 %collective-permute-start.19 = (bf16[16,16,256]{2,1,0:T(8,128)(2,1)S(1)}, bf16[16,16,256]{2,1,0:T(8,128)(2,1)S(1)}, u32[]{:S(2)}, u32[]{:S(2)}) collective-permute-start(bf16[16,16,256]{2,1,0:T(8,128)(2,1)S(1)} %get-tuple-element.25), channel_id=1, source_target_pairs={{0,11},{1,10},{2,9},{3,8},{4,15},{5,14},{6,13},{7,12},{8,3},{9,2},... | collective-permute-start | bytes 393224 | tf_op jit(solution)/shard_map/ppermute | solution.py:151
  58.9 5.1 %collective-permute-start.20 = (bf16[16,16,256]{2,1,0:T(8,128)(2,1)S(1)}, bf16[16,16,256]{2,1,0:T(8,128)(2,1)S(1)}, u32[]{:S(2)}, u32[]{:S(2)}) collective-permute-start(bf16[16,16,256]{2,1,0:T(8,128)(2,1)S(1)} %get-tuple-element.26), channel_id=1, source_target_pairs={{0,15},{1,14},{2,13},{3,12},{4,3},{5,2},{6,1},{7,0},{8,7},{9,6},{1... | collective-permute-start | bytes 393224 | tf_op jit(solution)/shard_map/ppermute | solution.py:151
  64.0 3.2 %collective-permute-start.10 = (bf16[16,16,256]{2,1,0:T(8,128)(2,1)S(1)}, bf16[16,16,256]{2,1,0:T(8,128)(2,1)S(1)}, u32[]{:S(2)}, u32[]{:S(2)}) collective-permute-start(bf16[16,16,256]{2,1,0:T(8,128)(2,1)S(1)} %get-tuple-element.48), channel_id=1, source_target_pairs={{0,5},{1,4},{2,7},{3,6},{4,9},{5,8},{6,11},{7,10},{8,13},{9,12},{1... | collective-permute-start | bytes 393224 | tf_op jit(solution)/shard_map/ppermute | solution.py:151
  67.2 2.0 %collective-permute-start.12 = (bf16[16,16,256]{2,1,0:T(8,128)(2,1)S(1)}, bf16[16,16,256]{2,1,0:T(8,128)(2,1)S(1)}, u32[]{:S(2)}, u32[]{:S(2)}) collective-permute-start(bf16[16,16,256]{2,1,0:T(8,128)(2,1)S(1)} %get-tuple-element.46), channel_id=1, source_target_pairs={{0,13},{1,12},{2,15},{3,14},{4,1},{5,0},{6,3},{7,2},{8,5},{9,4},{1... | collective-permute-start | bytes 393224 | tf_op jit(solution)/shard_map/ppermute | solution.py:151
  69.2 6.4 %collective-permute-done.19.refs_14_ = bf16[16,16,256]{2,1,0:T(8,128)(2,1)S(1)} collective-permute-done((bf16[16,16,256]{2,1,0:T(8,128)(2,1)S(1)}, bf16[16,16,256]{2,1,0:T(8,128)(2,1)S(1)}, u32[]{:S(2)}, u32[]{:S(2)}) %collective-permute-start.19) | collective-permute-done | bytes 131104 | tf_op jit(solution)/shard_map/ppermute | solution.py:151
  75.6 0.8 collective-permute-start.13
  76.4 1.0 slice_bitcast_fusion.5
  77.5 1.5 collective-permute-start.6
  79.0 2.6 %collective-permute-start.7 = (bf16[16,16,256]{2,1,0:T(8,128)(2,1)S(1)}, bf16[16,16,256]{2,1,0:T(8,128)(2,1)S(1)}, u32[]{:S(2)}, u32[]{:S(2)}) collective-permute-start(bf16[16,16,256]{2,1,0:T(8,128)(2,1)S(1)} %get-tuple-element.51), channel_id=1, source_target_pairs={{0,8},{1,9},{2,10},{3,11},{4,12},{5,13},{6,14},{7,15},{8,0},{9,1},... | collective-permute-start | bytes 393224 | tf_op jit(solution)/shard_map/ppermute | solution.py:151
  81.6 3.7 %collective-permute-start.8 = (bf16[16,16,256]{2,1,0:T(8,128)(2,1)S(1)}, bf16[16,16,256]{2,1,0:T(8,128)(2,1)S(1)}, u32[]{:S(2)}, u32[]{:S(2)}) collective-permute-start(bf16[16,16,256]{2,1,0:T(8,128)(2,1)S(1)} %get-tuple-element.50), channel_id=1, source_target_pairs={{0,12},{1,13},{2,14},{3,15},{4,0},{5,1},{6,2},{7,3},{8,4},{9,5},{1... | collective-permute-start | bytes 393224 | tf_op jit(solution)/shard_map/ppermute | solution.py:151
  85.3 4.3 %collective-permute-start.21 = (bf16[16,16,256]{2,1,0:T(8,128)(2,1)S(1)}, bf16[16,16,256]{2,1,0:T(8,128)(2,1)S(1)}, u32[]{:S(2)}, u32[]{:S(2)}) collective-permute-start(bf16[16,16,256]{2,1,0:T(8,128)(2,1)S(1)} %get-tuple-element.68), channel_id=1, source_target_pairs={{0,4},{1,5},{2,6},{3,7},{4,8},{5,9},{6,10},{7,11},{8,12},{9,13},{1... | collective-permute-start | bytes 393224 | tf_op jit(solution)/shard_map/ppermute | solution.py:151
  89.6 2.5 %collective-permute-start.22 = (bf16[16,16,256]{2,1,0:T(8,128)(2,1)}, bf16[16,16,256]{2,1,0:T(8,128)(2,1)S(1)}, u32[]{:S(2)}, u32[]{:S(2)}) collective-permute-start(bf16[16,16,256]{2,1,0:T(8,128)(2,1)} %get-tuple-element.67), channel_id=1, source_target_pairs={{0,8},{1,9},{2,10},{3,11},{4,12},{5,13},{6,14},{7,15},{8,0},{9,1},... | collective-permute-start | bytes 393224 | tf_op jit(solution)/shard_map/ppermute | solution.py:151
  92.1 1.1 collective-permute-done.7.refs_2_
  93.3 2.7 %collective-permute-start.23 = (bf16[16,16,256]{2,1,0:T(8,128)(2,1)}, bf16[16,16,256]{2,1,0:T(8,128)(2,1)S(1)}, u32[]{:S(2)}, u32[]{:S(2)}) collective-permute-start(bf16[16,16,256]{2,1,0:T(8,128)(2,1)} %get-tuple-element.66), channel_id=1, source_target_pairs={{0,12},{1,13},{2,14},{3,15},{4,0},{5,1},{6,2},{7,3},{8,4},{9,5},{1... | collective-permute-start | bytes 393224 | tf_op jit(solution)/shard_map/ppermute | solution.py:151
  96.0 1.4 collective-permute-start.24
  97.3 3.0 %collective-permute-start.25 = (bf16[16,16,256]{2,1,0:T(8,128)(2,1)}, bf16[16,16,256]{2,1,0:T(8,128)(2,1)S(1)}, u32[]{:S(2)}, u32[]{:S(2)}) collective-permute-start(bf16[16,16,256]{2,1,0:T(8,128)(2,1)} %get-tuple-element.64), channel_id=1, source_target_pairs={{0,5},{1,4},{2,7},{3,6},{4,9},{5,8},{6,11},{7,10},{8,13},{9,12},{1... | collective-permute-start | bytes 393224 | tf_op jit(solution)/shard_map/ppermute | solution.py:151
  100.3 3.3 %collective-permute-start.26 = (bf16[16,16,256]{2,1,0:T(8,128)(2,1)}, bf16[16,16,256]{2,1,0:T(8,128)(2,1)S(1)}, u32[]{:S(2)}, u32[]{:S(2)}) collective-permute-start(bf16[16,16,256]{2,1,0:T(8,128)(2,1)} %get-tuple-element.63), channel_id=1, source_target_pairs={{0,9},{1,8},{2,11},{3,10},{4,13},{5,12},{6,15},{7,14},{8,1},{9,0},... | collective-permute-start | bytes 393224 | tf_op jit(solution)/shard_map/ppermute | solution.py:151
  103.6 3.2 %copy.67 = bf16[1024,4,256]{2,0,1:T(8,128)(2,1)} copy(bf16[1024,4,256]{2,1,0:T(4,128)(2,1)} %param.9) | data formatting | bytes 4194304 | tf_op args[3]
  106.9 2.2 %all_to_all.10 = bf16[32,16384]{1,0:T(8,128)(2,1)} reshape(bf16[16,2,16384]{2,1,0:T(2,128)(2,1)} %all-to-all-done) | data formatting | bytes 2097152 | tf_op jit(solution)/shard_map/all_to_all | solution.py:28
  109.6 2.6 %collective-permute-start.29 = (bf16[16,16,256]{2,1,0:T(8,128)(2,1)S(1)}, bf16[16,16,256]{2,1,0:T(8,128)(2,1)S(1)}, u32[]{:S(2)}, u32[]{:S(2)}) collective-permute-start(bf16[16,16,256]{2,1,0:T(8,128)(2,1)S(1)} %get-tuple-element.60), channel_id=1, source_target_pairs={{0,6},{1,7},{2,4},{3,5},{4,10},{5,11},{6,8},{7,9},{8,14},{9,15},{1... | collective-permute-start | bytes 393224 | tf_op jit(solution)/shard_map/ppermute | solution.py:151
  112.7 1.7 collective-permute-done.26.refs_6_
  114.4 4.1 %collective-permute-start.31 = (bf16[16,16,256]{2,1,0:T(8,128)(2,1)S(1)}, bf16[16,16,256]{2,1,0:T(8,128)(2,1)S(1)}, u32[]{:S(2)}, u32[]{:S(2)}) collective-permute-start(bf16[16,16,256]{2,1,0:T(8,128)(2,1)S(1)} %get-tuple-element.58), channel_id=1, source_target_pairs={{0,14},{1,15},{2,12},{3,13},{4,2},{5,3},{6,0},{7,1},{8,6},{9,7},{1... | collective-permute-start | bytes 393224 | tf_op jit(solution)/shard_map/ppermute | solution.py:151
  118.5 1.7 convolution_convert_fusion
  120.2 1.0 collective-permute-start.32
  121.1 3.4 %collective-permute-start.33 = (bf16[16,16,256]{2,1,0:T(8,128)(2,1)}, bf16[16,16,256]{2,1,0:T(8,128)(2,1)S(1)}, u32[]{:S(2)}, u32[]{:S(2)}) collective-permute-start(bf16[16,16,256]{2,1,0:T(8,128)(2,1)} %get-tuple-element.56), channel_id=1, source_target_pairs={{0,7},{1,6},{2,5},{3,4},{4,11},{5,10},{6,9},{7,8},{8,15},{9,14},{1... | collective-permute-start | bytes 393224 | tf_op jit(solution)/shard_map/ppermute | solution.py:151
  124.6 2.6 %collective-permute-start.34 = (bf16[16,16,256]{2,1,0:T(8,128)(2,1)}, bf16[16,16,256]{2,1,0:T(8,128)(2,1)S(1)}, u32[]{:S(2)}, u32[]{:S(2)}) collective-permute-start(bf16[16,16,256]{2,1,0:T(8,128)(2,1)} %get-tuple-element.55), channel_id=1, source_target_pairs={{0,11},{1,10},{2,9},{3,8},{4,15},{5,14},{6,13},{7,12},{8,3},{9,2},... | collective-permute-start | bytes 393224 | tf_op jit(solution)/shard_map/ppermute | solution.py:151
  127.2 3.8 %collective-permute-start.35 = (bf16[16,16,256]{2,1,0:T(8,128)(2,1)}, bf16[16,16,256]{2,1,0:T(8,128)(2,1)S(1)}, u32[]{:S(2)}, u32[]{:S(2)}) collective-permute-start(bf16[16,16,256]{2,1,0:T(8,128)(2,1)} %get-tuple-element.54), channel_id=1, source_target_pairs={{0,15},{1,14},{2,13},{3,12},{4,3},{5,2},{6,1},{7,0},{8,7},{9,6},{1... | collective-permute-start | bytes 393224 | tf_op jit(solution)/shard_map/ppermute | solution.py:151
  131.3 4.2 %shard_map.77 = (bf16[16,64,256]{2,1,0:T(8,128)(2,1)S(1)}, bf16[16,16,256]{2,1,0:T(8,128)(2,1)S(1)}, bf16[16,16,256]{2,1,0:T(8,128)(2,1)S(1)}, bf16[16,16,256]{2,1,0:T(8,128)(2,1)S(1)}, bf16[16,16,256]{2,1,0:T(8,128)(2,1)S(1)}) custom-call(s32[20]{0:T(128)S(1)} %stack.169.place_ref, bf16[16,64,256]{2,1,0:T(8,128)(2,1)S(1)} %bitcast.193, ...), custom_call_target="tpu_custom_call" | custom-call | flops 671088640 | bytes 3670016 | tf_op jit(solution)/shard_map/pallas_call | solution.py:110
  135.6 2.1 %collective-permute-done.34.refs_14_ = bf16[16,16,256]{2,1,0:T(8,128)(2,1)S(1)} collective-permute-done((bf16[16,16,256]{2,1,0:T(8,128)(2,1)}, bf16[16,16,256]{2,1,0:T(8,128)(2,1)S(1)}, u32[]{:S(2)}, u32[]{:S(2)}) %collective-permute-start.34) | collective-permute-done | bytes 131104 | tf_op jit(solution)/shard_map/ppermute | solution.py:151
  137.6 4.2 %shard_map.78 = (bf16[16,64,256]{2,1,0:T(8,128)(2,1)S(1)}, bf16[16,16,256]{2,1,0:T(8,128)(2,1)S(1)}, bf16[16,16,256]{2,1,0:T(8,128)(2,1)S(1)}, bf16[16,16,256]{2,1,0:T(8,128)(2,1)S(1)}, bf16[16,16,256]{2,1,0:T(8,128)(2,1)S(1)}) custom-call(s32[20]{0:T(128)S(1)} %stack.169.place_ref, bf16[16,64,256]{2,1,0:T(8,128)(2,1)S(1)} %bitcast.192, ...), custom_call_target="tpu_custom_call" | custom-call | flops 671088640 | bytes 3670016 | tf_op jit(solution)/shard_map/pallas_call | solution.py:110
  142.0 0.8 dynamic-slice_bitcast_fusion.2
  142.7 3.1 %collective-permute-start.36 = (bf16[32,8,256]{2,1,0:T(8,128)(2,1)S(1)}, bf16[32,8,256]{2,1,0:T(8,128)(2,1)S(1)}, u32[]{:S(2)}, u32[]{:S(2)}) collective-permute-start(bf16[32,8,256]{2,1,0:T(8,128)(2,1)S(1)} %get-tuple-element.77), channel_id=1, source_target_pairs={{0,4},{1,5},{2,6},{3,7},{4,8},{5,9},{6,10},{7,11},{8,12},{9,13},{1... | collective-permute-start | bytes 393224 | tf_op jit(solution)/shard_map/ppermute | solution.py:151
  145.8 1.8 collective-permute-start.37
  148.2 0.8 collective-permute-start.39
  149.0 2.4 %collective-permute-done.36 = bf16[32,8,256]{2,1,0:T(8,128)(2,1)S(1)} collective-permute-done((bf16[32,8,256]{2,1,0:T(8,128)(2,1)S(1)}, bf16[32,8,256]{2,1,0:T(8,128)(2,1)S(1)}, u32[]{:S(2)}, u32[]{:S(2)}) %collective-permute-start.36) | collective-permute-done | bytes 131104 | tf_op jit(solution)/shard_map/ppermute | solution.py:151
  151.5 5.6 %collective-permute-done.37 = bf16[32,8,256]{2,1,0:T(8,128)(2,1)S(1)} collective-permute-done((bf16[32,8,256]{2,1,0:T(8,128)(2,1)S(1)}, bf16[32,8,256]{2,1,0:T(8,128)(2,1)S(1)}, u32[]{:S(2)}, u32[]{:S(2)}) %collective-permute-start.37) | collective-permute-done | bytes 131104 | tf_op jit(solution)/shard_map/ppermute | solution.py:151
  157.2 4.2 %collective-permute-start.42 = (bf16[32,8,256]{2,1,0:T(8,128)(2,1)S(1)}, bf16[32,8,256]{2,1,0:T(8,128)(2,1)S(1)}, u32[]{:S(2)}, u32[]{:S(2)}) collective-permute-start(bf16[32,8,256]{2,1,0:T(8,128)(2,1)S(1)} %get-tuple-element.72), channel_id=1, source_target_pairs={{0,14},{1,15},{2,12},{3,13},{4,2},{5,3},{6,0},{7,1},{8,6},{9,7},{1... | collective-permute-start | bytes 393224 | tf_op jit(solution)/shard_map/ppermute | solution.py:151
  161.7 6.6 %collective-permute-done.41 = bf16[32,8,256]{2,1,0:T(8,128)(2,1)S(1)} collective-permute-done((bf16[32,8,256]{2,1,0:T(8,128)(2,1)}, bf16[32,8,256]{2,1,0:T(8,128)(2,1)S(1)}, u32[]{:S(2)}, u32[]{:S(2)}) %collective-permute-start.41) | collective-permute-done | bytes 131104 | tf_op jit(solution)/shard_map/ppermute | solution.py:151
  168.3 2.7 %collective-permute-done.42 = bf16[32,8,256]{2,1,0:T(8,128)(2,1)S(1)} collective-permute-done((bf16[32,8,256]{2,1,0:T(8,128)(2,1)S(1)}, bf16[32,8,256]{2,1,0:T(8,128)(2,1)S(1)}, u32[]{:S(2)}, u32[]{:S(2)}) %collective-permute-start.42) | collective-permute-done | bytes 131104 | tf_op jit(solution)/shard_map/ppermute | solution.py:151
  171.3 3.5 %fusion.25 = (bf16[8,32,1024]{2,1,0:T(8,128)(2,1)S(1)}, f32[8,32,1024]{2,1,0:T(8,128)S(1)}) fusion(bf16[4,1024,256]{2,1,0:T(8,128)(2,1)} %collective-permute-done.43, bf16[4,1024,256]{2,1,0:T(8,128)(2,1)} %bitcast.204, bf16[8,32,4,256]{3,1,2,0:T(8,128)(2,1)S(1)} %get-tuple-element.71, bf16[8,32,4,256]{3,1,2,0:T(8,128)(2,1)S(1)} %get-tuple-element.70), kind=kOutput, calls=%fused_computation.97 | convolution fusion | flops 1076625408 | bytes 6815744 | tf_op jit(solution)/shard_map/rpej,egj->rpg/dot_general | solution.py:190
  175.0 2.1 %collective-permute-start.45 = (bf16[32,1024]{1,0:T(8,128)(2,1)S(1)}, bf16[32,1024]{1,0:T(8,128)(2,1)S(1)}, u32[]{:S(2)}, u32[]{:S(2)}) collective-permute-start(bf16[32,1024]{1,0:T(8,128)(2,1)S(1)} %get-tuple-element.88), channel_id=1, source_target_pairs={{0,8},{1,9},{2,10},{3,11},{4,12},{5,13},{6,14},{7,15},{8,0},{9,1},... | collective-permute-start | bytes 196616 | tf_op jit(solution)/shard_map/ppermute | solution.py:151
  177.1 1.1 collective-permute-start.47
  178.2 4.2 %collective-permute-start.48 = (bf16[32,1024]{1,0:T(8,128)(2,1)S(1)}, bf16[32,1024]{1,0:T(8,128)(2,1)S(1)}, u32[]{:S(2)}, u32[]{:S(2)}) collective-permute-start(bf16[32,1024]{1,0:T(8,128)(2,1)S(1)} %get-tuple-element.85), channel_id=1, source_target_pairs={{0,14},{1,15},{2,12},{3,13},{4,2},{5,3},{6,0},{7,1},{8,6},{9,7},{1... | collective-permute-start | bytes 196616 | tf_op jit(solution)/shard_map/ppermute | solution.py:151
  182.6 2.3 %collective-permute-done.45 = bf16[32,1024]{1,0:T(8,128)(2,1)S(1)} collective-permute-done((bf16[32,1024]{1,0:T(8,128)(2,1)S(1)}, bf16[32,1024]{1,0:T(8,128)(2,1)S(1)}, u32[]{:S(2)}, u32[]{:S(2)}) %collective-permute-start.45) | collective-permute-done | bytes 65568 | tf_op jit(solution)/shard_map/ppermute | solution.py:151
  184.9 1.1 pad_maximum_fusion.1
  186.0 3.1 %collective-permute-done.49 = bf16[32,1024]{1,0:T(8,128)(2,1)S(1)} collective-permute-done((bf16[32,1024]{1,0:T(8,128)(2,1)S(1)}, bf16[32,1024]{1,0:T(8,128)(2,1)S(1)}, u32[]{:S(2)}, u32[]{:S(2)}) %collective-permute-start.49) | collective-permute-done | bytes 65568 | tf_op jit(solution)/shard_map/ppermute | solution.py:151
  189.1 2.8 %collective-permute-done.50 = bf16[32,1024]{1,0:T(8,128)(2,1)S(1)} collective-permute-done((bf16[32,1024]{1,0:T(8,128)(2,1)S(1)}, bf16[32,1024]{1,0:T(8,128)(2,1)S(1)}, u32[]{:S(2)}, u32[]{:S(2)}) %collective-permute-start.50) | collective-permute-done | bytes 65568 | tf_op jit(solution)/shard_map/ppermute | solution.py:151
  (92 shorter events, 7.2 us)
Async XLA Ops:
  0.6 8.8 %collective-permute-start = (bf16[32,1024]{1,0:T(8,128)(2,1)}, bf16[32,1024]{1,0:T(8,128)(2,1)S(1)}, u32[]{:S(2)}, u32[]{:S(2)}) collective-permute-start(bf16[32,1024]{1,0:T(8,128)(2,1)} %param.7), channel_id=1, source_target_pairs={{0,12},{1,13},{2,14},{3,15},{4,0},{5,1},{6,2},{7,3},{8,4},{9,5},{1... | collective-permute-start | bytes 196616 | tf_op jit(solution)/shard_map/ppermute | solution.py:151
  5.7 6.7 %collective-permute-start.1 = (bf16[32,1024]{1,0:T(8,128)(2,1)}, bf16[32,1024]{1,0:T(8,128)(2,1)S(1)}, u32[]{:S(2)}, u32[]{:S(2)}) collective-permute-start(bf16[32,1024]{1,0:T(8,128)(2,1)} %param.7), channel_id=1, source_target_pairs={{0,8},{1,9},{2,10},{3,11},{4,12},{5,13},{6,14},{7,15},{8,0},{9,1},... | collective-permute-start | bytes 196616 | tf_op jit(solution)/shard_map/ppermute | solution.py:151
  5.7 6.7 %collective-permute-start.2 = (bf16[32,1024]{1,0:T(8,128)(2,1)}, bf16[32,1024]{1,0:T(8,128)(2,1)S(1)}, u32[]{:S(2)}, u32[]{:S(2)}) collective-permute-start(bf16[32,1024]{1,0:T(8,128)(2,1)} %param.7), channel_id=1, source_target_pairs={{0,4},{1,5},{2,6},{3,7},{4,8},{5,9},{6,10},{7,11},{8,12},{9,13},{1... | collective-permute-start | bytes 196616 | tf_op jit(solution)/shard_map/ppermute | solution.py:151
  13.3 8.3 %collective-permute-start.3 = (bf16[4,32,1024]{2,1,0:T(8,128)(2,1)S(1)}, bf16[4,32,1024]{2,1,0:T(8,128)(2,1)S(1)}, u32[]{:S(2)}, u32[]{:S(2)}) collective-permute-start(bf16[4,32,1024]{2,1,0:T(8,128)(2,1)S(1)} %get-tuple-element.90), channel_id=1, source_target_pairs={{0,1},{1,0},{2,3},{3,2},{4,5},{5,4},{6,7},{7,6},{8,9},{9,8},{10,11... | collective-permute-start | bytes 786440 | tf_op jit(solution)/shard_map/ppermute | solution.py:151
  13.4 9.2 %collective-permute-start.4 = (bf16[4,32,1024]{2,1,0:T(8,128)(2,1)S(1)}, bf16[4,32,1024]{2,1,0:T(8,128)(2,1)S(1)}, u32[]{:S(2)}, u32[]{:S(2)}) collective-permute-start(bf16[4,32,1024]{2,1,0:T(8,128)(2,1)S(1)} %get-tuple-element.90), channel_id=1, source_target_pairs={{0,2},{1,3},{2,0},{3,1},{4,6},{5,7},{6,4},{7,5},{8,10},{9,11},{10,... | collective-permute-start | bytes 786440 | tf_op jit(solution)/shard_map/ppermute | solution.py:151
  15.0 14.5 %collective-permute-start.5 = (bf16[4,32,1024]{2,1,0:T(8,128)(2,1)S(1)}, bf16[4,32,1024]{2,1,0:T(8,128)(2,1)S(1)}, u32[]{:S(2)}, u32[]{:S(2)}) collective-permute-start(bf16[4,32,1024]{2,1,0:T(8,128)(2,1)S(1)} %get-tuple-element.90), channel_id=1, source_target_pairs={{0,3},{1,2},{2,1},{3,0},{4,7},{5,6},{6,5},{7,4},{8,11},{9,10},{10,... | collective-permute-start | bytes 786440 | tf_op jit(solution)/shard_map/ppermute | solution.py:151
  17.2 89.7 %all-to-all-start = ((bf16[16,2,16384]{2,1,0:T(2,128)(2,1)}), bf16[16,2,16384]{2,1,0:T(2,128)(2,1)}, u32[]{:S(2)}, u32[]{:S(2)}) async-start(bf16[16,2,16384]{2,1,0:T(2,128)(2,1)} %all_to_all.8), calls=%async_computation | async-start | bytes 2097152 | tf_op jit(solution)/shard_map/all_to_all | solution.py:28
  29.5 6.7 %slice-start = ((s8[8388608]{0:T(1024)(128)(4,1)}), s8[4194304]{0:T(1024)(128)(4,1)S(1)}, s32[]{:S(2)}) async-start(s8[8388608]{0:T(1024)(128)(4,1)} %bitcast.224), calls=%async_computation.1 | async-start | bytes 8388608
  29.6 6.6 %slice-start.1 = ((s8[8388608]{0:T(1024)(128)(4,1)}), s8[4194304]{0:T(1024)(128)(4,1)S(1)}, s32[]{:S(2)}) async-start(s8[8388608]{0:T(1024)(128)(4,1)} %bitcast.224), calls=%async_computation.2 | async-start | bytes 8388608
  44.3 8.8 %collective-permute-start.14 = (bf16[16,16,256]{2,1,0:T(8,128)(2,1)S(1)}, bf16[16,16,256]{2,1,0:T(8,128)(2,1)S(1)}, u32[]{:S(2)}, u32[]{:S(2)}) collective-permute-start(bf16[16,16,256]{2,1,0:T(8,128)(2,1)S(1)} %get-tuple-element.20), channel_id=1, source_target_pairs={{0,6},{1,7},{2,4},{3,5},{4,10},{5,11},{6,8},{7,9},{8,14},{9,15},{1... | collective-permute-start | bytes 393224 | tf_op jit(solution)/shard_map/ppermute | solution.py:151
  44.6 14.3 %collective-permute-start.15 = (bf16[16,16,256]{2,1,0:T(8,128)(2,1)S(1)}, bf16[16,16,256]{2,1,0:T(8,128)(2,1)S(1)}, u32[]{:S(2)}, u32[]{:S(2)}) collective-permute-start(bf16[16,16,256]{2,1,0:T(8,128)(2,1)S(1)} %get-tuple-element.21), channel_id=1, source_target_pairs={{0,10},{1,11},{2,8},{3,9},{4,14},{5,15},{6,12},{7,13},{8,2},{9,3},... | collective-permute-start | bytes 393224 | tf_op jit(solution)/shard_map/ppermute | solution.py:151
  47.0 17.0 %collective-permute-start.16 = (bf16[16,16,256]{2,1,0:T(8,128)(2,1)S(1)}, bf16[16,16,256]{2,1,0:T(8,128)(2,1)S(1)}, u32[]{:S(2)}, u32[]{:S(2)}) collective-permute-start(bf16[16,16,256]{2,1,0:T(8,128)(2,1)S(1)} %get-tuple-element.22), channel_id=1, source_target_pairs={{0,14},{1,15},{2,12},{3,13},{4,2},{5,3},{6,0},{7,1},{8,6},{9,7},{1... | collective-permute-start | bytes 393224 | tf_op jit(solution)/shard_map/ppermute | solution.py:151
  50.0 17.1 %collective-permute-start.17 = (bf16[16,16,256]{2,1,0:T(8,128)(2,1)S(1)}, bf16[16,16,256]{2,1,0:T(8,128)(2,1)S(1)}, u32[]{:S(2)}, u32[]{:S(2)}) collective-permute-start(bf16[16,16,256]{2,1,0:T(8,128)(2,1)S(1)} %get-tuple-element.23), channel_id=1, source_target_pairs={{0,3},{1,2},{2,1},{3,0},{4,7},{5,6},{6,5},{7,4},{8,11},{9,10},{10,... | collective-permute-start | bytes 393224 | tf_op jit(solution)/shard_map/ppermute | solution.py:151
  50.3 16.8 %collective-permute-start.18 = (bf16[16,16,256]{2,1,0:T(8,128)(2,1)S(1)}, bf16[16,16,256]{2,1,0:T(8,128)(2,1)S(1)}, u32[]{:S(2)}, u32[]{:S(2)}) collective-permute-start(bf16[16,16,256]{2,1,0:T(8,128)(2,1)S(1)} %get-tuple-element.24), channel_id=1, source_target_pairs={{0,7},{1,6},{2,5},{3,4},{4,11},{5,10},{6,9},{7,8},{8,15},{9,14},{1... | collective-permute-start | bytes 393224 | tf_op jit(solution)/shard_map/ppermute | solution.py:151
  53.1 22.5 %collective-permute-start.19 = (bf16[16,16,256]{2,1,0:T(8,128)(2,1)S(1)}, bf16[16,16,256]{2,1,0:T(8,128)(2,1)S(1)}, u32[]{:S(2)}, u32[]{:S(2)}) collective-permute-start(bf16[16,16,256]{2,1,0:T(8,128)(2,1)S(1)} %get-tuple-element.25), channel_id=1, source_target_pairs={{0,11},{1,10},{2,9},{3,8},{4,15},{5,14},{6,13},{7,12},{8,3},{9,2},... | collective-permute-start | bytes 393224 | tf_op jit(solution)/shard_map/ppermute | solution.py:151
  58.9 18.5 %collective-permute-start.20 = (bf16[16,16,256]{2,1,0:T(8,128)(2,1)S(1)}, bf16[16,16,256]{2,1,0:T(8,128)(2,1)S(1)}, u32[]{:S(2)}, u32[]{:S(2)}) collective-permute-start(bf16[16,16,256]{2,1,0:T(8,128)(2,1)S(1)} %get-tuple-element.26), channel_id=1, source_target_pairs={{0,15},{1,14},{2,13},{3,12},{4,3},{5,2},{6,1},{7,0},{8,7},{9,6},{1... | collective-permute-start | bytes 393224 | tf_op jit(solution)/shard_map/ppermute | solution.py:151
  64.0 15.0 %collective-permute-start.10 = (bf16[16,16,256]{2,1,0:T(8,128)(2,1)S(1)}, bf16[16,16,256]{2,1,0:T(8,128)(2,1)S(1)}, u32[]{:S(2)}, u32[]{:S(2)}) collective-permute-start(bf16[16,16,256]{2,1,0:T(8,128)(2,1)S(1)} %get-tuple-element.48), channel_id=1, source_target_pairs={{0,5},{1,4},{2,7},{3,6},{4,9},{5,8},{6,11},{7,10},{8,13},{9,12},{1... | collective-permute-start | bytes 393224 | tf_op jit(solution)/shard_map/ppermute | solution.py:151
  67.2 14.4 %collective-permute-start.11 = (bf16[16,16,256]{2,1,0:T(8,128)(2,1)S(1)}, bf16[16,16,256]{2,1,0:T(8,128)(2,1)S(1)}, u32[]{:S(2)}, u32[]{:S(2)}) collective-permute-start(bf16[16,16,256]{2,1,0:T(8,128)(2,1)S(1)} %get-tuple-element.47), channel_id=1, source_target_pairs={{0,9},{1,8},{2,11},{3,10},{4,13},{5,12},{6,15},{7,14},{8,1},{9,0},... | collective-permute-start | bytes 393224 | tf_op jit(solution)/shard_map/ppermute | solution.py:151
  67.2 18.2 %collective-permute-start.12 = (bf16[16,16,256]{2,1,0:T(8,128)(2,1)S(1)}, bf16[16,16,256]{2,1,0:T(8,128)(2,1)S(1)}, u32[]{:S(2)}, u32[]{:S(2)}) collective-permute-start(bf16[16,16,256]{2,1,0:T(8,128)(2,1)S(1)} %get-tuple-element.46), channel_id=1, source_target_pairs={{0,13},{1,12},{2,15},{3,14},{4,1},{5,0},{6,3},{7,2},{8,5},{9,4},{1... | collective-permute-start | bytes 393224 | tf_op jit(solution)/shard_map/ppermute | solution.py:151
  75.6 9.8 %collective-permute-start.13 = (bf16[16,16,256]{2,1,0:T(8,128)(2,1)S(1)}, bf16[16,16,256]{2,1,0:T(8,128)(2,1)S(1)}, u32[]{:S(2)}, u32[]{:S(2)}) collective-permute-start(bf16[16,16,256]{2,1,0:T(8,128)(2,1)S(1)} %get-tuple-element.45), channel_id=1, source_target_pairs={{0,2},{1,3},{2,0},{3,1},{4,6},{5,7},{6,4},{7,5},{8,10},{9,11},{10,... | collective-permute-start | bytes 393224 | tf_op jit(solution)/shard_map/ppermute | solution.py:151
  77.5 41.0 %copy-start = (s32[32]{0:T(128)S(1)}, s32[32]{0:T(128)}, u32[]{:S(2)}) copy-start(s32[32]{0:T(128)} %param.11) | copy-start | bytes 388
  77.5 12.2 %collective-permute-start.6 = (bf16[16,16,256]{2,1,0:T(8,128)(2,1)S(1)}, bf16[16,16,256]{2,1,0:T(8,128)(2,1)S(1)}, u32[]{:S(2)}, u32[]{:S(2)}) collective-permute-start(bf16[16,16,256]{2,1,0:T(8,128)(2,1)S(1)} %get-tuple-element.52), channel_id=1, source_target_pairs={{0,4},{1,5},{2,6},{3,7},{4,8},{5,9},{6,10},{7,11},{8,12},{9,13},{1... | collective-permute-start | bytes 393224 | tf_op jit(solution)/shard_map/ppermute | solution.py:151
  79.0 14.3 %collective-permute-start.7 = (bf16[16,16,256]{2,1,0:T(8,128)(2,1)S(1)}, bf16[16,16,256]{2,1,0:T(8,128)(2,1)S(1)}, u32[]{:S(2)}, u32[]{:S(2)}) collective-permute-start(bf16[16,16,256]{2,1,0:T(8,128)(2,1)S(1)} %get-tuple-element.51), channel_id=1, source_target_pairs={{0,8},{1,9},{2,10},{3,11},{4,12},{5,13},{6,14},{7,15},{8,0},{9,1},... | collective-permute-start | bytes 393224 | tf_op jit(solution)/shard_map/ppermute | solution.py:151
  81.6 14.4 %collective-permute-start.8 = (bf16[16,16,256]{2,1,0:T(8,128)(2,1)S(1)}, bf16[16,16,256]{2,1,0:T(8,128)(2,1)S(1)}, u32[]{:S(2)}, u32[]{:S(2)}) collective-permute-start(bf16[16,16,256]{2,1,0:T(8,128)(2,1)S(1)} %get-tuple-element.50), channel_id=1, source_target_pairs={{0,12},{1,13},{2,14},{3,15},{4,0},{5,1},{6,2},{7,3},{8,4},{9,5},{1... | collective-permute-start | bytes 393224 | tf_op jit(solution)/shard_map/ppermute | solution.py:151
  85.3 12.0 %collective-permute-start.9 = (bf16[16,16,256]{2,1,0:T(8,128)(2,1)S(1)}, bf16[16,16,256]{2,1,0:T(8,128)(2,1)S(1)}, u32[]{:S(2)}, u32[]{:S(2)}) collective-permute-start(bf16[16,16,256]{2,1,0:T(8,128)(2,1)S(1)} %get-tuple-element.49), channel_id=1, source_target_pairs={{0,1},{1,0},{2,3},{3,2},{4,5},{5,4},{6,7},{7,6},{8,9},{9,8},{10,11... | collective-permute-start | bytes 393224 | tf_op jit(solution)/shard_map/ppermute | solution.py:151
  85.3 15.0 %collective-permute-start.21 = (bf16[16,16,256]{2,1,0:T(8,128)(2,1)S(1)}, bf16[16,16,256]{2,1,0:T(8,128)(2,1)S(1)}, u32[]{:S(2)}, u32[]{:S(2)}) collective-permute-start(bf16[16,16,256]{2,1,0:T(8,128)(2,1)S(1)} %get-tuple-element.68), channel_id=1, source_target_pairs={{0,4},{1,5},{2,6},{3,7},{4,8},{5,9},{6,10},{7,11},{8,12},{9,13},{1... | collective-permute-start | bytes 393224 | tf_op jit(solution)/shard_map/ppermute | solution.py:151
  89.6 19.5 %collective-permute-start.22 = (bf16[16,16,256]{2,1,0:T(8,128)(2,1)}, bf16[16,16,256]{2,1,0:T(8,128)(2,1)S(1)}, u32[]{:S(2)}, u32[]{:S(2)}) collective-permute-start(bf16[16,16,256]{2,1,0:T(8,128)(2,1)} %get-tuple-element.67), channel_id=1, source_target_pairs={{0,8},{1,9},{2,10},{3,11},{4,12},{5,13},{6,14},{7,15},{8,0},{9,1},... | collective-permute-start | bytes 393224 | tf_op jit(solution)/shard_map/ppermute | solution.py:151
  93.3 15.9 %collective-permute-start.23 = (bf16[16,16,256]{2,1,0:T(8,128)(2,1)}, bf16[16,16,256]{2,1,0:T(8,128)(2,1)S(1)}, u32[]{:S(2)}, u32[]{:S(2)}) collective-permute-start(bf16[16,16,256]{2,1,0:T(8,128)(2,1)} %get-tuple-element.66), channel_id=1, source_target_pairs={{0,12},{1,13},{2,14},{3,15},{4,0},{5,1},{6,2},{7,3},{8,4},{9,5},{1... | collective-permute-start | bytes 393224 | tf_op jit(solution)/shard_map/ppermute | solution.py:151
  96.0 13.6 %collective-permute-start.24 = (bf16[16,16,256]{2,1,0:T(8,128)(2,1)}, bf16[16,16,256]{2,1,0:T(8,128)(2,1)S(1)}, u32[]{:S(2)}, u32[]{:S(2)}) collective-permute-start(bf16[16,16,256]{2,1,0:T(8,128)(2,1)} %get-tuple-element.65), channel_id=1, source_target_pairs={{0,1},{1,0},{2,3},{3,2},{4,5},{5,4},{6,7},{7,6},{8,9},{9,8},{10,11... | collective-permute-start | bytes 393224 | tf_op jit(solution)/shard_map/ppermute | solution.py:151
  97.3 14.9 %collective-permute-start.25 = (bf16[16,16,256]{2,1,0:T(8,128)(2,1)}, bf16[16,16,256]{2,1,0:T(8,128)(2,1)S(1)}, u32[]{:S(2)}, u32[]{:S(2)}) collective-permute-start(bf16[16,16,256]{2,1,0:T(8,128)(2,1)} %get-tuple-element.64), channel_id=1, source_target_pairs={{0,5},{1,4},{2,7},{3,6},{4,9},{5,8},{6,11},{7,10},{8,13},{9,12},{1... | collective-permute-start | bytes 393224 | tf_op jit(solution)/shard_map/ppermute | solution.py:151
  100.3 14.1 %collective-permute-start.26 = (bf16[16,16,256]{2,1,0:T(8,128)(2,1)}, bf16[16,16,256]{2,1,0:T(8,128)(2,1)S(1)}, u32[]{:S(2)}, u32[]{:S(2)}) collective-permute-start(bf16[16,16,256]{2,1,0:T(8,128)(2,1)} %get-tuple-element.63), channel_id=1, source_target_pairs={{0,9},{1,8},{2,11},{3,10},{4,13},{5,12},{6,15},{7,14},{8,1},{9,0},... | collective-permute-start | bytes 393224 | tf_op jit(solution)/shard_map/ppermute | solution.py:151
  109.2 11.0 %collective-permute-start.27 = (bf16[16,16,256]{2,1,0:T(8,128)(2,1)}, bf16[16,16,256]{2,1,0:T(8,128)(2,1)S(1)}, u32[]{:S(2)}, u32[]{:S(2)}) collective-permute-start(bf16[16,16,256]{2,1,0:T(8,128)(2,1)} %get-tuple-element.62), channel_id=1, source_target_pairs={{0,13},{1,12},{2,15},{3,14},{4,1},{5,0},{6,3},{7,2},{8,5},{9,4},{1... | collective-permute-start | bytes 393224 | tf_op jit(solution)/shard_map/ppermute | solution.py:151
  109.2 12.0 %collective-permute-start.28 = (bf16[16,16,256]{2,1,0:T(8,128)(2,1)S(1)}, bf16[16,16,256]{2,1,0:T(8,128)(2,1)S(1)}, u32[]{:S(2)}, u32[]{:S(2)}) collective-permute-start(bf16[16,16,256]{2,1,0:T(8,128)(2,1)S(1)} %get-tuple-element.61), channel_id=1, source_target_pairs={{0,2},{1,3},{2,0},{3,1},{4,6},{5,7},{6,4},{7,5},{8,10},{9,11},{10,... | collective-permute-start | bytes 393224 | tf_op jit(solution)/shard_map/ppermute | solution.py:151
  109.6 15.0 %collective-permute-start.29 = (bf16[16,16,256]{2,1,0:T(8,128)(2,1)S(1)}, bf16[16,16,256]{2,1,0:T(8,128)(2,1)S(1)}, u32[]{:S(2)}, u32[]{:S(2)}) collective-permute-start(bf16[16,16,256]{2,1,0:T(8,128)(2,1)S(1)} %get-tuple-element.60), channel_id=1, source_target_pairs={{0,6},{1,7},{2,4},{3,5},{4,10},{5,11},{6,8},{7,9},{8,14},{9,15},{1... | collective-permute-start | bytes 393224 | tf_op jit(solution)/shard_map/ppermute | solution.py:151
  112.2 14.9 %collective-permute-start.30 = (bf16[16,16,256]{2,1,0:T(8,128)(2,1)S(1)}, bf16[16,16,256]{2,1,0:T(8,128)(2,1)S(1)}, u32[]{:S(2)}, u32[]{:S(2)}) collective-permute-start(bf16[16,16,256]{2,1,0:T(8,128)(2,1)S(1)} %get-tuple-element.59), channel_id=1, source_target_pairs={{0,10},{1,11},{2,8},{3,9},{4,14},{5,15},{6,12},{7,13},{8,2},{9,3},... | collective-permute-start | bytes 393224 | tf_op jit(solution)/shard_map/ppermute | solution.py:151
  114.4 16.6 %collective-permute-start.31 = (bf16[16,16,256]{2,1,0:T(8,128)(2,1)S(1)}, bf16[16,16,256]{2,1,0:T(8,128)(2,1)S(1)}, u32[]{:S(2)}, u32[]{:S(2)}) collective-permute-start(bf16[16,16,256]{2,1,0:T(8,128)(2,1)S(1)} %get-tuple-element.58), channel_id=1, source_target_pairs={{0,14},{1,15},{2,12},{3,13},{4,2},{5,3},{6,0},{7,1},{8,6},{9,7},{1... | collective-permute-start | bytes 393224 | tf_op jit(solution)/shard_map/ppermute | solution.py:151
  120.2 15.4 %collective-permute-start.32 = (bf16[16,16,256]{2,1,0:T(8,128)(2,1)}, bf16[16,16,256]{2,1,0:T(8,128)(2,1)S(1)}, u32[]{:S(2)}, u32[]{:S(2)}) collective-permute-start(bf16[16,16,256]{2,1,0:T(8,128)(2,1)} %get-tuple-element.57), channel_id=1, source_target_pairs={{0,3},{1,2},{2,1},{3,0},{4,7},{5,6},{6,5},{7,4},{8,11},{9,10},{10,... | collective-permute-start | bytes 393224 | tf_op jit(solution)/shard_map/ppermute | solution.py:151
  121.1 14.4 %collective-permute-start.33 = (bf16[16,16,256]{2,1,0:T(8,128)(2,1)}, bf16[16,16,256]{2,1,0:T(8,128)(2,1)S(1)}, u32[]{:S(2)}, u32[]{:S(2)}) collective-permute-start(bf16[16,16,256]{2,1,0:T(8,128)(2,1)} %get-tuple-element.56), channel_id=1, source_target_pairs={{0,7},{1,6},{2,5},{3,4},{4,11},{5,10},{6,9},{7,8},{8,15},{9,14},{1... | collective-permute-start | bytes 393224 | tf_op jit(solution)/shard_map/ppermute | solution.py:151
  124.6 13.1 %collective-permute-start.34 = (bf16[16,16,256]{2,1,0:T(8,128)(2,1)}, bf16[16,16,256]{2,1,0:T(8,128)(2,1)S(1)}, u32[]{:S(2)}, u32[]{:S(2)}) collective-permute-start(bf16[16,16,256]{2,1,0:T(8,128)(2,1)} %get-tuple-element.55), channel_id=1, source_target_pairs={{0,11},{1,10},{2,9},{3,8},{4,15},{5,14},{6,13},{7,12},{8,3},{9,2},... | collective-permute-start | bytes 393224 | tf_op jit(solution)/shard_map/ppermute | solution.py:151
  127.2 10.5 %collective-permute-start.35 = (bf16[16,16,256]{2,1,0:T(8,128)(2,1)}, bf16[16,16,256]{2,1,0:T(8,128)(2,1)S(1)}, u32[]{:S(2)}, u32[]{:S(2)}) collective-permute-start(bf16[16,16,256]{2,1,0:T(8,128)(2,1)} %get-tuple-element.54), channel_id=1, source_target_pairs={{0,15},{1,14},{2,13},{3,12},{4,3},{5,2},{6,1},{7,0},{8,7},{9,6},{1... | collective-permute-start | bytes 393224 | tf_op jit(solution)/shard_map/ppermute | solution.py:151
  131.0 40.3 %collective-permute-start.43 = (bf16[4,1024,256]{2,1,0:T(8,128)(2,1)}, bf16[4,1024,256]{2,1,0:T(8,128)(2,1)}, u32[]{:S(2)}, u32[]{:S(2)}) collective-permute-start(bf16[4,1024,256]{2,1,0:T(8,128)(2,1)} %bitcast.203), channel_id=1, source_target_pairs={{0,1},{1,0},{2,3},{3,2},{4,5},{5,4},{6,7},{7,6},{8,9},{9,8},{10,11... | collective-permute-start | bytes 6291464 | tf_op jit(solution)/shard_map/ppermute | solution.py:151
  142.7 8.7 %collective-permute-start.36 = (bf16[32,8,256]{2,1,0:T(8,128)(2,1)S(1)}, bf16[32,8,256]{2,1,0:T(8,128)(2,1)S(1)}, u32[]{:S(2)}, u32[]{:S(2)}) collective-permute-start(bf16[32,8,256]{2,1,0:T(8,128)(2,1)S(1)} %get-tuple-element.77), channel_id=1, source_target_pairs={{0,4},{1,5},{2,6},{3,7},{4,8},{5,9},{6,10},{7,11},{8,12},{9,13},{1... | collective-permute-start | bytes 393224 | tf_op jit(solution)/shard_map/ppermute | solution.py:151
  145.8 11.3 %collective-permute-start.37 = (bf16[32,8,256]{2,1,0:T(8,128)(2,1)S(1)}, bf16[32,8,256]{2,1,0:T(8,128)(2,1)S(1)}, u32[]{:S(2)}, u32[]{:S(2)}) collective-permute-start(bf16[32,8,256]{2,1,0:T(8,128)(2,1)S(1)} %get-tuple-element.76), channel_id=1, source_target_pairs={{0,8},{1,9},{2,10},{3,11},{4,12},{5,13},{6,14},{7,15},{8,0},{9,1},... | collective-permute-start | bytes 393224 | tf_op jit(solution)/shard_map/ppermute | solution.py:151
  147.6 9.6 %collective-permute-start.38 = (bf16[32,8,256]{2,1,0:T(8,128)(2,1)S(1)}, bf16[32,8,256]{2,1,0:T(8,128)(2,1)S(1)}, u32[]{:S(2)}, u32[]{:S(2)}) collective-permute-start(bf16[32,8,256]{2,1,0:T(8,128)(2,1)S(1)} %get-tuple-element.79), channel_id=1, source_target_pairs={{0,12},{1,13},{2,14},{3,15},{4,0},{5,1},{6,2},{7,3},{8,4},{9,5},{1... | collective-permute-start | bytes 393224 | tf_op jit(solution)/shard_map/ppermute | solution.py:151
  148.2 13.4 %collective-permute-start.39 = (bf16[32,8,256]{2,1,0:T(8,128)(2,1)}, bf16[32,8,256]{2,1,0:T(8,128)(2,1)S(1)}, u32[]{:S(2)}, u32[]{:S(2)}) collective-permute-start(bf16[32,8,256]{2,1,0:T(8,128)(2,1)} %get-tuple-element.75), channel_id=1, source_target_pairs={{0,2},{1,3},{2,0},{3,1},{4,6},{5,7},{6,4},{7,5},{8,10},{9,11},{10,... | collective-permute-start | bytes 393224 | tf_op jit(solution)/shard_map/ppermute | solution.py:151
  151.5 10.2 %collective-permute-start.40 = (bf16[32,8,256]{2,1,0:T(8,128)(2,1)}, bf16[32,8,256]{2,1,0:T(8,128)(2,1)S(1)}, u32[]{:S(2)}, u32[]{:S(2)}) collective-permute-start(bf16[32,8,256]{2,1,0:T(8,128)(2,1)} %get-tuple-element.74), channel_id=1, source_target_pairs={{0,6},{1,7},{2,4},{3,5},{4,10},{5,11},{6,8},{7,9},{8,14},{9,15},{1... | collective-permute-start | bytes 393224 | tf_op jit(solution)/shard_map/ppermute | solution.py:151
  157.1 11.2 %collective-permute-start.41 = (bf16[32,8,256]{2,1,0:T(8,128)(2,1)}, bf16[32,8,256]{2,1,0:T(8,128)(2,1)S(1)}, u32[]{:S(2)}, u32[]{:S(2)}) collective-permute-start(bf16[32,8,256]{2,1,0:T(8,128)(2,1)} %get-tuple-element.73), channel_id=1, source_target_pairs={{0,10},{1,11},{2,8},{3,9},{4,14},{5,15},{6,12},{7,13},{8,2},{9,3},... | collective-permute-start | bytes 393224 | tf_op jit(solution)/shard_map/ppermute | solution.py:151
  157.2 13.8 %collective-permute-start.42 = (bf16[32,8,256]{2,1,0:T(8,128)(2,1)S(1)}, bf16[32,8,256]{2,1,0:T(8,128)(2,1)S(1)}, u32[]{:S(2)}, u32[]{:S(2)}) collective-permute-start(bf16[32,8,256]{2,1,0:T(8,128)(2,1)S(1)} %get-tuple-element.72), channel_id=1, source_target_pairs={{0,14},{1,15},{2,12},{3,13},{4,2},{5,3},{6,0},{7,1},{8,6},{9,7},{1... | collective-permute-start | bytes 393224 | tf_op jit(solution)/shard_map/ppermute | solution.py:151
  174.8 7.5 %collective-permute-start.44 = (bf16[32,1024]{1,0:T(8,128)(2,1)S(1)}, bf16[32,1024]{1,0:T(8,128)(2,1)S(1)}, u32[]{:S(2)}, u32[]{:S(2)}) collective-permute-start(bf16[32,1024]{1,0:T(8,128)(2,1)S(1)} %get-tuple-element.82), channel_id=1, source_target_pairs={{0,12},{1,13},{2,14},{3,15},{4,0},{5,1},{6,2},{7,3},{8,4},{9,5},{1... | collective-permute-start | bytes 196616 | tf_op jit(solution)/shard_map/ppermute | solution.py:151
  175.0 9.9 %collective-permute-start.45 = (bf16[32,1024]{1,0:T(8,128)(2,1)S(1)}, bf16[32,1024]{1,0:T(8,128)(2,1)S(1)}, u32[]{:S(2)}, u32[]{:S(2)}) collective-permute-start(bf16[32,1024]{1,0:T(8,128)(2,1)S(1)} %get-tuple-element.88), channel_id=1, source_target_pairs={{0,8},{1,9},{2,10},{3,11},{4,12},{5,13},{6,14},{7,15},{8,0},{9,1},... | collective-permute-start | bytes 196616 | tf_op jit(solution)/shard_map/ppermute | solution.py:151
  177.1 8.9 %collective-permute-start.46 = (bf16[32,1024]{1,0:T(8,128)(2,1)S(1)}, bf16[32,1024]{1,0:T(8,128)(2,1)S(1)}, u32[]{:S(2)}, u32[]{:S(2)}) collective-permute-start(bf16[32,1024]{1,0:T(8,128)(2,1)S(1)} %get-tuple-element.87), channel_id=1, source_target_pairs={{0,4},{1,5},{2,6},{3,7},{4,8},{5,9},{6,10},{7,11},{8,12},{9,13},{1... | collective-permute-start | bytes 196616 | tf_op jit(solution)/shard_map/ppermute | solution.py:151
  177.1 8.9 %collective-permute-start.47 = (bf16[32,1024]{1,0:T(8,128)(2,1)S(1)}, bf16[32,1024]{1,0:T(8,128)(2,1)S(1)}, u32[]{:S(2)}, u32[]{:S(2)}) collective-permute-start(bf16[32,1024]{1,0:T(8,128)(2,1)S(1)} %get-tuple-element.86), channel_id=1, source_target_pairs={{0,2},{1,3},{2,0},{3,1},{4,6},{5,7},{6,4},{7,5},{8,10},{9,11},{10,... | collective-permute-start | bytes 196616 | tf_op jit(solution)/shard_map/ppermute | solution.py:151
  178.2 7.8 %collective-permute-start.48 = (bf16[32,1024]{1,0:T(8,128)(2,1)S(1)}, bf16[32,1024]{1,0:T(8,128)(2,1)S(1)}, u32[]{:S(2)}, u32[]{:S(2)}) collective-permute-start(bf16[32,1024]{1,0:T(8,128)(2,1)S(1)} %get-tuple-element.85), channel_id=1, source_target_pairs={{0,14},{1,15},{2,12},{3,13},{4,2},{5,3},{6,0},{7,1},{8,6},{9,7},{1... | collective-permute-start | bytes 196616 | tf_op jit(solution)/shard_map/ppermute | solution.py:151
  182.4 6.7 %collective-permute-start.49 = (bf16[32,1024]{1,0:T(8,128)(2,1)S(1)}, bf16[32,1024]{1,0:T(8,128)(2,1)S(1)}, u32[]{:S(2)}, u32[]{:S(2)}) collective-permute-start(bf16[32,1024]{1,0:T(8,128)(2,1)S(1)} %get-tuple-element.84), channel_id=1, source_target_pairs={{0,10},{1,11},{2,8},{3,9},{4,14},{5,15},{6,12},{7,13},{8,2},{9,3},... | collective-permute-start | bytes 196616 | tf_op jit(solution)/shard_map/ppermute | solution.py:151
  184.9 7.0 %collective-permute-start.50 = (bf16[32,1024]{1,0:T(8,128)(2,1)S(1)}, bf16[32,1024]{1,0:T(8,128)(2,1)S(1)}, u32[]{:S(2)}, u32[]{:S(2)}) collective-permute-start(bf16[32,1024]{1,0:T(8,128)(2,1)S(1)} %get-tuple-element.83), channel_id=1, source_target_pairs={{0,6},{1,7},{2,4},{3,5},{4,10},{5,11},{6,8},{7,9},{8,14},{9,15},{1... | collective-permute-start | bytes 196616 | tf_op jit(solution)/shard_map/ppermute | solution.py:151

commit v5 on v4

--- a/solution.py
+++ b/solution.py
@@ -163,7 +163,8 @@
     ]
     place = jnp.stack(sources + [(plane + k) % planes for k in range(planes)]).astype(jnp.int32)
 
-    pairs = [(k, m) for m in range(0, inner, 2) for k in range(planes)]
+    shifts = sorted(range(planes), key=lambda k: -min(k, planes - k))
+    pairs = [(0, 0)] + [(k, m) for m in range(0, inner, 2) for k in shifts if (k, m) != (0, 0)]
     quarter = electrons // devices
 
     def send_electrons(parts):

time: 193 us -> 191 us (0.990)
  waiting for transfers between devices: 49.7 us -> 38.6 us
  starting transfers between devices: 97.9 us -> 107 us
    ppermute x51, waiting for transfers between devices: 49.7 us -> 38.6 us  [move(): return lax.ppermute(x, 'chol', route)]
    ppermute x51, starting transfers between devices: 93.6 us -> 102 us  [move(): return lax.ppermute(x, 'chol', route)]
  transfers between devices with their start and end apart: 52 -> 52, of which waited for: 15 -> 14; matrix products, arithmetic and copies ran while one was open for 14% -> 14% of each run, Pallas kernels for 4% -> 4%
where the time goes in v5:
time: 191 us; the launch traced here: 190 us
  starting transfers between devices  107 us (56%)
  waiting for transfers between devices  38.6 us (20%)
  matrix products  15.5 us (8%)
  local copies, waits for them, and re-layouts  12.4 us (6%)
  Pallas kernels  8.41 us (4%)
  other arithmetic  7.57 us (4%)
    ppermute x51, starting transfers between devices, move(): return lax.ppermute(x, 'chol', route)  102 us
    ppermute x51, waiting for transfers between devices, move(): return lax.ppermute(x, 'chol', route)  38.6 us
    dot_general x2, matrix products, operator_rows(): jnp.einsum('mkpg,gij->mkpij', part, chol_vectors, preferred_element_type=...  9.8 us
    pallas_call x2, Pallas kernels, propagate(): pl.pallas_call(functools.partial(propagate_kernel, len(pieces), planes, r...  8.41 us
    unnamed x18, local copies, waits for them, and re-layouts  6.08 us
    convert_element_type x2, other arithmetic, operator_rows(): return (made * scale).astype(jnp.bfloat16)  4.63 us
    all_to_all x1, starting transfers between devices, branch_walkers(): lax.all_to_all(outgoing, 'chol', split_axis=0, concat_axis=0, tiled=True)  4.34 us
  transfers between devices with their start and end apart: 52, of which 14 were waited for; matrix products, arithmetic and copies ran while one was open for 14% of the time, Pallas kernels for 4%

profile of v5, /device:TPU:0, one launch (start us, length us, event | category | flops | bytes accessed | tf_op | source)
XLA Modules:
  0.0 190.2 jit_solution(7211507030240808091)
XLA Ops:
  0.6 5.1 %collective-permute-start = (bf16[32,1024]{1,0:T(8,128)(2,1)}, bf16[32,1024]{1,0:T(8,128)(2,1)S(1)}, u32[]{:S(2)}, u32[]{:S(2)}) collective-permute-start(bf16[32,1024]{1,0:T(8,128)(2,1)} %param.7), channel_id=1, source_target_pairs={{0,12},{1,13},{2,14},{3,15},{4,0},{5,1},{6,2},{7,3},{8,4},{9,5},{1... | collective-permute-start | bytes 196616 | tf_op jit(solution)/shard_map/ppermute | solution.py:151
  5.7 1.0 collective-permute-start.2
  6.7 1.8 copy.53
  9.4 3.0 %collective-permute-done.1 = bf16[32,1024]{1,0:T(8,128)(2,1)S(1)} collective-permute-done((bf16[32,1024]{1,0:T(8,128)(2,1)}, bf16[32,1024]{1,0:T(8,128)(2,1)S(1)}, u32[]{:S(2)}, u32[]{:S(2)}) %collective-permute-start.1) | collective-permute-done | bytes 65568 | tf_op jit(solution)/shard_map/ppermute | solution.py:151
  12.4 0.9 fusion.23
  13.4 1.6 collective-permute-start.4
  15.7 1.5 all_to_all.8
  17.2 4.3 %all-to-all-start = ((bf16[16,2,16384]{2,1,0:T(2,128)(2,1)}), bf16[16,2,16384]{2,1,0:T(2,128)(2,1)}, u32[]{:S(2)}, u32[]{:S(2)}) async-start(bf16[16,2,16384]{2,1,0:T(2,128)(2,1)} %all_to_all.8), calls=%async_computation | async-start | bytes 2097152 | tf_op jit(solution)/shard_map/all_to_all | solution.py:28
  21.6 1.0 collective-permute-done.4
  22.6 6.9 %collective-permute-done.5 = bf16[4,32,1024]{2,1,0:T(8,128)(2,1)S(1)} collective-permute-done((bf16[4,32,1024]{2,1,0:T(8,128)(2,1)S(1)}, bf16[4,32,1024]{2,1,0:T(8,128)(2,1)S(1)}, u32[]{:S(2)}, u32[]{:S(2)}) %collective-permute-start.5) | collective-permute-done | bytes 262176 | tf_op jit(solution)/shard_map/ppermute | solution.py:151
  29.6 6.6 %fusion.2 = f32[4,4,16,16,256]{4,2,3,1,0:T(8,128)S(1)} fusion(bf16[1024,16,256,1,1]{2,1,0,4,3:T(8,128)(2,1)} %bitcast.223, bf16[4,4,32,1024]{3,2,1,0:T(8,128)(2,1)S(1)} %pad_maximum_fusion), kind=kOutput, calls=%fused_computation.4 | convolution fusion | flops 2147483648 | bytes 13107200 | tf_op jit(solution)/shard_map/mkpg,gij->mkpij/dot_general | solution.py:195
  36.2 3.2 %fusion = f32[4,4,16,16,256]{4,2,3,1,0:T(8,128)S(1)} fusion(bf16[1024,16,256,1,1]{2,1,0,4,3:T(8,128)(2,1)S(1)} %bitcast.226, bf16[4,4,32,1024]{3,2,1,0:T(8,128)(2,1)S(1)} %pad_maximum_fusion), kind=kOutput, calls=%fused_computation.2 | convolution fusion | flops 2147483648 | bytes 13107200 | tf_op jit(solution)/shard_map/mkpg,gij->mkpij/dot_general | solution.py:195
  39.5 2.3 %fusion.8 = bf16[4,4,16,16,256]{4,3,2,1,0:T(8,128)(2,1)S(1)} fusion(f32[4,4,16,16,256]{4,2,3,1,0:T(8,128)S(1)} %fusion.2), kind=kLoop, calls=%fused_computation.13 | loop fusion | flops 2097152 | bytes 6291456 | tf_op jit(solution)/shard_map/convert_element_type | solution.py:198
  42.0 2.3 %fusion.7 = bf16[4,4,16,16,256]{4,3,2,1,0:T(8,128)(2,1)S(1)} fusion(f32[4,4,16,16,256]{4,2,3,1,0:T(8,128)S(1)} %fusion), kind=kLoop, calls=%fused_computation.11 | loop fusion | flops 2097152 | bytes 6291456 | tf_op jit(solution)/shard_map/convert_element_type | solution.py:198
  44.6 2.3 %collective-permute-start.15 = (bf16[16,16,256]{2,1,0:T(8,128)(2,1)S(1)}, bf16[16,16,256]{2,1,0:T(8,128)(2,1)S(1)}, u32[]{:S(2)}, u32[]{:S(2)}) collective-permute-start(bf16[16,16,256]{2,1,0:T(8,128)(2,1)S(1)} %get-tuple-element.21), channel_id=1, source_target_pairs={{0,10},{1,11},{2,8},{3,9},{4,14},{5,15},{6,12},{7,13},{8,2},{9,3},... | collective-permute-start | bytes 393224 | tf_op jit(solution)/shard_map/ppermute | solution.py:151
  47.0 3.1 %collective-permute-start.16 = (bf16[16,16,256]{2,1,0:T(8,128)(2,1)S(1)}, bf16[16,16,256]{2,1,0:T(8,128)(2,1)S(1)}, u32[]{:S(2)}, u32[]{:S(2)}) collective-permute-start(bf16[16,16,256]{2,1,0:T(8,128)(2,1)S(1)} %get-tuple-element.22), channel_id=1, source_target_pairs={{0,14},{1,15},{2,12},{3,13},{4,2},{5,3},{6,0},{7,1},{8,6},{9,7},{1... | collective-permute-start | bytes 393224 | tf_op jit(solution)/shard_map/ppermute | solution.py:151
  51.1 2.0 %collective-permute-done.14.refs_9_ = bf16[16,16,256]{2,1,0:T(8,128)(2,1)S(1)} collective-permute-done((bf16[16,16,256]{2,1,0:T(8,128)(2,1)S(1)}, bf16[16,16,256]{2,1,0:T(8,128)(2,1)S(1)}, u32[]{:S(2)}, u32[]{:S(2)}) %collective-permute-start.14) | collective-permute-done | bytes 131104 | tf_op jit(solution)/shard_map/ppermute | solution.py:151
  53.1 5.9 %collective-permute-start.19 = (bf16[16,16,256]{2,1,0:T(8,128)(2,1)S(1)}, bf16[16,16,256]{2,1,0:T(8,128)(2,1)S(1)}, u32[]{:S(2)}, u32[]{:S(2)}) collective-permute-start(bf16[16,16,256]{2,1,0:T(8,128)(2,1)S(1)} %get-tuple-element.25), channel_id=1, source_target_pairs={{0,11},{1,10},{2,9},{3,8},{4,15},{5,14},{6,13},{7,12},{8,3},{9,2},... | collective-permute-start | bytes 393224 | tf_op jit(solution)/shard_map/ppermute | solution.py:151
  58.9 5.1 %collective-permute-start.20 = (bf16[16,16,256]{2,1,0:T(8,128)(2,1)S(1)}, bf16[16,16,256]{2,1,0:T(8,128)(2,1)S(1)}, u32[]{:S(2)}, u32[]{:S(2)}) collective-permute-start(bf16[16,16,256]{2,1,0:T(8,128)(2,1)S(1)} %get-tuple-element.26), channel_id=1, source_target_pairs={{0,15},{1,14},{2,13},{3,12},{4,3},{5,2},{6,1},{7,0},{8,7},{9,6},{1... | collective-permute-start | bytes 393224 | tf_op jit(solution)/shard_map/ppermute | solution.py:151
  64.0 3.2 %collective-permute-start.10 = (bf16[16,16,256]{2,1,0:T(8,128)(2,1)S(1)}, bf16[16,16,256]{2,1,0:T(8,128)(2,1)S(1)}, u32[]{:S(2)}, u32[]{:S(2)}) collective-permute-start(bf16[16,16,256]{2,1,0:T(8,128)(2,1)S(1)} %get-tuple-element.48), channel_id=1, source_target_pairs={{0,5},{1,4},{2,7},{3,6},{4,9},{5,8},{6,11},{7,10},{8,13},{9,12},{1... | collective-permute-start | bytes 393224 | tf_op jit(solution)/shard_map/ppermute | solution.py:151
  67.2 2.0 %collective-permute-start.12 = (bf16[16,16,256]{2,1,0:T(8,128)(2,1)S(1)}, bf16[16,16,256]{2,1,0:T(8,128)(2,1)S(1)}, u32[]{:S(2)}, u32[]{:S(2)}) collective-permute-start(bf16[16,16,256]{2,1,0:T(8,128)(2,1)S(1)} %get-tuple-element.46), channel_id=1, source_target_pairs={{0,13},{1,12},{2,15},{3,14},{4,1},{5,0},{6,3},{7,2},{8,5},{9,4},{1... | collective-permute-start | bytes 393224 | tf_op jit(solution)/shard_map/ppermute | solution.py:151
  69.2 6.4 %collective-permute-done.19.refs_14_ = bf16[16,16,256]{2,1,0:T(8,128)(2,1)S(1)} collective-permute-done((bf16[16,16,256]{2,1,0:T(8,128)(2,1)S(1)}, bf16[16,16,256]{2,1,0:T(8,128)(2,1)S(1)}, u32[]{:S(2)}, u32[]{:S(2)}) %collective-permute-start.19) | collective-permute-done | bytes 131104 | tf_op jit(solution)/shard_map/ppermute | solution.py:151
  76.4 1.0 slice_bitcast_fusion.5
  77.5 1.5 collective-permute-start.6
  79.0 2.6 %collective-permute-start.7 = (bf16[16,16,256]{2,1,0:T(8,128)(2,1)S(1)}, bf16[16,16,256]{2,1,0:T(8,128)(2,1)S(1)}, u32[]{:S(2)}, u32[]{:S(2)}) collective-permute-start(bf16[16,16,256]{2,1,0:T(8,128)(2,1)S(1)} %get-tuple-element.51), channel_id=1, source_target_pairs={{0,8},{1,9},{2,10},{3,11},{4,12},{5,13},{6,14},{7,15},{8,0},{9,1},... | collective-permute-start | bytes 393224 | tf_op jit(solution)/shard_map/ppermute | solution.py:151
  81.6 3.7 %collective-permute-start.8 = (bf16[16,16,256]{2,1,0:T(8,128)(2,1)S(1)}, bf16[16,16,256]{2,1,0:T(8,128)(2,1)S(1)}, u32[]{:S(2)}, u32[]{:S(2)}) collective-permute-start(bf16[16,16,256]{2,1,0:T(8,128)(2,1)S(1)} %get-tuple-element.50), channel_id=1, source_target_pairs={{0,12},{1,13},{2,14},{3,15},{4,0},{5,1},{6,2},{7,3},{8,4},{9,5},{1... | collective-permute-start | bytes 393224 | tf_op jit(solution)/shard_map/ppermute | solution.py:151
  85.3 4.3 %collective-permute-start.21 = (bf16[16,16,256]{2,1,0:T(8,128)(2,1)S(1)}, bf16[16,16,256]{2,1,0:T(8,128)(2,1)S(1)}, u32[]{:S(2)}, u32[]{:S(2)}) collective-permute-start(bf16[16,16,256]{2,1,0:T(8,128)(2,1)S(1)} %get-tuple-element.68), channel_id=1, source_target_pairs={{0,4},{1,5},{2,6},{3,7},{4,8},{5,9},{6,10},{7,11},{8,12},{9,13},{1... | collective-permute-start | bytes 393224 | tf_op jit(solution)/shard_map/ppermute | solution.py:151
  89.6 2.5 %collective-permute-start.22 = (bf16[16,16,256]{2,1,0:T(8,128)(2,1)}, bf16[16,16,256]{2,1,0:T(8,128)(2,1)S(1)}, u32[]{:S(2)}, u32[]{:S(2)}) collective-permute-start(bf16[16,16,256]{2,1,0:T(8,128)(2,1)} %get-tuple-element.67), channel_id=1, source_target_pairs={{0,8},{1,9},{2,10},{3,11},{4,12},{5,13},{6,14},{7,15},{8,0},{9,1},... | collective-permute-start | bytes 393224 | tf_op jit(solution)/shard_map/ppermute | solution.py:151
  92.1 1.1 collective-permute-done.7.refs_2_
  93.3 2.7 %collective-permute-start.23 = (bf16[16,16,256]{2,1,0:T(8,128)(2,1)}, bf16[16,16,256]{2,1,0:T(8,128)(2,1)S(1)}, u32[]{:S(2)}, u32[]{:S(2)}) collective-permute-start(bf16[16,16,256]{2,1,0:T(8,128)(2,1)} %get-tuple-element.66), channel_id=1, source_target_pairs={{0,12},{1,13},{2,14},{3,15},{4,0},{5,1},{6,2},{7,3},{8,4},{9,5},{1... | collective-permute-start | bytes 393224 | tf_op jit(solution)/shard_map/ppermute | solution.py:151
  96.0 1.4 collective-permute-start.24
  97.3 3.0 %collective-permute-start.25 = (bf16[16,16,256]{2,1,0:T(8,128)(2,1)}, bf16[16,16,256]{2,1,0:T(8,128)(2,1)S(1)}, u32[]{:S(2)}, u32[]{:S(2)}) collective-permute-start(bf16[16,16,256]{2,1,0:T(8,128)(2,1)} %get-tuple-element.64), channel_id=1, source_target_pairs={{0,5},{1,4},{2,7},{3,6},{4,9},{5,8},{6,11},{7,10},{8,13},{9,12},{1... | collective-permute-start | bytes 393224 | tf_op jit(solution)/shard_map/ppermute | solution.py:151
  100.3 3.3 %collective-permute-start.26 = (bf16[16,16,256]{2,1,0:T(8,128)(2,1)}, bf16[16,16,256]{2,1,0:T(8,128)(2,1)S(1)}, u32[]{:S(2)}, u32[]{:S(2)}) collective-permute-start(bf16[16,16,256]{2,1,0:T(8,128)(2,1)} %get-tuple-element.63), channel_id=1, source_target_pairs={{0,9},{1,8},{2,11},{3,10},{4,13},{5,12},{6,15},{7,14},{8,1},{9,0},... | collective-permute-start | bytes 393224 | tf_op jit(solution)/shard_map/ppermute | solution.py:151
  103.6 3.2 %copy.67 = bf16[1024,4,256]{2,0,1:T(8,128)(2,1)} copy(bf16[1024,4,256]{2,1,0:T(4,128)(2,1)} %param.9) | data formatting | bytes 4194304 | tf_op args[3]
  106.9 2.2 %all_to_all.10 = bf16[32,16384]{1,0:T(8,128)(2,1)} reshape(bf16[16,2,16384]{2,1,0:T(2,128)(2,1)} %all-to-all-done) | data formatting | bytes 2097152 | tf_op jit(solution)/shard_map/all_to_all | solution.py:28
  109.6 2.6 %collective-permute-start.29 = (bf16[16,16,256]{2,1,0:T(8,128)(2,1)S(1)}, bf16[16,16,256]{2,1,0:T(8,128)(2,1)S(1)}, u32[]{:S(2)}, u32[]{:S(2)}) collective-permute-start(bf16[16,16,256]{2,1,0:T(8,128)(2,1)S(1)} %get-tuple-element.60), channel_id=1, source_target_pairs={{0,6},{1,7},{2,4},{3,5},{4,10},{5,11},{6,8},{7,9},{8,14},{9,15},{1... | collective-permute-start | bytes 393224 | tf_op jit(solution)/shard_map/ppermute | solution.py:151
  112.7 1.7 collective-permute-done.26.refs_6_
  114.4 4.1 %collective-permute-start.31 = (bf16[16,16,256]{2,1,0:T(8,128)(2,1)S(1)}, bf16[16,16,256]{2,1,0:T(8,128)(2,1)S(1)}, u32[]{:S(2)}, u32[]{:S(2)}) collective-permute-start(bf16[16,16,256]{2,1,0:T(8,128)(2,1)S(1)} %get-tuple-element.58), channel_id=1, source_target_pairs={{0,14},{1,15},{2,12},{3,13},{4,2},{5,3},{6,0},{7,1},{8,6},{9,7},{1... | collective-permute-start | bytes 393224 | tf_op jit(solution)/shard_map/ppermute | solution.py:151
  118.5 1.7 convolution_convert_fusion
  120.2 1.0 collective-permute-start.32
  121.1 3.4 %collective-permute-start.33 = (bf16[16,16,256]{2,1,0:T(8,128)(2,1)}, bf16[16,16,256]{2,1,0:T(8,128)(2,1)S(1)}, u32[]{:S(2)}, u32[]{:S(2)}) collective-permute-start(bf16[16,16,256]{2,1,0:T(8,128)(2,1)} %get-tuple-element.56), channel_id=1, source_target_pairs={{0,7},{1,6},{2,5},{3,4},{4,11},{5,10},{6,9},{7,8},{8,15},{9,14},{1... | collective-permute-start | bytes 393224 | tf_op jit(solution)/shard_map/ppermute | solution.py:151
  124.6 2.6 %collective-permute-start.34 = (bf16[16,16,256]{2,1,0:T(8,128)(2,1)}, bf16[16,16,256]{2,1,0:T(8,128)(2,1)S(1)}, u32[]{:S(2)}, u32[]{:S(2)}) collective-permute-start(bf16[16,16,256]{2,1,0:T(8,128)(2,1)} %get-tuple-element.55), channel_id=1, source_target_pairs={{0,11},{1,10},{2,9},{3,8},{4,15},{5,14},{6,13},{7,12},{8,3},{9,2},... | collective-permute-start | bytes 393224 | tf_op jit(solution)/shard_map/ppermute | solution.py:151
  127.2 3.8 %collective-permute-start.35 = (bf16[16,16,256]{2,1,0:T(8,128)(2,1)}, bf16[16,16,256]{2,1,0:T(8,128)(2,1)S(1)}, u32[]{:S(2)}, u32[]{:S(2)}) collective-permute-start(bf16[16,16,256]{2,1,0:T(8,128)(2,1)} %get-tuple-element.54), channel_id=1, source_target_pairs={{0,15},{1,14},{2,13},{3,12},{4,3},{5,2},{6,1},{7,0},{8,7},{9,6},{1... | collective-permute-start | bytes 393224 | tf_op jit(solution)/shard_map/ppermute | solution.py:151
  131.3 4.2 %shard_map.77 = (bf16[16,64,256]{2,1,0:T(8,128)(2,1)S(1)}, bf16[16,16,256]{2,1,0:T(8,128)(2,1)S(1)}, bf16[16,16,256]{2,1,0:T(8,128)(2,1)S(1)}, bf16[16,16,256]{2,1,0:T(8,128)(2,1)S(1)}, bf16[16,16,256]{2,1,0:T(8,128)(2,1)S(1)}) custom-call(s32[20]{0:T(128)S(1)} %stack.169.place_ref, bf16[16,64,256]{2,1,0:T(8,128)(2,1)S(1)} %bitcast.193, ...), custom_call_target="tpu_custom_call" | custom-call | flops 671088640 | bytes 3670016 | tf_op jit(solution)/shard_map/pallas_call | solution.py:110
  135.6 2.1 %collective-permute-done.34.refs_14_ = bf16[16,16,256]{2,1,0:T(8,128)(2,1)S(1)} collective-permute-done((bf16[16,16,256]{2,1,0:T(8,128)(2,1)}, bf16[16,16,256]{2,1,0:T(8,128)(2,1)S(1)}, u32[]{:S(2)}, u32[]{:S(2)}) %collective-permute-start.34) | collective-permute-done | bytes 131104 | tf_op jit(solution)/shard_map/ppermute | solution.py:151
  137.6 4.2 %shard_map.78 = (bf16[16,64,256]{2,1,0:T(8,128)(2,1)S(1)}, bf16[16,16,256]{2,1,0:T(8,128)(2,1)S(1)}, bf16[16,16,256]{2,1,0:T(8,128)(2,1)S(1)}, bf16[16,16,256]{2,1,0:T(8,128)(2,1)S(1)}, bf16[16,16,256]{2,1,0:T(8,128)(2,1)S(1)}) custom-call(s32[20]{0:T(128)S(1)} %stack.169.place_ref, bf16[16,64,256]{2,1,0:T(8,128)(2,1)S(1)} %bitcast.192, ...), custom_call_target="tpu_custom_call" | custom-call | flops 671088640 | bytes 3670016 | tf_op jit(solution)/shard_map/pallas_call | solution.py:110
  143.5 4.2 %collective-permute-start.37 = (bf16[32,8,256]{2,1,0:T(8,128)(2,1)S(1)}, bf16[32,8,256]{2,1,0:T(8,128)(2,1)S(1)}, u32[]{:S(2)}, u32[]{:S(2)}) collective-permute-start(bf16[32,8,256]{2,1,0:T(8,128)(2,1)S(1)} %get-tuple-element.76), channel_id=1, source_target_pairs={{0,4},{1,5},{2,6},{3,7},{4,8},{5,9},{6,10},{7,11},{8,12},{9,13},{1... | collective-permute-start | bytes 393224 | tf_op jit(solution)/shard_map/ppermute | solution.py:151
  148.2 1.7 collective-permute-start.39
  149.9 3.7 %collective-permute-start.40 = (bf16[32,8,256]{2,1,0:T(8,128)(2,1)}, bf16[32,8,256]{2,1,0:T(8,128)(2,1)S(1)}, u32[]{:S(2)}, u32[]{:S(2)}) collective-permute-start(bf16[32,8,256]{2,1,0:T(8,128)(2,1)} %get-tuple-element.74), channel_id=1, source_target_pairs={{0,6},{1,7},{2,4},{3,5},{4,10},{5,11},{6,8},{7,9},{8,14},{9,15},{1... | collective-permute-start | bytes 393224 | tf_op jit(solution)/shard_map/ppermute | solution.py:151
  153.6 1.8 collective-permute-done.37
  155.4 3.9 %collective-permute-start.41 = (bf16[32,8,256]{2,1,0:T(8,128)(2,1)}, bf16[32,8,256]{2,1,0:T(8,128)(2,1)S(1)}, u32[]{:S(2)}, u32[]{:S(2)}) collective-permute-start(bf16[32,8,256]{2,1,0:T(8,128)(2,1)} %get-tuple-element.73), channel_id=1, source_target_pairs={{0,14},{1,15},{2,12},{3,13},{4,2},{5,3},{6,0},{7,1},{8,6},{9,7},{1... | collective-permute-start | bytes 393224 | tf_op jit(solution)/shard_map/ppermute | solution.py:151
  160.4 5.5 %collective-permute-done.39 = bf16[32,8,256]{2,1,0:T(8,128)(2,1)S(1)} collective-permute-done((bf16[32,8,256]{2,1,0:T(8,128)(2,1)}, bf16[32,8,256]{2,1,0:T(8,128)(2,1)S(1)}, u32[]{:S(2)}, u32[]{:S(2)}) %collective-permute-start.39) | collective-permute-done | bytes 131104 | tf_op jit(solution)/shard_map/ppermute | solution.py:151
  165.9 2.5 %collective-permute-done.41 = bf16[32,8,256]{2,1,0:T(8,128)(2,1)S(1)} collective-permute-done((bf16[32,8,256]{2,1,0:T(8,128)(2,1)}, bf16[32,8,256]{2,1,0:T(8,128)(2,1)S(1)}, u32[]{:S(2)}, u32[]{:S(2)}) %collective-permute-start.41) | collective-permute-done | bytes 131104 | tf_op jit(solution)/shard_map/ppermute | solution.py:151
  168.5 1.7 collective-permute-done.42
  170.5 3.5 %fusion.25 = (bf16[8,32,1024]{2,1,0:T(8,128)(2,1)S(1)}, f32[8,32,1024]{2,1,0:T(8,128)S(1)}) fusion(bf16[4,1024,256]{2,1,0:T(8,128)(2,1)} %collective-permute-done.43, bf16[4,1024,256]{2,1,0:T(8,128)(2,1)} %bitcast.204, bf16[8,32,4,256]{3,1,2,0:T(8,128)(2,1)S(1)} %get-tuple-element.71, bf16[8,32,4,256]{3,1,2,0:T(8,128)(2,1)S(1)} %get-tuple-element.70), kind=kOutput, calls=%fused_computation.97 | convolution fusion | flops 1076625408 | bytes 6815744 | tf_op jit(solution)/shard_map/rpej,egj->rpg/dot_general | solution.py:191
  174.0 3.2 %collective-permute-start.44 = (bf16[32,1024]{1,0:T(8,128)(2,1)S(1)}, bf16[32,1024]{1,0:T(8,128)(2,1)S(1)}, u32[]{:S(2)}, u32[]{:S(2)}) collective-permute-start(bf16[32,1024]{1,0:T(8,128)(2,1)S(1)} %get-tuple-element.82), channel_id=1, source_target_pairs={{0,8},{1,9},{2,10},{3,11},{4,12},{5,13},{6,14},{7,15},{8,0},{9,1},... | collective-permute-start | bytes 196616 | tf_op jit(solution)/shard_map/ppermute | solution.py:151
  177.2 2.0 %collective-permute-start.46 = (bf16[32,1024]{1,0:T(8,128)(2,1)S(1)}, bf16[32,1024]{1,0:T(8,128)(2,1)S(1)}, u32[]{:S(2)}, u32[]{:S(2)}) collective-permute-start(bf16[32,1024]{1,0:T(8,128)(2,1)S(1)} %get-tuple-element.87), channel_id=1, source_target_pairs={{0,4},{1,5},{2,6},{3,7},{4,8},{5,9},{6,10},{7,11},{8,12},{9,13},{1... | collective-permute-start | bytes 196616 | tf_op jit(solution)/shard_map/ppermute | solution.py:151
  179.3 1.2 collective-permute-start.47
  180.5 2.0 %collective-permute-start.48 = (bf16[32,1024]{1,0:T(8,128)(2,1)S(1)}, bf16[32,1024]{1,0:T(8,128)(2,1)S(1)}, u32[]{:S(2)}, u32[]{:S(2)}) collective-permute-start(bf16[32,1024]{1,0:T(8,128)(2,1)S(1)} %get-tuple-element.85), channel_id=1, source_target_pairs={{0,14},{1,15},{2,12},{3,13},{4,2},{5,3},{6,0},{7,1},{8,6},{9,7},{1... | collective-permute-start | bytes 196616 | tf_op jit(solution)/shard_map/ppermute | solution.py:151
  182.5 0.9 collective-permute-start.49
  183.4 2.1 %collective-permute-start.50 = (bf16[32,1024]{1,0:T(8,128)(2,1)S(1)}, bf16[32,1024]{1,0:T(8,128)(2,1)S(1)}, u32[]{:S(2)}, u32[]{:S(2)}) collective-permute-start(bf16[32,1024]{1,0:T(8,128)(2,1)S(1)} %get-tuple-element.83), channel_id=1, source_target_pairs={{0,2},{1,3},{2,0},{3,1},{4,6},{5,7},{6,4},{7,5},{8,10},{9,11},{10,... | collective-permute-start | bytes 196616 | tf_op jit(solution)/shard_map/ppermute | solution.py:151
  185.6 1.1 pad_maximum_fusion.1
  186.6 1.0 collective-permute-done.47
  187.7 1.8 collective-permute-done.49
  (92 shorter events, 9.8 us)
Async XLA Ops:
  0.6 8.8 %collective-permute-start = (bf16[32,1024]{1,0:T(8,128)(2,1)}, bf16[32,1024]{1,0:T(8,128)(2,1)S(1)}, u32[]{:S(2)}, u32[]{:S(2)}) collective-permute-start(bf16[32,1024]{1,0:T(8,128)(2,1)} %param.7), channel_id=1, source_target_pairs={{0,12},{1,13},{2,14},{3,15},{4,0},{5,1},{6,2},{7,3},{8,4},{9,5},{1... | collective-permute-start | bytes 196616 | tf_op jit(solution)/shard_map/ppermute | solution.py:151
  5.7 6.7 %collective-permute-start.1 = (bf16[32,1024]{1,0:T(8,128)(2,1)}, bf16[32,1024]{1,0:T(8,128)(2,1)S(1)}, u32[]{:S(2)}, u32[]{:S(2)}) collective-permute-start(bf16[32,1024]{1,0:T(8,128)(2,1)} %param.7), channel_id=1, source_target_pairs={{0,8},{1,9},{2,10},{3,11},{4,12},{5,13},{6,14},{7,15},{8,0},{9,1},... | collective-permute-start | bytes 196616 | tf_op jit(solution)/shard_map/ppermute | solution.py:151
  5.7 6.7 %collective-permute-start.2 = (bf16[32,1024]{1,0:T(8,128)(2,1)}, bf16[32,1024]{1,0:T(8,128)(2,1)S(1)}, u32[]{:S(2)}, u32[]{:S(2)}) collective-permute-start(bf16[32,1024]{1,0:T(8,128)(2,1)} %param.7), channel_id=1, source_target_pairs={{0,4},{1,5},{2,6},{3,7},{4,8},{5,9},{6,10},{7,11},{8,12},{9,13},{1... | collective-permute-start | bytes 196616 | tf_op jit(solution)/shard_map/ppermute | solution.py:151
  13.3 8.3 %collective-permute-start.3 = (bf16[4,32,1024]{2,1,0:T(8,128)(2,1)S(1)}, bf16[4,32,1024]{2,1,0:T(8,128)(2,1)S(1)}, u32[]{:S(2)}, u32[]{:S(2)}) collective-permute-start(bf16[4,32,1024]{2,1,0:T(8,128)(2,1)S(1)} %get-tuple-element.90), channel_id=1, source_target_pairs={{0,1},{1,0},{2,3},{3,2},{4,5},{5,4},{6,7},{7,6},{8,9},{9,8},{10,11... | collective-permute-start | bytes 786440 | tf_op jit(solution)/shard_map/ppermute | solution.py:151
  13.4 9.2 %collective-permute-start.4 = (bf16[4,32,1024]{2,1,0:T(8,128)(2,1)S(1)}, bf16[4,32,1024]{2,1,0:T(8,128)(2,1)S(1)}, u32[]{:S(2)}, u32[]{:S(2)}) collective-permute-start(bf16[4,32,1024]{2,1,0:T(8,128)(2,1)S(1)} %get-tuple-element.90), channel_id=1, source_target_pairs={{0,2},{1,3},{2,0},{3,1},{4,6},{5,7},{6,4},{7,5},{8,10},{9,11},{10,... | collective-permute-start | bytes 786440 | tf_op jit(solution)/shard_map/ppermute | solution.py:151
  15.0 14.5 %collective-permute-start.5 = (bf16[4,32,1024]{2,1,0:T(8,128)(2,1)S(1)}, bf16[4,32,1024]{2,1,0:T(8,128)(2,1)S(1)}, u32[]{:S(2)}, u32[]{:S(2)}) collective-permute-start(bf16[4,32,1024]{2,1,0:T(8,128)(2,1)S(1)} %get-tuple-element.90), channel_id=1, source_target_pairs={{0,3},{1,2},{2,1},{3,0},{4,7},{5,6},{6,5},{7,4},{8,11},{9,10},{10,... | collective-permute-start | bytes 786440 | tf_op jit(solution)/shard_map/ppermute | solution.py:151
  17.2 89.7 %all-to-all-start = ((bf16[16,2,16384]{2,1,0:T(2,128)(2,1)}), bf16[16,2,16384]{2,1,0:T(2,128)(2,1)}, u32[]{:S(2)}, u32[]{:S(2)}) async-start(bf16[16,2,16384]{2,1,0:T(2,128)(2,1)} %all_to_all.8), calls=%async_computation | async-start | bytes 2097152 | tf_op jit(solution)/shard_map/all_to_all | solution.py:28
  29.5 6.7 %slice-start = ((s8[8388608]{0:T(1024)(128)(4,1)}), s8[4194304]{0:T(1024)(128)(4,1)S(1)}, s32[]{:S(2)}) async-start(s8[8388608]{0:T(1024)(128)(4,1)} %bitcast.224), calls=%async_computation.1 | async-start | bytes 8388608
  29.6 6.6 %slice-start.1 = ((s8[8388608]{0:T(1024)(128)(4,1)}), s8[4194304]{0:T(1024)(128)(4,1)S(1)}, s32[]{:S(2)}) async-start(s8[8388608]{0:T(1024)(128)(4,1)} %bitcast.224), calls=%async_computation.2 | async-start | bytes 8388608
  44.3 8.8 %collective-permute-start.14 = (bf16[16,16,256]{2,1,0:T(8,128)(2,1)S(1)}, bf16[16,16,256]{2,1,0:T(8,128)(2,1)S(1)}, u32[]{:S(2)}, u32[]{:S(2)}) collective-permute-start(bf16[16,16,256]{2,1,0:T(8,128)(2,1)S(1)} %get-tuple-element.20), channel_id=1, source_target_pairs={{0,6},{1,7},{2,4},{3,5},{4,10},{5,11},{6,8},{7,9},{8,14},{9,15},{1... | collective-permute-start | bytes 393224 | tf_op jit(solution)/shard_map/ppermute | solution.py:151
  44.6 14.3 %collective-permute-start.15 = (bf16[16,16,256]{2,1,0:T(8,128)(2,1)S(1)}, bf16[16,16,256]{2,1,0:T(8,128)(2,1)S(1)}, u32[]{:S(2)}, u32[]{:S(2)}) collective-permute-start(bf16[16,16,256]{2,1,0:T(8,128)(2,1)S(1)} %get-tuple-element.21), channel_id=1, source_target_pairs={{0,10},{1,11},{2,8},{3,9},{4,14},{5,15},{6,12},{7,13},{8,2},{9,3},... | collective-permute-start | bytes 393224 | tf_op jit(solution)/shard_map/ppermute | solution.py:151
  47.0 17.0 %collective-permute-start.16 = (bf16[16,16,256]{2,1,0:T(8,128)(2,1)S(1)}, bf16[16,16,256]{2,1,0:T(8,128)(2,1)S(1)}, u32[]{:S(2)}, u32[]{:S(2)}) collective-permute-start(bf16[16,16,256]{2,1,0:T(8,128)(2,1)S(1)} %get-tuple-element.22), channel_id=1, source_target_pairs={{0,14},{1,15},{2,12},{3,13},{4,2},{5,3},{6,0},{7,1},{8,6},{9,7},{1... | collective-permute-start | bytes 393224 | tf_op jit(solution)/shard_map/ppermute | solution.py:151
  50.0 17.1 %collective-permute-start.17 = (bf16[16,16,256]{2,1,0:T(8,128)(2,1)S(1)}, bf16[16,16,256]{2,1,0:T(8,128)(2,1)S(1)}, u32[]{:S(2)}, u32[]{:S(2)}) collective-permute-start(bf16[16,16,256]{2,1,0:T(8,128)(2,1)S(1)} %get-tuple-element.23), channel_id=1, source_target_pairs={{0,3},{1,2},{2,1},{3,0},{4,7},{5,6},{6,5},{7,4},{8,11},{9,10},{10,... | collective-permute-start | bytes 393224 | tf_op jit(solution)/shard_map/ppermute | solution.py:151
  50.3 16.8 %collective-permute-start.18 = (bf16[16,16,256]{2,1,0:T(8,128)(2,1)S(1)}, bf16[16,16,256]{2,1,0:T(8,128)(2,1)S(1)}, u32[]{:S(2)}, u32[]{:S(2)}) collective-permute-start(bf16[16,16,256]{2,1,0:T(8,128)(2,1)S(1)} %get-tuple-element.24), channel_id=1, source_target_pairs={{0,7},{1,6},{2,5},{3,4},{4,11},{5,10},{6,9},{7,8},{8,15},{9,14},{1... | collective-permute-start | bytes 393224 | tf_op jit(solution)/shard_map/ppermute | solution.py:151
  53.1 22.5 %collective-permute-start.19 = (bf16[16,16,256]{2,1,0:T(8,128)(2,1)S(1)}, bf16[16,16,256]{2,1,0:T(8,128)(2,1)S(1)}, u32[]{:S(2)}, u32[]{:S(2)}) collective-permute-start(bf16[16,16,256]{2,1,0:T(8,128)(2,1)S(1)} %get-tuple-element.25), channel_id=1, source_target_pairs={{0,11},{1,10},{2,9},{3,8},{4,15},{5,14},{6,13},{7,12},{8,3},{9,2},... | collective-permute-start | bytes 393224 | tf_op jit(solution)/shard_map/ppermute | solution.py:151
  58.9 18.5 %collective-permute-start.20 = (bf16[16,16,256]{2,1,0:T(8,128)(2,1)S(1)}, bf16[16,16,256]{2,1,0:T(8,128)(2,1)S(1)}, u32[]{:S(2)}, u32[]{:S(2)}) collective-permute-start(bf16[16,16,256]{2,1,0:T(8,128)(2,1)S(1)} %get-tuple-element.26), channel_id=1, source_target_pairs={{0,15},{1,14},{2,13},{3,12},{4,3},{5,2},{6,1},{7,0},{8,7},{9,6},{1... | collective-permute-start | bytes 393224 | tf_op jit(solution)/shard_map/ppermute | solution.py:151
  64.0 15.0 %collective-permute-start.10 = (bf16[16,16,256]{2,1,0:T(8,128)(2,1)S(1)}, bf16[16,16,256]{2,1,0:T(8,128)(2,1)S(1)}, u32[]{:S(2)}, u32[]{:S(2)}) collective-permute-start(bf16[16,16,256]{2,1,0:T(8,128)(2,1)S(1)} %get-tuple-element.48), channel_id=1, source_target_pairs={{0,5},{1,4},{2,7},{3,6},{4,9},{5,8},{6,11},{7,10},{8,13},{9,12},{1... | collective-permute-start | bytes 393224 | tf_op jit(solution)/shard_map/ppermute | solution.py:151
  67.2 14.4 %collective-permute-start.11 = (bf16[16,16,256]{2,1,0:T(8,128)(2,1)S(1)}, bf16[16,16,256]{2,1,0:T(8,128)(2,1)S(1)}, u32[]{:S(2)}, u32[]{:S(2)}) collective-permute-start(bf16[16,16,256]{2,1,0:T(8,128)(2,1)S(1)} %get-tuple-element.47), channel_id=1, source_target_pairs={{0,9},{1,8},{2,11},{3,10},{4,13},{5,12},{6,15},{7,14},{8,1},{9,0},... | collective-permute-start | bytes 393224 | tf_op jit(solution)/shard_map/ppermute | solution.py:151
  67.2 18.2 %collective-permute-start.12 = (bf16[16,16,256]{2,1,0:T(8,128)(2,1)S(1)}, bf16[16,16,256]{2,1,0:T(8,128)(2,1)S(1)}, u32[]{:S(2)}, u32[]{:S(2)}) collective-permute-start(bf16[16,16,256]{2,1,0:T(8,128)(2,1)S(1)} %get-tuple-element.46), channel_id=1, source_target_pairs={{0,13},{1,12},{2,15},{3,14},{4,1},{5,0},{6,3},{7,2},{8,5},{9,4},{1... | collective-permute-start | bytes 393224 | tf_op jit(solution)/shard_map/ppermute | solution.py:151
  75.6 9.8 %collective-permute-start.13 = (bf16[16,16,256]{2,1,0:T(8,128)(2,1)S(1)}, bf16[16,16,256]{2,1,0:T(8,128)(2,1)S(1)}, u32[]{:S(2)}, u32[]{:S(2)}) collective-permute-start(bf16[16,16,256]{2,1,0:T(8,128)(2,1)S(1)} %get-tuple-element.45), channel_id=1, source_target_pairs={{0,2},{1,3},{2,0},{3,1},{4,6},{5,7},{6,4},{7,5},{8,10},{9,11},{10,... | collective-permute-start | bytes 393224 | tf_op jit(solution)/shard_map/ppermute | solution.py:151
  77.5 41.0 %copy-start = (s32[32]{0:T(128)S(1)}, s32[32]{0:T(128)}, u32[]{:S(2)}) copy-start(s32[32]{0:T(128)} %param.11) | copy-start | bytes 388
  77.5 12.2 %collective-permute-start.6 = (bf16[16,16,256]{2,1,0:T(8,128)(2,1)S(1)}, bf16[16,16,256]{2,1,0:T(8,128)(2,1)S(1)}, u32[]{:S(2)}, u32[]{:S(2)}) collective-permute-start(bf16[16,16,256]{2,1,0:T(8,128)(2,1)S(1)} %get-tuple-element.52), channel_id=1, source_target_pairs={{0,4},{1,5},{2,6},{3,7},{4,8},{5,9},{6,10},{7,11},{8,12},{9,13},{1... | collective-permute-start | bytes 393224 | tf_op jit(solution)/shard_map/ppermute | solution.py:151
  79.0 14.3 %collective-permute-start.7 = (bf16[16,16,256]{2,1,0:T(8,128)(2,1)S(1)}, bf16[16,16,256]{2,1,0:T(8,128)(2,1)S(1)}, u32[]{:S(2)}, u32[]{:S(2)}) collective-permute-start(bf16[16,16,256]{2,1,0:T(8,128)(2,1)S(1)} %get-tuple-element.51), channel_id=1, source_target_pairs={{0,8},{1,9},{2,10},{3,11},{4,12},{5,13},{6,14},{7,15},{8,0},{9,1},... | collective-permute-start | bytes 393224 | tf_op jit(solution)/shard_map/ppermute | solution.py:151
  81.6 14.4 %collective-permute-start.8 = (bf16[16,16,256]{2,1,0:T(8,128)(2,1)S(1)}, bf16[16,16,256]{2,1,0:T(8,128)(2,1)S(1)}, u32[]{:S(2)}, u32[]{:S(2)}) collective-permute-start(bf16[16,16,256]{2,1,0:T(8,128)(2,1)S(1)} %get-tuple-element.50), channel_id=1, source_target_pairs={{0,12},{1,13},{2,14},{3,15},{4,0},{5,1},{6,2},{7,3},{8,4},{9,5},{1... | collective-permute-start | bytes 393224 | tf_op jit(solution)/shard_map/ppermute | solution.py:151
  85.3 12.0 %collective-permute-start.9 = (bf16[16,16,256]{2,1,0:T(8,128)(2,1)S(1)}, bf16[16,16,256]{2,1,0:T(8,128)(2,1)S(1)}, u32[]{:S(2)}, u32[]{:S(2)}) collective-permute-start(bf16[16,16,256]{2,1,0:T(8,128)(2,1)S(1)} %get-tuple-element.49), channel_id=1, source_target_pairs={{0,1},{1,0},{2,3},{3,2},{4,5},{5,4},{6,7},{7,6},{8,9},{9,8},{10,11... | collective-permute-start | bytes 393224 | tf_op jit(solution)/shard_map/ppermute | solution.py:151
  85.3 15.0 %collective-permute-start.21 = (bf16[16,16,256]{2,1,0:T(8,128)(2,1)S(1)}, bf16[16,16,256]{2,1,0:T(8,128)(2,1)S(1)}, u32[]{:S(2)}, u32[]{:S(2)}) collective-permute-start(bf16[16,16,256]{2,1,0:T(8,128)(2,1)S(1)} %get-tuple-element.68), channel_id=1, source_target_pairs={{0,4},{1,5},{2,6},{3,7},{4,8},{5,9},{6,10},{7,11},{8,12},{9,13},{1... | collective-permute-start | bytes 393224 | tf_op jit(solution)/shard_map/ppermute | solution.py:151
  89.6 19.5 %collective-permute-start.22 = (bf16[16,16,256]{2,1,0:T(8,128)(2,1)}, bf16[16,16,256]{2,1,0:T(8,128)(2,1)S(1)}, u32[]{:S(2)}, u32[]{:S(2)}) collective-permute-start(bf16[16,16,256]{2,1,0:T(8,128)(2,1)} %get-tuple-element.67), channel_id=1, source_target_pairs={{0,8},{1,9},{2,10},{3,11},{4,12},{5,13},{6,14},{7,15},{8,0},{9,1},... | collective-permute-start | bytes 393224 | tf_op jit(solution)/shard_map/ppermute | solution.py:151
  93.3 15.9 %collective-permute-start.23 = (bf16[16,16,256]{2,1,0:T(8,128)(2,1)}, bf16[16,16,256]{2,1,0:T(8,128)(2,1)S(1)}, u32[]{:S(2)}, u32[]{:S(2)}) collective-permute-start(bf16[16,16,256]{2,1,0:T(8,128)(2,1)} %get-tuple-element.66), channel_id=1, source_target_pairs={{0,12},{1,13},{2,14},{3,15},{4,0},{5,1},{6,2},{7,3},{8,4},{9,5},{1... | collective-permute-start | bytes 393224 | tf_op jit(solution)/shard_map/ppermute | solution.py:151
  96.0 13.6 %collective-permute-start.24 = (bf16[16,16,256]{2,1,0:T(8,128)(2,1)}, bf16[16,16,256]{2,1,0:T(8,128)(2,1)S(1)}, u32[]{:S(2)}, u32[]{:S(2)}) collective-permute-start(bf16[16,16,256]{2,1,0:T(8,128)(2,1)} %get-tuple-element.65), channel_id=1, source_target_pairs={{0,1},{1,0},{2,3},{3,2},{4,5},{5,4},{6,7},{7,6},{8,9},{9,8},{10,11... | collective-permute-start | bytes 393224 | tf_op jit(solution)/shard_map/ppermute | solution.py:151
  97.3 14.9 %collective-permute-start.25 = (bf16[16,16,256]{2,1,0:T(8,128)(2,1)}, bf16[16,16,256]{2,1,0:T(8,128)(2,1)S(1)}, u32[]{:S(2)}, u32[]{:S(2)}) collective-permute-start(bf16[16,16,256]{2,1,0:T(8,128)(2,1)} %get-tuple-element.64), channel_id=1, source_target_pairs={{0,5},{1,4},{2,7},{3,6},{4,9},{5,8},{6,11},{7,10},{8,13},{9,12},{1... | collective-permute-start | bytes 393224 | tf_op jit(solution)/shard_map/ppermute | solution.py:151
  100.3 14.1 %collective-permute-start.26 = (bf16[16,16,256]{2,1,0:T(8,128)(2,1)}, bf16[16,16,256]{2,1,0:T(8,128)(2,1)S(1)}, u32[]{:S(2)}, u32[]{:S(2)}) collective-permute-start(bf16[16,16,256]{2,1,0:T(8,128)(2,1)} %get-tuple-element.63), channel_id=1, source_target_pairs={{0,9},{1,8},{2,11},{3,10},{4,13},{5,12},{6,15},{7,14},{8,1},{9,0},... | collective-permute-start | bytes 393224 | tf_op jit(solution)/shard_map/ppermute | solution.py:151
  109.2 11.0 %collective-permute-start.27 = (bf16[16,16,256]{2,1,0:T(8,128)(2,1)}, bf16[16,16,256]{2,1,0:T(8,128)(2,1)S(1)}, u32[]{:S(2)}, u32[]{:S(2)}) collective-permute-start(bf16[16,16,256]{2,1,0:T(8,128)(2,1)} %get-tuple-element.62), channel_id=1, source_target_pairs={{0,13},{1,12},{2,15},{3,14},{4,1},{5,0},{6,3},{7,2},{8,5},{9,4},{1... | collective-permute-start | bytes 393224 | tf_op jit(solution)/shard_map/ppermute | solution.py:151
  109.2 12.0 %collective-permute-start.28 = (bf16[16,16,256]{2,1,0:T(8,128)(2,1)S(1)}, bf16[16,16,256]{2,1,0:T(8,128)(2,1)S(1)}, u32[]{:S(2)}, u32[]{:S(2)}) collective-permute-start(bf16[16,16,256]{2,1,0:T(8,128)(2,1)S(1)} %get-tuple-element.61), channel_id=1, source_target_pairs={{0,2},{1,3},{2,0},{3,1},{4,6},{5,7},{6,4},{7,5},{8,10},{9,11},{10,... | collective-permute-start | bytes 393224 | tf_op jit(solution)/shard_map/ppermute | solution.py:151
  109.6 15.0 %collective-permute-start.29 = (bf16[16,16,256]{2,1,0:T(8,128)(2,1)S(1)}, bf16[16,16,256]{2,1,0:T(8,128)(2,1)S(1)}, u32[]{:S(2)}, u32[]{:S(2)}) collective-permute-start(bf16[16,16,256]{2,1,0:T(8,128)(2,1)S(1)} %get-tuple-element.60), channel_id=1, source_target_pairs={{0,6},{1,7},{2,4},{3,5},{4,10},{5,11},{6,8},{7,9},{8,14},{9,15},{1... | collective-permute-start | bytes 393224 | tf_op jit(solution)/shard_map/ppermute | solution.py:151
  112.2 14.9 %collective-permute-start.30 = (bf16[16,16,256]{2,1,0:T(8,128)(2,1)S(1)}, bf16[16,16,256]{2,1,0:T(8,128)(2,1)S(1)}, u32[]{:S(2)}, u32[]{:S(2)}) collective-permute-start(bf16[16,16,256]{2,1,0:T(8,128)(2,1)S(1)} %get-tuple-element.59), channel_id=1, source_target_pairs={{0,10},{1,11},{2,8},{3,9},{4,14},{5,15},{6,12},{7,13},{8,2},{9,3},... | collective-permute-start | bytes 393224 | tf_op jit(solution)/shard_map/ppermute | solution.py:151
  114.4 16.6 %collective-permute-start.31 = (bf16[16,16,256]{2,1,0:T(8,128)(2,1)S(1)}, bf16[16,16,256]{2,1,0:T(8,128)(2,1)S(1)}, u32[]{:S(2)}, u32[]{:S(2)}) collective-permute-start(bf16[16,16,256]{2,1,0:T(8,128)(2,1)S(1)} %get-tuple-element.58), channel_id=1, source_target_pairs={{0,14},{1,15},{2,12},{3,13},{4,2},{5,3},{6,0},{7,1},{8,6},{9,7},{1... | collective-permute-start | bytes 393224 | tf_op jit(solution)/shard_map/ppermute | solution.py:151
  120.2 15.4 %collective-permute-start.32 = (bf16[16,16,256]{2,1,0:T(8,128)(2,1)}, bf16[16,16,256]{2,1,0:T(8,128)(2,1)S(1)}, u32[]{:S(2)}, u32[]{:S(2)}) collective-permute-start(bf16[16,16,256]{2,1,0:T(8,128)(2,1)} %get-tuple-element.57), channel_id=1, source_target_pairs={{0,3},{1,2},{2,1},{3,0},{4,7},{5,6},{6,5},{7,4},{8,11},{9,10},{10,... | collective-permute-start | bytes 393224 | tf_op jit(solution)/shard_map/ppermute | solution.py:151
  121.1 14.4 %collective-permute-start.33 = (bf16[16,16,256]{2,1,0:T(8,128)(2,1)}, bf16[16,16,256]{2,1,0:T(8,128)(2,1)S(1)}, u32[]{:S(2)}, u32[]{:S(2)}) collective-permute-start(bf16[16,16,256]{2,1,0:T(8,128)(2,1)} %get-tuple-element.56), channel_id=1, source_target_pairs={{0,7},{1,6},{2,5},{3,4},{4,11},{5,10},{6,9},{7,8},{8,15},{9,14},{1... | collective-permute-start | bytes 393224 | tf_op jit(solution)/shard_map/ppermute | solution.py:151
  124.6 13.1 %collective-permute-start.34 = (bf16[16,16,256]{2,1,0:T(8,128)(2,1)}, bf16[16,16,256]{2,1,0:T(8,128)(2,1)S(1)}, u32[]{:S(2)}, u32[]{:S(2)}) collective-permute-start(bf16[16,16,256]{2,1,0:T(8,128)(2,1)} %get-tuple-element.55), channel_id=1, source_target_pairs={{0,11},{1,10},{2,9},{3,8},{4,15},{5,14},{6,13},{7,12},{8,3},{9,2},... | collective-permute-start | bytes 393224 | tf_op jit(solution)/shard_map/ppermute | solution.py:151
  127.2 10.5 %collective-permute-start.35 = (bf16[16,16,256]{2,1,0:T(8,128)(2,1)}, bf16[16,16,256]{2,1,0:T(8,128)(2,1)S(1)}, u32[]{:S(2)}, u32[]{:S(2)}) collective-permute-start(bf16[16,16,256]{2,1,0:T(8,128)(2,1)} %get-tuple-element.54), channel_id=1, source_target_pairs={{0,15},{1,14},{2,13},{3,12},{4,3},{5,2},{6,1},{7,0},{8,7},{9,6},{1... | collective-permute-start | bytes 393224 | tf_op jit(solution)/shard_map/ppermute | solution.py:151
  131.0 39.5 %collective-permute-start.43 = (bf16[4,1024,256]{2,1,0:T(8,128)(2,1)}, bf16[4,1024,256]{2,1,0:T(8,128)(2,1)}, u32[]{:S(2)}, u32[]{:S(2)}) collective-permute-start(bf16[4,1024,256]{2,1,0:T(8,128)(2,1)} %bitcast.203), channel_id=1, source_target_pairs={{0,1},{1,0},{2,3},{3,2},{4,5},{5,4},{6,7},{7,6},{8,9},{9,8},{10,11... | collective-permute-start | bytes 6291464 | tf_op jit(solution)/shard_map/ppermute | solution.py:151
  142.7 7.2 %collective-permute-start.36 = (bf16[32,8,256]{2,1,0:T(8,128)(2,1)S(1)}, bf16[32,8,256]{2,1,0:T(8,128)(2,1)S(1)}, u32[]{:S(2)}, u32[]{:S(2)}) collective-permute-start(bf16[32,8,256]{2,1,0:T(8,128)(2,1)S(1)} %get-tuple-element.77), channel_id=1, source_target_pairs={{0,8},{1,9},{2,10},{3,11},{4,12},{5,13},{6,14},{7,15},{8,0},{9,1},... | collective-permute-start | bytes 393224 | tf_op jit(solution)/shard_map/ppermute | solution.py:151
  143.5 11.9 %collective-permute-start.37 = (bf16[32,8,256]{2,1,0:T(8,128)(2,1)S(1)}, bf16[32,8,256]{2,1,0:T(8,128)(2,1)S(1)}, u32[]{:S(2)}, u32[]{:S(2)}) collective-permute-start(bf16[32,8,256]{2,1,0:T(8,128)(2,1)S(1)} %get-tuple-element.76), channel_id=1, source_target_pairs={{0,4},{1,5},{2,6},{3,7},{4,8},{5,9},{6,10},{7,11},{8,12},{9,13},{1... | collective-permute-start | bytes 393224 | tf_op jit(solution)/shard_map/ppermute | solution.py:151
  147.6 11.7 %collective-permute-start.38 = (bf16[32,8,256]{2,1,0:T(8,128)(2,1)S(1)}, bf16[32,8,256]{2,1,0:T(8,128)(2,1)S(1)}, u32[]{:S(2)}, u32[]{:S(2)}) collective-permute-start(bf16[32,8,256]{2,1,0:T(8,128)(2,1)S(1)} %get-tuple-element.79), channel_id=1, source_target_pairs={{0,12},{1,13},{2,14},{3,15},{4,0},{5,1},{6,2},{7,3},{8,4},{9,5},{1... | collective-permute-start | bytes 393224 | tf_op jit(solution)/shard_map/ppermute | solution.py:151
  148.2 17.7 %collective-permute-start.39 = (bf16[32,8,256]{2,1,0:T(8,128)(2,1)}, bf16[32,8,256]{2,1,0:T(8,128)(2,1)S(1)}, u32[]{:S(2)}, u32[]{:S(2)}) collective-permute-start(bf16[32,8,256]{2,1,0:T(8,128)(2,1)} %get-tuple-element.75), channel_id=1, source_target_pairs={{0,10},{1,11},{2,8},{3,9},{4,14},{5,15},{6,12},{7,13},{8,2},{9,3},... | collective-permute-start | bytes 393224 | tf_op jit(solution)/shard_map/ppermute | solution.py:151
  149.9 15.9 %collective-permute-start.40 = (bf16[32,8,256]{2,1,0:T(8,128)(2,1)}, bf16[32,8,256]{2,1,0:T(8,128)(2,1)S(1)}, u32[]{:S(2)}, u32[]{:S(2)}) collective-permute-start(bf16[32,8,256]{2,1,0:T(8,128)(2,1)} %get-tuple-element.74), channel_id=1, source_target_pairs={{0,6},{1,7},{2,4},{3,5},{4,10},{5,11},{6,8},{7,9},{8,14},{9,15},{1... | collective-permute-start | bytes 393224 | tf_op jit(solution)/shard_map/ppermute | solution.py:151
  155.4 13.0 %collective-permute-start.41 = (bf16[32,8,256]{2,1,0:T(8,128)(2,1)}, bf16[32,8,256]{2,1,0:T(8,128)(2,1)S(1)}, u32[]{:S(2)}, u32[]{:S(2)}) collective-permute-start(bf16[32,8,256]{2,1,0:T(8,128)(2,1)} %get-tuple-element.73), channel_id=1, source_target_pairs={{0,14},{1,15},{2,12},{3,13},{4,2},{5,3},{6,0},{7,1},{8,6},{9,7},{1... | collective-permute-start | bytes 393224 | tf_op jit(solution)/shard_map/ppermute | solution.py:151
  159.3 10.9 %collective-permute-start.42 = (bf16[32,8,256]{2,1,0:T(8,128)(2,1)S(1)}, bf16[32,8,256]{2,1,0:T(8,128)(2,1)S(1)}, u32[]{:S(2)}, u32[]{:S(2)}) collective-permute-start(bf16[32,8,256]{2,1,0:T(8,128)(2,1)S(1)} %get-tuple-element.72), channel_id=1, source_target_pairs={{0,2},{1,3},{2,0},{3,1},{4,6},{5,7},{6,4},{7,5},{8,10},{9,11},{10,... | collective-permute-start | bytes 393224 | tf_op jit(solution)/shard_map/ppermute | solution.py:151
  174.0 8.5 %collective-permute-start.44 = (bf16[32,1024]{1,0:T(8,128)(2,1)S(1)}, bf16[32,1024]{1,0:T(8,128)(2,1)S(1)}, u32[]{:S(2)}, u32[]{:S(2)}) collective-permute-start(bf16[32,1024]{1,0:T(8,128)(2,1)S(1)} %get-tuple-element.82), channel_id=1, source_target_pairs={{0,8},{1,9},{2,10},{3,11},{4,12},{5,13},{6,14},{7,15},{8,0},{9,1},... | collective-permute-start | bytes 196616 | tf_op jit(solution)/shard_map/ppermute | solution.py:151
  177.2 6.2 %collective-permute-start.45 = (bf16[32,1024]{1,0:T(8,128)(2,1)S(1)}, bf16[32,1024]{1,0:T(8,128)(2,1)S(1)}, u32[]{:S(2)}, u32[]{:S(2)}) collective-permute-start(bf16[32,1024]{1,0:T(8,128)(2,1)S(1)} %get-tuple-element.88), channel_id=1, source_target_pairs={{0,12},{1,13},{2,14},{3,15},{4,0},{5,1},{6,2},{7,3},{8,4},{9,5},{1... | collective-permute-start | bytes 196616 | tf_op jit(solution)/shard_map/ppermute | solution.py:151
  177.2 9.4 %collective-permute-start.46 = (bf16[32,1024]{1,0:T(8,128)(2,1)S(1)}, bf16[32,1024]{1,0:T(8,128)(2,1)S(1)}, u32[]{:S(2)}, u32[]{:S(2)}) collective-permute-start(bf16[32,1024]{1,0:T(8,128)(2,1)S(1)} %get-tuple-element.87), channel_id=1, source_target_pairs={{0,4},{1,5},{2,6},{3,7},{4,8},{5,9},{6,10},{7,11},{8,12},{9,13},{1... | collective-permute-start | bytes 196616 | tf_op jit(solution)/shard_map/ppermute | solution.py:151
  179.3 8.4 %collective-permute-start.47 = (bf16[32,1024]{1,0:T(8,128)(2,1)S(1)}, bf16[32,1024]{1,0:T(8,128)(2,1)S(1)}, u32[]{:S(2)}, u32[]{:S(2)}) collective-permute-start(bf16[32,1024]{1,0:T(8,128)(2,1)S(1)} %get-tuple-element.86), channel_id=1, source_target_pairs={{0,10},{1,11},{2,8},{3,9},{4,14},{5,15},{6,12},{7,13},{8,2},{9,3},... | collective-permute-start | bytes 196616 | tf_op jit(solution)/shard_map/ppermute | solution.py:151
  180.5 7.2 %collective-permute-start.48 = (bf16[32,1024]{1,0:T(8,128)(2,1)S(1)}, bf16[32,1024]{1,0:T(8,128)(2,1)S(1)}, u32[]{:S(2)}, u32[]{:S(2)}) collective-permute-start(bf16[32,1024]{1,0:T(8,128)(2,1)S(1)} %get-tuple-element.85), channel_id=1, source_target_pairs={{0,14},{1,15},{2,12},{3,13},{4,2},{5,3},{6,0},{7,1},{8,6},{9,7},{1... | collective-permute-start | bytes 196616 | tf_op jit(solution)/shard_map/ppermute | solution.py:151
  182.5 7.0 %collective-permute-start.49 = (bf16[32,1024]{1,0:T(8,128)(2,1)S(1)}, bf16[32,1024]{1,0:T(8,128)(2,1)S(1)}, u32[]{:S(2)}, u32[]{:S(2)}) collective-permute-start(bf16[32,1024]{1,0:T(8,128)(2,1)S(1)} %get-tuple-element.84), channel_id=1, source_target_pairs={{0,6},{1,7},{2,4},{3,5},{4,10},{5,11},{6,8},{7,9},{8,14},{9,15},{1... | collective-permute-start | bytes 196616 | tf_op jit(solution)/shard_map/ppermute | solution.py:151
  183.4 6.1 %collective-permute-start.50 = (bf16[32,1024]{1,0:T(8,128)(2,1)S(1)}, bf16[32,1024]{1,0:T(8,128)(2,1)S(1)}, u32[]{:S(2)}, u32[]{:S(2)}) collective-permute-start(bf16[32,1024]{1,0:T(8,128)(2,1)S(1)} %get-tuple-element.83), channel_id=1, source_target_pairs={{0,2},{1,3},{2,0},{3,1},{4,6},{5,7},{6,4},{7,5},{8,10},{9,11},{10,... | collective-permute-start | bytes 196616 | tf_op jit(solution)/shard_map/ppermute | solution.py:151
